TPU v7x, 32 devices: a whole 2x2x4 slice. The times are simulated.
32 devices in a mesh: groups: 2 (over x), spatial: 16 (over z, y, core).
Axes of the slice: x: 2, y: 2, z: 4, core: 2. Of those that a mesh axis runs over, the one named last changes fastest.
Arguments:
- volume: bfloat16 [32, 64, 8, 256], P(None, 'spatial', 'groups'), parts along dimension 2, may hold values from -6 to 6
- weights_mid: bfloat16 [64, 27, 32], replicated, may hold values from -0.21875 to 0.21875
- weights_top: bfloat16 [128, 27, 64], replicated, may hold values from -0.15625 to 0.15625
- cotangent: bfloat16 [128, 32, 4, 128], P(None, 'spatial', 'groups'), parts along dimension 2, may hold values from -6 to 6
Outputs:
- input_grad: bfloat16 [32, 64, 8, 256], P(None, 'spatial', 'groups'), parts along dimension 2
- mid_grad: float32 [128, 27, 32], P('groups'), parts along dimension 0
- top_grad: float32 [256, 27, 64], P('groups'), parts along dimension 0
There are 2 independent parts, one for each index of `groups`. A program takes and returns all parts, laid end to end along the dimension named above; an argument that names none is the same for every part. Nothing has to cross between parts.
All inputs are finite; a program needn't handle non-finite values.
Results may differ from a plain program's by a relative error of at most 0.0059.
Values may be sent and summed in bfloat16 or wider, within the bound.
No kernel may reach another device: no remote copies, remote signals or barrier semaphores. Data moves between devices by JAX's collectives and lax.ppermute only.
A program may use at most 128 MiB of HBM per device.

v0:
```python
import math

import jax
import jax.numpy as jnp
from jax import lax
from jax.experimental import pallas as pl
from jax.experimental.pallas import tpu as pltpu
from jax.sharding import PartitionSpec as P

BF16 = jnp.bfloat16
F32 = jnp.float32
ROOT = math.sqrt(2.0 / math.pi)
CUBIC = 0.044715
THREE = (0, 1, 2)
VMEM_LIMIT = 50 << 20


def kernel_call(body, name, outs, args, scratch=(), flops=0, moved=0):
    whole = pl.BlockSpec(memory_space=pltpu.VMEM)
    return pl.pallas_call(
        body,
        name=name,
        out_shape=outs,
        in_specs=[whole] * len(args),
        out_specs=jax.tree.map(lambda _: whole, outs),
        scratch_shapes=list(scratch),
        compiler_params=pltpu.CompilerParams(vmem_limit_bytes=VMEM_LIMIT),
        cost_estimate=pl.CostEstimate(flops=flops, bytes_accessed=moved, transcendentals=0),
    )(*args)


def dot(a, b, contract=((1,), (0,))):
    return lax.dot_general(a, b, (contract, ((), ())), preferred_element_type=F32)


def parity_matrix(width, inverse):
    first = lax.broadcasted_iota(jnp.int32, (width, width), 0)
    second = lax.broadcasted_iota(jnp.int32, (width, width), 1)
    cell, slot = (second, first) if inverse else (first, second)
    half = width // 2
    source = jnp.where(slot < half, 2 * slot, 2 * (slot - half) + 1)
    return (cell == source).astype(F32).astype(BF16)


def later(row):
    lane = lax.broadcasted_iota(jnp.int32, row.shape, 1)
    return jnp.where(lane == 0, 0.0, pltpu.roll(row, 1, 1))


def earlier(row):
    lane = lax.broadcasted_iota(jnp.int32, row.shape, 1)
    last = row.shape[1] - 1
    return jnp.where(lane == last, 0.0, pltpu.roll(row, last, 1))


def gelu_parts(value):
    square = value * value
    tanh = jnp.tanh(ROOT * value * (1.0 + CUBIC * square))
    outer = 0.5 * (1.0 + tanh)
    slope = outer + 0.5 * value * (1.0 - tanh * tanh) * (ROOT * (1.0 + 3.0 * CUBIC * square))
    return value * outer, slope


def forward_kernel(prev_ref, own_ref, next_ref, wmid_ref, wtop_ref, cot_ref, delta_ref, slope_ref, vol_ref, pool_ref, *, h, w, spatial):
    half = w // 2
    here = lax.axis_index("spatial")
    split = parity_matrix(w, False)
    vrows = h + 2
    zero_row = jnp.zeros((vol_ref.shape[0], w), BF16)
    planes = []
    for ref in (prev_ref, own_ref, next_ref):
        for start in range(0, ref.shape[1], h * w):
            planes.append((ref, start))
    channels = vol_ref.shape[0]
    for z, (ref, start) in enumerate(planes):
        rows = jnp.concatenate([ref[:, start + y * w : start + (y + 1) * w] for y in range(h)], axis=0)
        sorted_rows = dot(rows, split).astype(BF16)
        base = z * vrows * w
        vol_ref[:, base : base + w] = zero_row
        vol_ref[:, base + (h + 1) * w : base + (h + 2) * w] = zero_row
        for y in range(h):
            vol_ref[:, base + (y + 1) * w : base + (y + 2) * w] = sorted_rows[y * channels : (y + 1) * channels]
    mid = slope_ref.shape[0]
    count = len(planes) - 2
    hp = h // 2
    prow = (hp + 2) * half
    pool_zero = jnp.zeros((pool_ref.shape[0], half), BF16)
    for pz in range(count // 2):
        sums = [None] * hp
        for j in (2 * pz, 2 * pz + 1):
            cols = jnp.concatenate(
                [vol_ref[:, ((j + a) * vrows + b) * w : ((j + a) * vrows + b + h) * w] for a in THREE for b in THREE],
                axis=0,
            )
            part = dot(wmid_ref[...], cols)
            for y in range(h):
                even = slice(y * w, y * w + half)
                odd = slice(y * w + half, (y + 1) * w)
                pre_even = part[mid : 2 * mid, even] + later(part[:mid, odd]) + part[2 * mid :, odd]
                pre_odd = part[mid : 2 * mid, odd] + part[:mid, even] + earlier(part[2 * mid :, even])
                value_even, slope_even = gelu_parts(pre_even)
                value_odd, slope_odd = gelu_parts(pre_odd)
                if 0 < j < count - 1:
                    out = ((j - 1) * h + y) * w
                    slope_ref[:, out : out + half] = slope_even * 0.125
                    slope_ref[:, out + half : out + w] = slope_odd * 0.125
                both = value_even + value_odd
                sums[y // 2] = both if sums[y // 2] is None else sums[y // 2] + both
        base = pz * prow
        pool_ref[:, base : base + half] = pool_zero
        pool_ref[:, base + (hp + 1) * half : base + prow] = pool_zero
        for y in range(hp):
            row = sums[y] * 0.125
            if pz == 0:
                row = jnp.where(here == 0, 0.0, row)
            if pz == count // 2 - 1:
                row = jnp.where(here == spatial - 1, 0.0, row)
            row = row.astype(BF16).astype(F32)
            at = slice(base + (y + 1) * half, base + (y + 2) * half)
            pool_ref[:mid, at] = later(row).astype(BF16)
            pool_ref[mid : 2 * mid, at] = row.astype(BF16)
            pool_ref[2 * mid :, at] = earlier(row).astype(BF16)
    for j in range(count // 2 - 2):
        cols = jnp.concatenate(
            [pool_ref[:, (j + a) * prow + b * half : (j + a) * prow + (b + hp) * half] for a in THREE for b in THREE], axis=0
        )
        pre_top = dot(wtop_ref[...], cols, ((0,), (0,)))
        at = slice(j * hp * half, (j + 1) * hp * half)
        delta_ref[:, at] = (cot_ref[:, at].astype(F32) * gelu_parts(pre_top)[1]).astype(BF16)


def top_kernel(delta_ref, pool_ref, out_ref, *, hp, wp):
    prow = (hp + 2) * wp
    planes = delta_ref.shape[1] // (hp * wp)
    for a in THREE:
        for b in THREE:
            block = jnp.concatenate(
                [pool_ref[:, (j + a) * prow + b * wp : (j + a) * prow + (b + hp) * wp] for j in range(planes)], axis=1
            )
            rows = slice((3 * a + b) * block.shape[0], (3 * a + b + 1) * block.shape[0])
            out_ref[rows, :] = dot(block, delta_ref[...], ((1,), (1,))).astype(BF16)


def backward_kernel(prev_ref, own_ref, next_ref, slope_ref, vol_ref, wtop_ref, mid_ref, field_ref, top_ref, shift_ref, *, h, w, spatial):
    half, hp = w // 2, h // 2
    here = lax.axis_index("spatial")
    trow = (hp + 2) * half
    top_zero = jnp.zeros((top_ref.shape[0], half), BF16)
    depth = own_ref.shape[1] // (hp * half)
    for z in range(3 * depth):
        ref = (prev_ref, own_ref, next_ref)[z // depth]
        start = (z % depth) * hp * half
        base = z * trow
        top_ref[:, base : base + half] = top_zero
        top_ref[:, base + half : base + (hp + 1) * half] = ref[:, start : start + hp * half]
        top_ref[:, base + (hp + 1) * half : base + trow] = top_zero
    mid = slope_ref.shape[0]
    weights = jnp.concatenate(
        [
            jnp.concatenate([wtop_ref[(3 * ab + c) * mid : (3 * ab + c + 1) * mid, :] for ab in range(9)], axis=1)
            for c in THREE
        ],
        axis=0,
    )
    outer = depth + 2
    first = depth - 1
    cols = jnp.concatenate(
        [
            jnp.concatenate(
                [
                    top_ref[:, (first + j + 1 - a) * trow + (2 - b) * half : (first + j + 1 - a) * trow + (2 - b + hp) * half]
                    for j in range(outer)
                ],
                axis=1,
            )
            for a in THREE
            for b in THREE
        ],
        axis=0,
    )
    part = dot(weights, cols)
    vrows = h + 2
    field_zero = jnp.zeros((mid, w), BF16)
    fine = 2 * depth
    for m in range(fine + 2):
        j = (m + 1) // 2
        base = m * vrows * w
        field_ref[:, base : base + w] = field_zero
        field_ref[:, base + (h + 1) * w : base + vrows * w] = field_zero
        for y in range(h):
            at = slice((j * hp + y // 2) * half, (j * hp + y // 2 + 1) * half)
            pool = part[mid : 2 * mid, at] + later(part[2 * mid :, at]) + earlier(part[:mid, at])
            if m == 0:
                pool = jnp.where(here == 0, 0.0, pool)
            if m == fine + 1:
                pool = jnp.where(here == spatial - 1, 0.0, pool)
            out = (m * h + y) * w
            even = (slope_ref[:, out : out + half] * pool).astype(BF16)
            odd = (slope_ref[:, out + half : out + w] * pool).astype(BF16)
            to = base + (y + 1) * w
            field_ref[:, to : to + half] = even
            field_ref[:, to + half : to + w] = odd
            if 0 < m <= fine:
                to = ((m - 1) * h + y) * w
                shift_ref[:mid, to : to + half] = odd
                shift_ref[:mid, to + half : to + w] = earlier(even.astype(F32)).astype(BF16)
                shift_ref[mid : 2 * mid, to : to + half] = even
                shift_ref[mid : 2 * mid, to + half : to + w] = odd
                shift_ref[2 * mid :, to : to + half] = later(odd.astype(F32)).astype(BF16)
                shift_ref[2 * mid :, to + half : to + w] = even
    total = None
    for z in range(fine):
        piece = jnp.concatenate(
            [
                vol_ref[:, ((z + 2 + a) * vrows + b) * w : ((z + 2 + a) * vrows + b + h) * w]
                for a in THREE
                for b in THREE
            ],
            axis=0,
        )
        product = dot(piece, shift_ref[:, z * h * w : (z + 1) * h * w], ((1,), (1,)))
        total = product if total is None else total + product
    rows = total.shape[0]
    mid_ref[:rows, :] = total[:, : 2 * mid].astype(BF16)
    mid_ref[rows:, :] = jnp.concatenate([total[:, 2 * mid :], jnp.zeros((rows, mid), F32)], axis=1).astype(BF16)


def input_kernel(field_ref, wback_ref, out_ref, *, h, w):
    half = w // 2
    vrows = h + 2
    join = parity_matrix(w, True)
    ch = out_ref.shape[0]
    for z in range(out_ref.shape[1] // (h * w)):
        cols = jnp.concatenate(
            [
                field_ref[:, ((z + 2 - a) * vrows + 2 - b) * w : ((z + 2 - a) * vrows + 2 - b + h) * w]
                for a in THREE
                for b in THREE
            ],
            axis=0,
        )
        part = dot(wback_ref[...], cols)
        rows = []
        for y in range(h):
            even = slice(y * w, y * w + half)
            odd = slice(y * w + half, (y + 1) * w)
            grad_even = part[ch : 2 * ch, even] + later(part[2 * ch :, odd]) + part[:ch, odd]
            grad_odd = part[ch : 2 * ch, odd] + part[2 * ch :, even] + earlier(part[:ch, even])
            rows.append(jnp.concatenate([grad_even, grad_odd], axis=1).astype(BF16))
        joined = dot(jnp.concatenate(rows, axis=0), join).astype(BF16)
        for y in range(h):
            out_ref[:, (z * h + y) * w : (z * h + y + 1) * w] = joined[y * ch : (y + 1) * ch]


def finish_kernel(sum_ref, top_ref, mid_ref, *, scale_top, scale_mid):
    top_rows = top_ref.shape[0]
    top_ref[...] = sum_ref[:top_rows].astype(F32) * scale_top
    rows = mid_ref.shape[0] // 3
    mid = mid_ref.shape[1]
    left = sum_ref[top_rows : top_rows + rows].astype(F32) * scale_mid
    right = sum_ref[top_rows + rows :].astype(F32) * scale_mid
    q = rows // 9
    for ab in range(9):
        block = slice(ab * q, (ab + 1) * q)
        mid_ref[(3 * ab) * q : (3 * ab + 1) * q, :] = left[block, :mid]
        mid_ref[(3 * ab + 1) * q : (3 * ab + 2) * q, :] = left[block, mid:]
        mid_ref[(3 * ab + 2) * q : (3 * ab + 3) * q, :] = right[block, :mid]


def neighbours(shard, upward):
    size = lax.axis_size("spatial")
    pairs = [(i, i + 1) if upward else (i + 1, i) for i in range(size - 1)]
    return lax.ppermute(shard, "spatial", pairs)


def partner(block, bit):
    size = lax.axis_size("spatial")
    return lax.ppermute(block, "spatial", [(i, i ^ bit) for i in range(size)])


def sum_over_slabs(block, halvings):
    here = lax.axis_index("spatial")
    bits = [1 << k for k in range(lax.axis_size("spatial").bit_length() - 1)]
    kept = []
    for number, bit in enumerate(bits):
        if number < halvings:
            rows = block.shape[0] // 2
            low = (here // bit) % 2 == 0
            mine = jnp.where(low, block[:rows], block[rows:])
            other = jnp.where(low, block[rows:], block[:rows])
            block = mine + partner(other, bit)
            kept.append((bit, low))
        else:
            block = block + partner(block, bit)
    for bit, low in reversed(kept):
        other = partner(block, bit)
        block = jnp.where(low, jnp.concatenate([block, other]), jnp.concatenate([other, block]))
    return block


def shards(volume, weights_mid, weights_top, cotangent):
    spatial = lax.axis_size("spatial")
    cin, nz, h, w = volume.shape
    mid = weights_mid.shape[0]
    cout, nzp, hp, wp = cotangent.shape
    shape = jax.ShapeDtypeStruct
    plane = h * w
    flat = volume.reshape(cin, nz * plane)
    prev = neighbours(flat[:, plane:], True)
    following = neighbours(flat[:, : (nz - 1) * plane], False)
    split = weights_mid.reshape(mid, 9, 3, cin)
    wmid = jnp.transpose(split, (2, 0, 1, 3)).reshape(3 * mid, 9 * cin)
    wback = jnp.transpose(split, (2, 3, 1, 0)).reshape(3 * cin, 9 * mid)
    wtop = jnp.transpose(weights_top, (1, 2, 0)).reshape(27 * mid, cout)
    cot = cotangent.reshape(cout, nzp * hp * wp)
    padded = (3 * nz - 2) * (h + 2) * w
    delta, slope, vol, pool = kernel_call(
        lambda *refs: forward_kernel(*refs, h=h, w=w, spatial=spatial),
        "forward",
        (
            shape(cot.shape, BF16),
            shape((mid, (nz + 2) * plane), F32),
            shape((cin, padded), BF16),
            shape((3 * mid, (nzp + 2) * (hp + 2) * wp), BF16),
        ),
        (prev, flat, following, wmid, wtop, cot),
        flops=1_200_000_000,
        moved=6_000_000,
    )
    delta_prev = neighbours(delta, True)
    delta_next = neighbours(delta, False)
    top_part = kernel_call(
        lambda *refs: top_kernel(*refs, hp=hp, wp=wp),
        "top_part",
        shape((27 * mid, cout), BF16),
        (delta, pool),
        flops=226_000_000,
        moved=1_500_000,
    )
    mid_part, field = kernel_call(
        lambda *refs: backward_kernel(*refs, h=h, w=w, spatial=spatial),
        "backward",
        (shape((18 * cin, 2 * mid), BF16), shape((mid, (nz + 2) * (h + 2) * w), BF16)),
        (delta_prev, delta, delta_next, slope, vol, wtop),
        scratch=(pltpu.VMEM((cout, 3 * nzp * (hp + 2) * wp), BF16), pltpu.VMEM((3 * mid, nz * plane), BF16)),
        flops=900_000_000,
        moved=5_000_000,
    )
    total = sum_over_slabs(jnp.concatenate([top_part, mid_part], axis=0), 2)
    input_grad = kernel_call(
        lambda *refs: input_kernel(*refs, h=h, w=w),
        "input_grad",
        shape((cin, nz * plane), BF16),
        (field, wback),
        flops=452_000_000,
        moved=2_000_000,
    ).reshape(volume.shape)
    top_grad, mid_grad = kernel_call(
        lambda *refs: finish_kernel(
            *refs,
            scale_top=1.0 / math.sqrt(nzp * hp * wp * spatial),
            scale_mid=1.0 / math.sqrt(nz * plane * spatial),
        ),
        "finish",
        (shape((27 * mid, cout), F32), shape((27 * cin, mid), F32)),
        (total,),
        moved=2_000_000,
    )
    return (
        input_grad,
        jnp.transpose(mid_grad.reshape(27, cin, mid), (2, 0, 1)),
        jnp.transpose(top_grad.reshape(27, mid, cout), (2, 0, 1)),
    )


def solution(mesh):
    return jax.shard_map(
        shards,
        mesh=mesh,
        in_specs=(P(None, "spatial", "groups", None), P(), P(), P(None, "spatial", "groups", None)),
        out_specs=(
            P(None, "spatial", "groups", None),
            P("groups", None, None),
            P("groups", None, None),
        ),
        check_vma=False,
    )
```

profile of v0, /device:TPU:0, one launch (start us, length us, event | category | flops | bytes accessed | tf_op | source)
XLA Modules:
  0.0 63.4 jit_solution(17631554156258207767)
XLA Ops:
  0.6 0.0 copy-start.3
  0.6 0.0 copy-start.4
  0.7 1.2 %reshape.33.refs_1_ = bf16[32,4096]{1,0:T(8,128)(2,1)S(1)} reshape(bf16[32,4,4,256]{3,2,1,0:T(4,128)(2,1)} %param.4) | data formatting | bytes 524288 | tf_op jit(solution)/shard_map/reshape | solution.py:308
  1.8 0.0 copy-start
  1.9 2.5 %collective-permute-start = (bf16[32,3072]{1,0:T(8,128)(2,1)S(1)}, bf16[32,3072]{1,0:T(8,128)(2,1)S(1)}, u32[]{:S(2)}, u32[]{:S(2)}) collective-permute-start(bf16[32,3072]{1,0:T(8,128)(2,1)S(1)} %get-tuple-element.20), channel_id=1, source_target_pairs={{0,1},{1,2},{2,3},{3,4},{4,5},{5,6},{6,7},{7,8},{8,9},{9,10},{10,1... | collective-permute-start | bytes 589832 | tf_op jit(solution)/shard_map/ppermute | solution.py:273
  4.4 1.3 %collective-permute-start.1 = (bf16[32,3072]{1,0:T(8,128)(2,1)S(1)}, bf16[32,3072]{1,0:T(8,128)(2,1)S(1)}, u32[]{:S(2)}, u32[]{:S(2)}) collective-permute-start(bf16[32,3072]{1,0:T(8,128)(2,1)S(1)} %get-tuple-element.19), channel_id=1, source_target_pairs={{1,0},{2,1},{3,2},{4,3},{5,4},{6,5},{7,6},{8,7},{9,8},{10,9},{11,1... | collective-permute-start | bytes 589832 | tf_op jit(solution)/shard_map/ppermute | solution.py:273
  5.7 0.0 copy-done.3
  5.7 0.2 copy.15
  5.9 0.2 reshape.35
  6.1 0.1 copy.10.refs_3_
  6.2 0.0 copy-done.4
  6.2 0.1 reshape.37.refs_5_
  6.3 0.0 collective-permute-done.refs_0_
  6.3 3.6 %collective-permute-done.1.refs_2_ = bf16[32,3072]{1,0:T(8,128)(2,1)S(1)} collective-permute-done((bf16[32,3072]{1,0:T(8,128)(2,1)S(1)}, bf16[32,3072]{1,0:T(8,128)(2,1)S(1)}, u32[]{:S(2)}, u32[]{:S(2)}) %collective-permute-start.1) | collective-permute-done | bytes 196640 | tf_op jit(solution)/shard_map/ppermute | solution.py:273
  9.8 0.0 copy-done
  9.8 3.4 %forward.1 = (bf16[128,512]{1,0:T(8,128)(2,1)S(1)}, f32[64,6144]{1,0:T(8,128)}, bf16[32,15360]{1,0:T(8,128)(2,1)S(1)}, bf16[192,2048]{1,0:T(8,128)(2,1)S(1)}) custom-call(bf16[32,3072]{1,0:T(8,128)(2,1)S(1)} %collective-permute-done.refs_0_, bf16[32,4096]{1,0:T(8,128)(2,1)S(1)} %reshape.33.refs_1_, bf16[32,3072]{1,0:T(8,128)(2,1)S(1)} %collective-permute-done.1.refs_2_, ...), custom_call_target="tpu_custom_call" | custom-call | flops 1200000000 | bytes 6000000 | tf_op jit(solution)/shard_map/forward/pallas_call | solution.py:20
  13.3 6.0 %collective-permute-start.2 = (bf16[128,512]{1,0:T(8,128)(2,1)S(1)}, bf16[128,512]{1,0:T(8,128)(2,1)S(1)}, u32[]{:S(2)}, u32[]{:S(2)}) collective-permute-start(bf16[128,512]{1,0:T(8,128)(2,1)S(1)} %get-tuple-element.11.refs_1_.refs_0_), channel_id=1, source_target_pairs={{0,1},{1,2},{2,3},{3,4},{4,5},{5,6},{6,7},{7,8},{8,9},{9,10},{10,1... | collective-permute-start | bytes 393224 | tf_op jit(solution)/shard_map/ppermute | solution.py:273
  19.3 1.3 %collective-permute-start.3 = (bf16[128,512]{1,0:T(8,128)(2,1)S(1)}, bf16[128,512]{1,0:T(8,128)(2,1)S(1)}, u32[]{:S(2)}, u32[]{:S(2)}) collective-permute-start(bf16[128,512]{1,0:T(8,128)(2,1)S(1)} %get-tuple-element.11.refs_1_.refs_0_), channel_id=1, source_target_pairs={{1,0},{2,1},{3,2},{4,3},{5,4},{6,5},{7,6},{8,7},{9,8},{10,9},{11,1... | collective-permute-start | bytes 393224 | tf_op jit(solution)/shard_map/ppermute | solution.py:273
  20.6 0.6 top_part.1
  21.3 0.0 collective-permute-done.2.refs_0_
  21.3 1.3 %collective-permute-done.3.refs_2_ = bf16[128,512]{1,0:T(8,128)(2,1)S(1)} collective-permute-done((bf16[128,512]{1,0:T(8,128)(2,1)S(1)}, bf16[128,512]{1,0:T(8,128)(2,1)S(1)}, u32[]{:S(2)}, u32[]{:S(2)}) %collective-permute-start.3) | collective-permute-done | bytes 131104 | tf_op jit(solution)/shard_map/ppermute | solution.py:273
  22.6 3.2 %backward.1 = (bf16[576,128]{1,0:T(8,128)(2,1)S(1)}, bf16[64,9216]{1,0:T(8,128)(2,1)S(1)}) custom-call(bf16[128,512]{1,0:T(8,128)(2,1)S(1)} %collective-permute-done.2.refs_0_, bf16[128,512]{1,0:T(8,128)(2,1)S(1)} %get-tuple-element.11.refs_1_.refs_0_, bf16[128,512]{1,0:T(8,128)(2,1)S(1)} %collective-permute-done.3.refs_2_, ...), custom_call_target="tpu_custom_call" | custom-call | flops 900000000 | bytes 5000000 | tf_op jit(solution)/shard_map/backward/pallas_call | solution.py:20
  25.8 0.0 copy-start.1
  25.8 1.0 %copy-done.1 = bf16[64,9216]{1,0:T(8,128)(2,1)} copy-done((bf16[64,9216]{1,0:T(8,128)(2,1)}, bf16[64,9216]{1,0:T(8,128)(2,1)S(1)}, u32[]{:S(2)}) %copy-start.1) | copy-done | bytes 1179672
  26.9 0.1 broadcast_select_fusion
  27.0 3.9 %collective-permute-start.4 = (bf16[1152,128]{1,0:T(8,128)(2,1)S(1)}, bf16[1152,128]{1,0:T(8,128)(2,1)S(1)}, u32[]{:S(2)}, u32[]{:S(2)}) collective-permute-start(bf16[1152,128]{1,0:T(8,128)(2,1)S(1)} %broadcast_select_fusion), channel_id=1, source_target_pairs={{0,1},{1,0},{2,3},{3,2},{4,5},{5,4},{6,7},{7,6},{8,9},{9,8},{10,11... | collective-permute-start | bytes 884744 | tf_op jit(solution)/shard_map/ppermute | solution.py:278
  30.9 1.2 %collective-permute-done.4 = bf16[1152,128]{1,0:T(8,128)(2,1)S(1)} collective-permute-done((bf16[1152,128]{1,0:T(8,128)(2,1)S(1)}, bf16[1152,128]{1,0:T(8,128)(2,1)S(1)}, u32[]{:S(2)}, u32[]{:S(2)}) %collective-permute-start.4) | collective-permute-done | bytes 294944 | tf_op jit(solution)/shard_map/ppermute | solution.py:278
  32.1 0.1 select_add_fusion
  32.2 2.6 %collective-permute-start.5 = (bf16[576,128]{1,0:T(8,128)(2,1)S(1)}, bf16[576,128]{1,0:T(8,128)(2,1)S(1)}, u32[]{:S(2)}, u32[]{:S(2)}) collective-permute-start(bf16[576,128]{1,0:T(8,128)(2,1)S(1)} %broadcast_select_fusion.1), channel_id=1, source_target_pairs={{0,2},{1,3},{2,0},{3,1},{4,6},{5,7},{6,4},{7,5},{8,10},{9,11},{10,... | collective-permute-start | bytes 442376 | tf_op jit(solution)/shard_map/ppermute | solution.py:278
  34.8 4.4 %collective-permute-done.5 = bf16[576,128]{1,0:T(8,128)(2,1)S(1)} collective-permute-done((bf16[576,128]{1,0:T(8,128)(2,1)S(1)}, bf16[576,128]{1,0:T(8,128)(2,1)S(1)}, u32[]{:S(2)}, u32[]{:S(2)}) %collective-permute-start.5) | collective-permute-done | bytes 147488 | tf_op jit(solution)/shard_map/ppermute | solution.py:278
  39.2 1.7 %collective-permute-start.6 = (bf16[576,128]{1,0:T(8,128)(2,1)S(1)}, bf16[576,128]{1,0:T(8,128)(2,1)S(1)}, u32[]{:S(2)}, u32[]{:S(2)}) collective-permute-start(bf16[576,128]{1,0:T(8,128)(2,1)S(1)} %select_add_fusion.1), channel_id=1, source_target_pairs={{0,4},{1,5},{2,6},{3,7},{4,0},{5,1},{6,2},{7,3},{8,12},{9,13},{10,... | collective-permute-start | bytes 442376 | tf_op jit(solution)/shard_map/ppermute | solution.py:278
  40.9 4.0 %collective-permute-done.6 = bf16[576,128]{1,0:T(8,128)(2,1)S(1)} collective-permute-done((bf16[576,128]{1,0:T(8,128)(2,1)S(1)}, bf16[576,128]{1,0:T(8,128)(2,1)S(1)}, u32[]{:S(2)}, u32[]{:S(2)}) %collective-permute-start.6) | collective-permute-done | bytes 147488 | tf_op jit(solution)/shard_map/ppermute | solution.py:278
  44.9 0.0 copy-start.2
  44.9 2.7 %collective-permute-start.7 = (bf16[576,128]{1,0:T(8,128)(2,1)S(1)}, bf16[576,128]{1,0:T(8,128)(2,1)S(1)}, u32[]{:S(2)}, u32[]{:S(2)}) collective-permute-start(bf16[576,128]{1,0:T(8,128)(2,1)S(1)} %add.25), channel_id=1, source_target_pairs={{0,8},{1,9},{2,10},{3,11},{4,12},{5,13},{6,14},{7,15},{8,0},{9,1},... | collective-permute-start | bytes 442376 | tf_op jit(solution)/shard_map/ppermute | solution.py:278
  47.6 6.1 %collective-permute-done.7 = bf16[576,128]{1,0:T(8,128)(2,1)S(1)} collective-permute-done((bf16[576,128]{1,0:T(8,128)(2,1)S(1)}, bf16[576,128]{1,0:T(8,128)(2,1)S(1)}, u32[]{:S(2)}, u32[]{:S(2)}) %collective-permute-start.7) | collective-permute-done | bytes 147488 | tf_op jit(solution)/shard_map/ppermute | solution.py:278
  53.7 1.3 %collective-permute-start.8 = (bf16[576,128]{1,0:T(8,128)(2,1)S(1)}, bf16[576,128]{1,0:T(8,128)(2,1)S(1)}, u32[]{:S(2)}, u32[]{:S(2)}) collective-permute-start(bf16[576,128]{1,0:T(8,128)(2,1)S(1)} %add.26), channel_id=1, source_target_pairs={{0,2},{1,3},{2,0},{3,1},{4,6},{5,7},{6,4},{7,5},{8,10},{9,11},{10,... | collective-permute-start | bytes 442376 | tf_op jit(solution)/shard_map/ppermute | solution.py:278
  55.0 3.9 %collective-permute-done.8 = bf16[576,128]{1,0:T(8,128)(2,1)S(1)} collective-permute-done((bf16[576,128]{1,0:T(8,128)(2,1)S(1)}, bf16[576,128]{1,0:T(8,128)(2,1)S(1)}, u32[]{:S(2)}, u32[]{:S(2)}) %collective-permute-start.8) | collective-permute-done | bytes 147488 | tf_op jit(solution)/shard_map/ppermute | solution.py:278
  58.9 0.1 maximum_select_fusion.1
  59.0 0.1 collective-permute-start.9
  59.1 0.1 copy.14
  59.2 0.2 reshape.38.refs_1_
  59.5 0.0 copy-done.2
  59.5 1.7 %input_grad.1 = bf16[32,4096]{1,0:T(8,128)(2,1)S(1)} custom-call(bf16[64,9216]{1,0:T(8,128)(2,1)S(1)} %copy-done.2, bf16[96,576]{1,0:T(8,128)(2,1)S(1)} %reshape.38.refs_1_), custom_call_target="tpu_custom_call" | custom-call | flops 452000000 | bytes 2000000 | tf_op jit(solution)/shard_map/input_grad/pallas_call | solution.py:20
  61.2 0.9 %reshape.39 = bf16[32,4,4,256]{3,2,1,0:T(4,128)(2,1)} reshape(bf16[32,4096]{1,0:T(8,128)(2,1)S(1)} %input_grad.1) | data formatting | bytes 524288 | tf_op jit(solution)/shard_map/reshape | solution.py:357
  62.1 0.0 collective-permute-done.9
  62.1 0.2 maximum_select_fusion.refs_0_
  62.3 1.2 %finish.1 = (f32[1728,128]{1,0:T(8,128)}, f32[864,64]{1,0:T(8,128)}) custom-call(bf16[2304,128]{1,0:T(8,128)(2,1)S(1)} %maximum_select_fusion.refs_0_), custom_call_target="tpu_custom_call" | custom-call | bytes 2000000 | tf_op jit(solution)/shard_map/finish/pallas_call | solution.py:20
  (5 shorter events, 0.2 us)
Async XLA Ops:
  0.6 5.1 %copy-start.3 = (bf16[64,27,32]{0,2,1:T(8,128)(2,1)S(1)}, bf16[64,27,32]{0,2,1:T(8,128)(2,1)}, u32[]{:S(2)}) copy-start(bf16[64,27,32]{0,2,1:T(8,128)(2,1)} %param.5) | copy-start | bytes 331780
  0.6 5.6 %copy-start.4 = (bf16[128,2,2,128]{3,2,1,0:T(2,128)(2,1)S(1)}, bf16[128,2,2,128]{3,2,1,0:T(2,128)(2,1)}, u32[]{:S(2)}) copy-start(bf16[128,2,2,128]{3,2,1,0:T(2,128)(2,1)} %param.7) | copy-start | bytes 393220
  1.8 8.0 %copy-start = (bf16[128,27,64]{0,2,1:T(8,128)(2,1)S(1)}, bf16[128,27,64]{0,2,1:T(8,128)(2,1)}, u32[]{:S(2)}) copy-start(bf16[128,27,64]{0,2,1:T(8,128)(2,1)} %param.6) | copy-start | bytes 1327108
  1.9 4.4 %collective-permute-start = (bf16[32,3072]{1,0:T(8,128)(2,1)S(1)}, bf16[32,3072]{1,0:T(8,128)(2,1)S(1)}, u32[]{:S(2)}, u32[]{:S(2)}) collective-permute-start(bf16[32,3072]{1,0:T(8,128)(2,1)S(1)} %get-tuple-element.20), channel_id=1, source_target_pairs={{0,1},{1,2},{2,3},{3,4},{4,5},{5,6},{6,7},{7,8},{8,9},{9,10},{10,1... | collective-permute-start | bytes 589832 | tf_op jit(solution)/shard_map/ppermute | solution.py:273
  4.4 5.5 %collective-permute-start.1 = (bf16[32,3072]{1,0:T(8,128)(2,1)S(1)}, bf16[32,3072]{1,0:T(8,128)(2,1)S(1)}, u32[]{:S(2)}, u32[]{:S(2)}) collective-permute-start(bf16[32,3072]{1,0:T(8,128)(2,1)S(1)} %get-tuple-element.19), channel_id=1, source_target_pairs={{1,0},{2,1},{3,2},{4,3},{5,4},{6,5},{7,6},{8,7},{9,8},{10,9},{11,1... | collective-permute-start | bytes 589832 | tf_op jit(solution)/shard_map/ppermute | solution.py:273
  13.3 8.0 %collective-permute-start.2 = (bf16[128,512]{1,0:T(8,128)(2,1)S(1)}, bf16[128,512]{1,0:T(8,128)(2,1)S(1)}, u32[]{:S(2)}, u32[]{:S(2)}) collective-permute-start(bf16[128,512]{1,0:T(8,128)(2,1)S(1)} %get-tuple-element.11.refs_1_.refs_0_), channel_id=1, source_target_pairs={{0,1},{1,2},{2,3},{3,4},{4,5},{5,6},{6,7},{7,8},{8,9},{9,10},{10,1... | collective-permute-start | bytes 393224 | tf_op jit(solution)/shard_map/ppermute | solution.py:273
  19.3 3.2 %collective-permute-start.3 = (bf16[128,512]{1,0:T(8,128)(2,1)S(1)}, bf16[128,512]{1,0:T(8,128)(2,1)S(1)}, u32[]{:S(2)}, u32[]{:S(2)}) collective-permute-start(bf16[128,512]{1,0:T(8,128)(2,1)S(1)} %get-tuple-element.11.refs_1_.refs_0_), channel_id=1, source_target_pairs={{1,0},{2,1},{3,2},{4,3},{5,4},{6,5},{7,6},{8,7},{9,8},{10,9},{11,1... | collective-permute-start | bytes 393224 | tf_op jit(solution)/shard_map/ppermute | solution.py:273
  25.8 1.1 %copy-start.1 = (bf16[64,9216]{1,0:T(8,128)(2,1)}, bf16[64,9216]{1,0:T(8,128)(2,1)S(1)}, u32[]{:S(2)}) copy-start(bf16[64,9216]{1,0:T(8,128)(2,1)S(1)} %get-tuple-element.14.refs_0_) | copy-start | bytes 3538948
  27.0 5.1 %collective-permute-start.4 = (bf16[1152,128]{1,0:T(8,128)(2,1)S(1)}, bf16[1152,128]{1,0:T(8,128)(2,1)S(1)}, u32[]{:S(2)}, u32[]{:S(2)}) collective-permute-start(bf16[1152,128]{1,0:T(8,128)(2,1)S(1)} %broadcast_select_fusion), channel_id=1, source_target_pairs={{0,1},{1,0},{2,3},{3,2},{4,5},{5,4},{6,7},{7,6},{8,9},{9,8},{10,11... | collective-permute-start | bytes 884744 | tf_op jit(solution)/shard_map/ppermute | solution.py:278
  32.2 7.0 %collective-permute-start.5 = (bf16[576,128]{1,0:T(8,128)(2,1)S(1)}, bf16[576,128]{1,0:T(8,128)(2,1)S(1)}, u32[]{:S(2)}, u32[]{:S(2)}) collective-permute-start(bf16[576,128]{1,0:T(8,128)(2,1)S(1)} %broadcast_select_fusion.1), channel_id=1, source_target_pairs={{0,2},{1,3},{2,0},{3,1},{4,6},{5,7},{6,4},{7,5},{8,10},{9,11},{10,... | collective-permute-start | bytes 442376 | tf_op jit(solution)/shard_map/ppermute | solution.py:278
  39.2 5.6 %collective-permute-start.6 = (bf16[576,128]{1,0:T(8,128)(2,1)S(1)}, bf16[576,128]{1,0:T(8,128)(2,1)S(1)}, u32[]{:S(2)}, u32[]{:S(2)}) collective-permute-start(bf16[576,128]{1,0:T(8,128)(2,1)S(1)} %select_add_fusion.1), channel_id=1, source_target_pairs={{0,4},{1,5},{2,6},{3,7},{4,0},{5,1},{6,2},{7,3},{8,12},{9,13},{10,... | collective-permute-start | bytes 442376 | tf_op jit(solution)/shard_map/ppermute | solution.py:278
  44.9 14.6 %copy-start.2 = (bf16[64,9216]{1,0:T(8,128)(2,1)S(1)}, bf16[64,9216]{1,0:T(8,128)(2,1)}, u32[]{:S(2)}) copy-start(bf16[64,9216]{1,0:T(8,128)(2,1)} %copy-done.1) | copy-start | bytes 3538948
  44.9 8.8 %collective-permute-start.7 = (bf16[576,128]{1,0:T(8,128)(2,1)S(1)}, bf16[576,128]{1,0:T(8,128)(2,1)S(1)}, u32[]{:S(2)}, u32[]{:S(2)}) collective-permute-start(bf16[576,128]{1,0:T(8,128)(2,1)S(1)} %add.25), channel_id=1, source_target_pairs={{0,8},{1,9},{2,10},{3,11},{4,12},{5,13},{6,14},{7,15},{8,0},{9,1},... | collective-permute-start | bytes 442376 | tf_op jit(solution)/shard_map/ppermute | solution.py:278
  53.7 5.2 %collective-permute-start.8 = (bf16[576,128]{1,0:T(8,128)(2,1)S(1)}, bf16[576,128]{1,0:T(8,128)(2,1)S(1)}, u32[]{:S(2)}, u32[]{:S(2)}) collective-permute-start(bf16[576,128]{1,0:T(8,128)(2,1)S(1)} %add.26), channel_id=1, source_target_pairs={{0,2},{1,3},{2,0},{3,1},{4,6},{5,7},{6,4},{7,5},{8,10},{9,11},{10,... | collective-permute-start | bytes 442376 | tf_op jit(solution)/shard_map/ppermute | solution.py:278
  59.0 3.0 %collective-permute-start.9 = (bf16[1152,128]{1,0:T(8,128)(2,1)S(1)}, bf16[1152,128]{1,0:T(8,128)(2,1)S(1)}, u32[]{:S(2)}, u32[]{:S(2)}) collective-permute-start(bf16[1152,128]{1,0:T(8,128)(2,1)S(1)} %maximum_select_fusion.1), channel_id=1, source_target_pairs={{0,1},{1,0},{2,3},{3,2},{4,5},{5,4},{6,7},{7,6},{8,9},{9,8},{10,11... | collective-permute-start | bytes 884744 | tf_op jit(solution)/shard_map/ppermute | solution.py:278
where the time goes:
time: 63.7 us; the launch traced here: 63.4 us
  waiting for transfers between devices  24.5 us (38%)
  starting transfers between devices  23.3 us (37%)
  Pallas kernels  10.1 us (16%)
  local copies, waits for them, and re-layouts  4.09 us (6%)
  between operations  0.86 us (1%)
    ppermute x6, waiting for transfers between devices, partner(): return lax.ppermute(block, 'spatial', [(i, i ^ bit) for i in range(size)])  19.6 us
    ppermute x6, starting transfers between devices, partner(): return lax.ppermute(block, 'spatial', [(i, i ^ bit) for i in range(size)])  12.2 us
    ppermute x4, starting transfers between devices, neighbours(): return lax.ppermute(shard, 'spatial', pairs)  11.1 us
    pallas_call x5, Pallas kernels, kernel_call(): pl.pallas_call(body, name=name, out_shape=outs, in_specs=[whole] * len(ar...  10.1 us
    ppermute x4, waiting for transfers between devices, neighbours(): return lax.ppermute(shard, 'spatial', pairs)  4.85 us
  transfers between devices with their start and end apart: 10, of which 7 were waited for; matrix products, arithmetic and copies ran while one was open for 3% of the time, Pallas kernels for 4%

commit v1 on v0

--- a/solution.py
+++ b/solution.py
@@ -61,19 +61,26 @@
     return value * outer, slope
 
 
-def forward_kernel(prev_ref, own_ref, next_ref, wmid_ref, wtop_ref, cot_ref, delta_ref, slope_ref, vol_ref, pool_ref, *, h, w, spatial):
+def forward_kernel(near_ref, own_ref, far_ref, wmid_ref, wtop_ref, cot_ref, delta_ref, slope_ref, vol_ref, pool_ref, *, h, w, spatial):
     half = w // 2
     here = lax.axis_index("spatial")
+    first = here % 2 == 0
     split = parity_matrix(w, False)
     vrows = h + 2
     zero_row = jnp.zeros((vol_ref.shape[0], w), BF16)
     planes = []
-    for ref in (prev_ref, own_ref, next_ref):
+    for part, ref in enumerate((near_ref, own_ref, near_ref)):
         for start in range(0, ref.shape[1], h * w):
-            planes.append((ref, start))
+            planes.append((part, start))
     channels = vol_ref.shape[0]
-    for z, (ref, start) in enumerate(planes):
-        rows = jnp.concatenate([ref[:, start + y * w : start + (y + 1) * w] for y in range(h)], axis=0)
+    for z, (part, start) in enumerate(planes):
+        rows = []
+        for at in range(start, start + h * w, w):
+            if part == 1:
+                rows.append(own_ref[:, at : at + w])
+            else:
+                rows.append(jnp.where(first == (part == 0), far_ref[:, at : at + w], near_ref[:, at : at + w]))
+        rows = jnp.concatenate(rows, axis=0)
         sorted_rows = dot(rows, split).astype(BF16)
         base = z * vrows * w
         vol_ref[:, base : base + w] = zero_row
@@ -129,7 +136,14 @@
         delta_ref[:, at] = (cot_ref[:, at].astype(F32) * gelu_parts(pre_top)[1]).astype(BF16)
 
 
-def top_kernel(delta_ref, pool_ref, out_ref, *, hp, wp):
+def halve(whole_ref, keep_ref, send_ref):
+    core = lax.axis_index("spatial") % 2
+    rows = keep_ref.shape[0]
+    keep_ref[...] = whole_ref[pl.ds(pl.multiple_of(core * rows, 16), rows), :]
+    send_ref[...] = whole_ref[pl.ds(pl.multiple_of((1 - core) * rows, 16), rows), :].astype(BF16)
+
+
+def top_kernel(delta_ref, pool_ref, keep_ref, send_ref, out_ref, *, hp, wp):
     prow = (hp + 2) * wp
     planes = delta_ref.shape[1] // (hp * wp)
     for a in THREE:
@@ -138,21 +152,28 @@
                 [pool_ref[:, (j + a) * prow + b * wp : (j + a) * prow + (b + hp) * wp] for j in range(planes)], axis=1
             )
             rows = slice((3 * a + b) * block.shape[0], (3 * a + b + 1) * block.shape[0])
-            out_ref[rows, :] = dot(block, delta_ref[...], ((1,), (1,))).astype(BF16)
-
-
-def backward_kernel(prev_ref, own_ref, next_ref, slope_ref, vol_ref, wtop_ref, mid_ref, field_ref, top_ref, shift_ref, *, h, w, spatial):
+            out_ref[rows, :] = dot(block, delta_ref[...], ((1,), (1,)))
+    halve(out_ref, keep_ref, send_ref)
+
+
+def backward_kernel(
+    near_ref, own_ref, far_ref, slope_ref, vol_ref, wtop_ref, keep_ref, send_ref, field_ref, top_ref, shift_ref, mid_ref, *, h, w, spatial
+):
     half, hp = w // 2, h // 2
     here = lax.axis_index("spatial")
     trow = (hp + 2) * half
     top_zero = jnp.zeros((top_ref.shape[0], half), BF16)
     depth = own_ref.shape[1] // (hp * half)
     for z in range(3 * depth):
-        ref = (prev_ref, own_ref, next_ref)[z // depth]
         start = (z % depth) * hp * half
+        at = slice(start, start + hp * half)
+        if z // depth == 1:
+            plane = own_ref[:, at]
+        else:
+            plane = jnp.where((here % 2 == 0) == (z < depth), far_ref[:, at], near_ref[:, at])
         base = z * trow
         top_ref[:, base : base + half] = top_zero
-        top_ref[:, base + half : base + (hp + 1) * half] = ref[:, start : start + hp * half]
+        top_ref[:, base + half : base + (hp + 1) * half] = plane
         top_ref[:, base + (hp + 1) * half : base + trow] = top_zero
     mid = slope_ref.shape[0]
     weights = jnp.concatenate(
@@ -221,8 +242,14 @@
         product = dot(piece, shift_ref[:, z * h * w : (z + 1) * h * w], ((1,), (1,)))
         total = product if total is None else total + product
     rows = total.shape[0]
-    mid_ref[:rows, :] = total[:, : 2 * mid].astype(BF16)
-    mid_ref[rows:, :] = jnp.concatenate([total[:, 2 * mid :], jnp.zeros((rows, mid), F32)], axis=1).astype(BF16)
+    half_rows = rows // 2
+    mid_ref[:rows, :] = total[:, : 2 * mid]
+    last = total[:, 2 * mid :]
+    mid_ref[rows : rows + half_rows, :] = jnp.concatenate([last[:half_rows], last[half_rows:]], axis=1)
+    spare = mid_ref.shape[0] - rows - half_rows
+    if spare:
+        mid_ref[rows + half_rows :, :] = jnp.zeros((spare, 2 * mid), F32)
+    halve(mid_ref, keep_ref, send_ref)
 
 
 def input_kernel(field_ref, wback_ref, out_ref, *, h, w):
@@ -252,25 +279,20 @@
             out_ref[:, (z * h + y) * w : (z * h + y + 1) * w] = joined[y * ch : (y + 1) * ch]
 
 
-def finish_kernel(sum_ref, top_ref, mid_ref, *, scale_top, scale_mid):
-    top_rows = top_ref.shape[0]
-    top_ref[...] = sum_ref[:top_rows].astype(F32) * scale_top
-    rows = mid_ref.shape[0] // 3
-    mid = mid_ref.shape[1]
-    left = sum_ref[top_rows : top_rows + rows].astype(F32) * scale_mid
-    right = sum_ref[top_rows + rows :].astype(F32) * scale_mid
+def finish_kernel(low_ref, high_ref, out_ref, *, scale):
+    rows = out_ref.shape[0] // 3
+    mid = out_ref.shape[1]
+    whole = jnp.concatenate([low_ref[...], high_ref[...]], axis=0) * scale
     q = rows // 9
     for ab in range(9):
-        block = slice(ab * q, (ab + 1) * q)
-        mid_ref[(3 * ab) * q : (3 * ab + 1) * q, :] = left[block, :mid]
-        mid_ref[(3 * ab + 1) * q : (3 * ab + 2) * q, :] = left[block, mid:]
-        mid_ref[(3 * ab + 2) * q : (3 * ab + 3) * q, :] = right[block, :mid]
-
-
-def neighbours(shard, upward):
-    size = lax.axis_size("spatial")
-    pairs = [(i, i + 1) if upward else (i + 1, i) for i in range(size - 1)]
-    return lax.ppermute(shard, "spatial", pairs)
+        block = whole[ab * q : (ab + 1) * q]
+        out_ref[(3 * ab) * q : (3 * ab + 1) * q, :] = block[:, :mid]
+        out_ref[(3 * ab + 1) * q : (3 * ab + 2) * q, :] = block[:, mid:]
+    half_rows = rows // 2
+    last = whole[rows : rows + half_rows]
+    last = jnp.concatenate([last[:, :mid], last[:, mid:]], axis=0)
+    for ab in range(9):
+        out_ref[(3 * ab + 2) * q : (3 * ab + 3) * q, :] = last[ab * q : (ab + 1) * q]
 
 
 def partner(block, bit):
@@ -278,24 +300,36 @@
     return lax.ppermute(block, "spatial", [(i, i ^ bit) for i in range(size)])
 
 
-def sum_over_slabs(block, halvings):
-    here = lax.axis_index("spatial")
-    bits = [1 << k for k in range(lax.axis_size("spatial").bit_length() - 1)]
-    kept = []
-    for number, bit in enumerate(bits):
-        if number < halvings:
-            rows = block.shape[0] // 2
-            low = (here // bit) % 2 == 0
-            mine = jnp.where(low, block[:rows], block[rows:])
-            other = jnp.where(low, block[rows:], block[:rows])
-            block = mine + partner(other, bit)
-            kept.append((bit, low))
-        else:
-            block = block + partner(block, bit)
-    for bit, low in reversed(kept):
-        other = partner(block, bit)
-        block = jnp.where(low, jnp.concatenate([block, other]), jnp.concatenate([other, block]))
-    return block
+def across(block):
+    size = lax.axis_size("spatial")
+    pairs = [(i, i + 1) for i in range(1, size - 1, 2)]
+    return lax.ppermute(block, "spatial", pairs + [(j, i) for i, j in pairs])
+
+
+def bit_is_clear(bit):
+    return (lax.axis_index("spatial") // bit) % 2 == 0
+
+
+def add_both(block, bit):
+    rounded = block.astype(BF16)
+    return rounded.astype(F32) + partner(rounded, bit).astype(F32)
+
+
+def halves(block, bit):
+    rows = block.shape[0] // 2
+    low = bit_is_clear(bit)
+    mine = jnp.where(low, block[:rows], block[rows:])
+    other = jnp.where(low, block[rows:], block[:rows])
+    return mine, other.astype(BF16)
+
+
+def in_order(block, other, bit):
+    low = bit_is_clear(bit)
+    return jnp.where(low, block, other), jnp.where(low, other, block)
+
+
+def far_bits():
+    return [1 << k for k in range(2, lax.axis_size("spatial").bit_length() - 1)]
 
 
 def shards(volume, weights_mid, weights_top, cotangent):
@@ -306,8 +340,10 @@
     shape = jax.ShapeDtypeStruct
     plane = h * w
     flat = volume.reshape(cin, nz * plane)
-    prev = neighbours(flat[:, plane:], True)
-    following = neighbours(flat[:, : (nz - 1) * plane], False)
+    early, late = flat[:, : (nz - 1) * plane], flat[:, plane:]
+    first_core = bit_is_clear(1)
+    far = across(jnp.where(first_core, early, late))
+    near = partner(jnp.where(first_core, late, early), 1)
     split = weights_mid.reshape(mid, 9, 3, cin)
     wmid = jnp.transpose(split, (2, 0, 1, 3)).reshape(3 * mid, 9 * cin)
     wback = jnp.transpose(split, (2, 3, 1, 0)).reshape(3 * cin, 9 * mid)
@@ -323,30 +359,62 @@
             shape((cin, padded), BF16),
             shape((3 * mid, (nzp + 2) * (hp + 2) * wp), BF16),
         ),
-        (prev, flat, following, wmid, wtop, cot),
+        (near, flat, far, wmid, wtop, cot),
         flops=1_200_000_000,
         moved=6_000_000,
     )
-    delta_prev = neighbours(delta, True)
-    delta_next = neighbours(delta, False)
-    top_part = kernel_call(
+    delta_far = across(delta)
+    delta_near = partner(delta, 1)
+    top_rows = 27 * mid
+    keep, send = kernel_call(
         lambda *refs: top_kernel(*refs, hp=hp, wp=wp),
         "top_part",
-        shape((27 * mid, cout), BF16),
+        (shape((top_rows // 2, cout), F32), shape((top_rows // 2, cout), BF16)),
         (delta, pool),
+        scratch=(pltpu.VMEM((top_rows, cout), F32),),
         flops=226_000_000,
         moved=1_500_000,
     )
-    mid_part, field = kernel_call(
+    top_sum = keep + partner(send, 1).astype(F32)
+    mine, other = halves(top_sum, 2)
+    other, delta_near, delta_far = lax.optimization_barrier((other, delta_near, delta_far))
+    top_sum = mine + partner(other, 2).astype(F32)
+    for bit in far_bits():
+        top_sum = add_both(top_sum, bit)
+    top_sum = top_sum.astype(BF16)
+    top_sum = jnp.concatenate(in_order(top_sum, partner(top_sum, 2), 2), axis=0)
+    top_sum = jnp.concatenate(in_order(top_sum, partner(top_sum, 1), 1), axis=0)
+    top_grad = top_sum.astype(F32) * (1.0 / math.sqrt(nzp * hp * wp * spatial))
+    mid_rows = -(-27 * cin // 64) * 16
+    keep, send, field = kernel_call(
         lambda *refs: backward_kernel(*refs, h=h, w=w, spatial=spatial),
         "backward",
-        (shape((18 * cin, 2 * mid), BF16), shape((mid, (nz + 2) * (h + 2) * w), BF16)),
-        (delta_prev, delta, delta_next, slope, vol, wtop),
-        scratch=(pltpu.VMEM((cout, 3 * nzp * (hp + 2) * wp), BF16), pltpu.VMEM((3 * mid, nz * plane), BF16)),
+        (
+            shape((mid_rows, 2 * mid), F32),
+            shape((mid_rows, 2 * mid), BF16),
+            shape((mid, (nz + 2) * (h + 2) * w), BF16),
+        ),
+        (delta_near, delta, delta_far, slope, vol, wtop),
+        scratch=(
+            pltpu.VMEM((cout, 3 * nzp * (hp + 2) * wp), BF16),
+            pltpu.VMEM((3 * mid, nz * plane), BF16),
+            pltpu.VMEM((2 * mid_rows, 2 * mid), F32),
+        ),
         flops=900_000_000,
         moved=5_000_000,
     )
-    total = sum_over_slabs(jnp.concatenate([top_part, mid_part], axis=0), 2)
+    mid_sum = keep + partner(send, 1).astype(F32)
+    mid_sum, field = lax.optimization_barrier((mid_sum, field))
+    for bit in [2] + far_bits():
+        mid_sum = add_both(mid_sum, bit)
+    mid_low, mid_high = in_order(mid_sum, partner(mid_sum, 1), 1)
+    mid_grad = kernel_call(
+        lambda *refs: finish_kernel(*refs, scale=1.0 / math.sqrt(nz * plane * spatial)),
+        "finish",
+        shape((27 * cin, mid), F32),
+        (mid_low, mid_high),
+        moved=1_000_000,
+    )
     input_grad = kernel_call(
         lambda *refs: input_kernel(*refs, h=h, w=w),
         "input_grad",
@@ -355,17 +423,6 @@
         flops=452_000_000,
         moved=2_000_000,
     ).reshape(volume.shape)
-    top_grad, mid_grad = kernel_call(
-        lambda *refs: finish_kernel(
-            *refs,
-            scale_top=1.0 / math.sqrt(nzp * hp * wp * spatial),
-            scale_mid=1.0 / math.sqrt(nz * plane * spatial),
-        ),
-        "finish",
-        (shape((27 * mid, cout), F32), shape((27 * cin, mid), F32)),
-        (total,),
-        moved=2_000_000,
-    )
     return (
         input_grad,
         jnp.transpose(mid_grad.reshape(27, cin, mid), (2, 0, 1)),

time: 63.7 us -> 55.5 us (0.87)
  waiting for transfers between devices: 24.5 us -> 8.79 us
  starting transfers between devices: 23.3 us -> 30.2 us
  other arithmetic: 0.57 us -> 1.39 us
    ppermute x6 -> x13, starting transfers between devices: 12.2 us -> 28.9 us  [partner(): return lax.ppermute(block, 'spatial', [(i, i ^ bit) for i in range(size)])]
    ppermute x6 -> x13, waiting for transfers between devices: 19.6 us -> 8.79 us  [partner(): return lax.ppermute(block, 'spatial', [(i, i ^ bit) for i in range(size)])]
    ppermute x4 -> x2, starting transfers between devices: 11.1 us -> 1.32 us  [across(): return lax.ppermute(block, 'spatial', pairs + [(j, i) for i, j in pairs])]
    ppermute x4 -> x2, waiting for transfers between devices: 4.85 us -> 0.01 us  [across(): return lax.ppermute(block, 'spatial', pairs + [(j, i) for i, j in pairs])]
    unnamed x10 -> x6, local copies, waits for them, and re-layouts: 1.07 us -> 0.01 us
    mul x0 -> x1, other arithmetic: none -> 0.98 us  [shards(): top_grad = top_sum.astype(F32) * (1.0 / math.sqrt(nzp * hp * wp * spatial))]
    reshape x2, local copies, waits for them, and re-layouts: 0.27 us -> 1.21 us  [shards(): split = weights_mid.reshape(mid, 9, 3, cin)]
  transfers between devices with their start and end apart: 10 -> 15, of which waited for: 7 -> 8; matrix products, arithmetic and copies ran while one was open for 3% -> 6% of each run, Pallas kernels for 4% -> 5%
where the time goes in v1:
time: 55.5 us; the launch traced here: 55.3 us
  starting transfers between devices  30.2 us (54%)
  Pallas kernels  10.1 us (18%)
  waiting for transfers between devices  8.79 us (16%)
  local copies, waits for them, and re-layouts  3.95 us (7%)
  other arithmetic  1.39 us (3%)
  between operations  0.84 us (2%)
    ppermute x13, starting transfers between devices, partner(): return lax.ppermute(block, 'spatial', [(i, i ^ bit) for i in range(size)])  28.9 us
    pallas_call x5, Pallas kernels, kernel_call(): pl.pallas_call(body, name=name, out_shape=outs, in_specs=[whole] * len(ar...  10.1 us
    ppermute x13, waiting for transfers between devices, partner(): return lax.ppermute(block, 'spatial', [(i, i ^ bit) for i in range(size)])  8.79 us
    ppermute x2, starting transfers between devices, across(): return lax.ppermute(block, 'spatial', pairs + [(j, i) for i, j in pairs])  1.32 us
    reshape x2, local copies, waits for them, and re-layouts, shards(): split = weights_mid.reshape(mid, 9, 3, cin)  1.21 us
    reshape x1, local copies, waits for them, and re-layouts, shards(): flat = volume.reshape(cin, nz * plane)  1.19 us
  transfers between devices with their start and end apart: 15, of which 8 were waited for; matrix products, arithmetic and copies ran while one was open for 6% of the time, Pallas kernels for 5%

profile of v1, /device:TPU:0, one launch (start us, length us, event | category | flops | bytes accessed | tf_op | source)
XLA Modules:
  0.0 55.3 jit_solution(4268180607413226170)
XLA Ops:
  0.6 0.0 copy-start.2
  0.6 0.0 copy-start
  0.7 1.2 %reshape.35.refs_1_ = bf16[32,4096]{1,0:T(8,128)(2,1)S(1)} reshape(bf16[32,4,4,256]{3,2,1,0:T(4,128)(2,1)} %param.4) | data formatting | bytes 524288 | tf_op jit(solution)/shard_map/reshape | solution.py:342
  1.9 0.5 collective-permute-start
  2.4 0.7 %collective-permute-start.1 = (bf16[32,3072]{1,0:T(8,128)(2,1)S(1)}, bf16[32,3072]{1,0:T(8,128)(2,1)S(1)}, u32[]{:S(2)}, u32[]{:S(2)}) collective-permute-start(bf16[32,3072]{1,0:T(8,128)(2,1)S(1)} %get-tuple-element.33), channel_id=1, source_target_pairs={{1,2},{3,4},{5,6},{7,8},{9,10},{11,12},{13,14},{2,1},{4,3},{6,5},{... | collective-permute-start | bytes 589832 | tf_op jit(solution)/shard_map/ppermute | solution.py:306
  3.1 1.1 %copy.15 = bf16[64,9,3,32]{0,2,3,1:T(4,128)(2,1)S(1)} copy(bf16[64,9,3,32]{0,3,2,1:T(8,128)(2,1)} %bitcast.22) | data formatting | bytes 221184 | tf_op jit(solution)/shard_map/reshape | solution.py:347
  4.2 0.2 reshape.37
  4.4 0.1 copy.10.refs_3_
  4.5 0.0 copy-done.2
  4.5 0.1 reshape.39.refs_5_
  4.6 0.0 collective-permute-done.refs_0_
  4.6 0.0 collective-permute-done.1.refs_2_
  4.6 3.4 %forward.1 = (bf16[128,512]{1,0:T(8,128)(2,1)S(1)}, f32[64,6144]{1,0:T(8,128)}, bf16[32,15360]{1,0:T(8,128)(2,1)S(1)}, bf16[192,2048]{1,0:T(8,128)(2,1)S(1)}) custom-call(bf16[32,3072]{1,0:T(8,128)(2,1)S(1)} %collective-permute-done.refs_0_, bf16[32,4096]{1,0:T(8,128)(2,1)S(1)} %reshape.35.refs_1_, bf16[32,3072]{1,0:T(8,128)(2,1)S(1)} %collective-permute-done.1.refs_2_, ...), custom_call_target="tpu_custom_call" | custom-call | flops 1200000000 | bytes 6000000 | tf_op jit(solution)/shard_map/forward/pallas_call | solution.py:20
  8.1 0.7 %top_part.1 = (f32[864,128]{1,0:T(8,128)S(1)}, bf16[864,128]{1,0:T(8,128)(2,1)S(1)}) custom-call(bf16[128,512]{1,0:T(8,128)(2,1)S(1)} %get-tuple-element.17.refs_0_.refs_1_, bf16[192,2048]{1,0:T(8,128)(2,1)S(1)} %get-tuple-element.18.refs_1_), custom_call_target="tpu_custom_call" | custom-call | flops 226000000 | bytes 1500000 | tf_op jit(solution)/shard_map/top_part/pallas_call | solution.py:20
  8.8 7.1 %collective-permute-start.2 = (bf16[864,128]{1,0:T(8,128)(2,1)S(1)}, bf16[864,128]{1,0:T(8,128)(2,1)S(1)}, u32[]{:S(2)}, u32[]{:S(2)}) collective-permute-start(bf16[864,128]{1,0:T(8,128)(2,1)S(1)} %get-tuple-element.20), channel_id=1, source_target_pairs={{0,1},{1,0},{2,3},{3,2},{4,5},{5,4},{6,7},{7,6},{8,9},{9,8},{10,11... | collective-permute-start | bytes 663560 | tf_op jit(solution)/shard_map/ppermute | solution.py:300
  15.9 0.1 collective-permute-start.3
  16.0 0.7 %collective-permute-start.4 = (bf16[128,512]{1,0:T(8,128)(2,1)S(1)}, bf16[128,512]{1,0:T(8,128)(2,1)S(1)}, u32[]{:S(2)}, u32[]{:S(2)}) collective-permute-start(bf16[128,512]{1,0:T(8,128)(2,1)S(1)} %get-tuple-element.17.refs_0_.refs_1_), channel_id=1, source_target_pairs={{1,2},{3,4},{5,6},{7,8},{9,10},{11,12},{13,14},{2,1},{4,3},{6,5},{... | collective-permute-start | bytes 393224 | tf_op jit(solution)/shard_map/ppermute | solution.py:306
  16.6 0.3 collective-permute-done.2
  17.0 0.2 collective-permute-done.3.refs_0_
  17.2 0.0 collective-permute-done.4.refs_2_
  17.2 3.4 %backward.1 = (f32[224,128]{1,0:T(8,128)S(1)}, bf16[224,128]{1,0:T(8,128)(2,1)S(1)}, bf16[64,9216]{1,0:T(8,128)(2,1)S(1)}) custom-call(bf16[128,512]{1,0:T(8,128)(2,1)S(1)} %collective-permute-done.3.refs_0_, bf16[128,512]{1,0:T(8,128)(2,1)S(1)} %get-tuple-element.17.refs_0_.refs_1_, bf16[128,512]{1,0:T(8,128)(2,1)S(1)} %collective-permute-done.4.refs_2_, ...), custom_call_target="tpu_custom_call" | custom-call | flops 900000000 | bytes 5000000 | tf_op jit(solution)/shard_map/backward/pallas_call | solution.py:20
  20.6 6.2 %collective-permute-start.5 = (bf16[224,128]{1,0:T(8,128)(2,1)S(1)}, bf16[224,128]{1,0:T(8,128)(2,1)S(1)}, u32[]{:S(2)}, u32[]{:S(2)}) collective-permute-start(bf16[224,128]{1,0:T(8,128)(2,1)S(1)} %get-tuple-element.26), channel_id=1, source_target_pairs={{0,1},{1,0},{2,3},{3,2},{4,5},{5,4},{6,7},{7,6},{8,9},{9,8},{10,11... | collective-permute-start | bytes 172040 | tf_op jit(solution)/shard_map/ppermute | solution.py:300
  26.8 0.1 copy.14
  27.0 0.2 reshape.40.refs_1_
  27.2 3.1 %collective-permute-start.10 = (bf16[432,128]{1,0:T(8,128)(2,1)S(1)}, bf16[432,128]{1,0:T(8,128)(2,1)S(1)}, u32[]{:S(2)}, u32[]{:S(2)}) collective-permute-start(bf16[432,128]{1,0:T(8,128)(2,1)S(1)} %select_convert_fusion), channel_id=1, source_target_pairs={{0,2},{1,3},{2,0},{3,1},{4,6},{5,7},{6,4},{7,5},{8,10},{9,11},{10,... | collective-permute-start | bytes 331784 | tf_op jit(solution)/shard_map/ppermute | solution.py:300
  30.3 0.0 collective-permute-done.5
  30.4 1.7 %input_grad.1 = bf16[32,4096]{1,0:T(8,128)(2,1)S(1)} custom-call(bf16[64,9216]{1,0:T(8,128)(2,1)S(1)} %get-tuple-element.28.refs_0_, bf16[96,576]{1,0:T(8,128)(2,1)S(1)} %reshape.40.refs_1_), custom_call_target="tpu_custom_call" | custom-call | flops 452000000 | bytes 2000000 | tf_op jit(solution)/shard_map/input_grad/pallas_call | solution.py:20
  32.0 0.9 %reshape.41 = bf16[32,4,4,256]{3,2,1,0:T(4,128)(2,1)} reshape(bf16[32,4096]{1,0:T(8,128)(2,1)S(1)} %input_grad.1) | data formatting | bytes 524288 | tf_op jit(solution)/shard_map/reshape | solution.py:425
  32.9 0.8 %collective-permute-start.6 = (bf16[224,128]{1,0:T(8,128)(2,1)S(1)}, bf16[224,128]{1,0:T(8,128)(2,1)S(1)}, u32[]{:S(2)}, u32[]{:S(2)}) collective-permute-start(bf16[224,128]{1,0:T(8,128)(2,1)S(1)} %convert_add_fusion.2), channel_id=1, source_target_pairs={{0,2},{1,3},{2,0},{3,1},{4,6},{5,7},{6,4},{7,5},{8,10},{9,11},{10,... | collective-permute-start | bytes 172040 | tf_op jit(solution)/shard_map/ppermute | solution.py:300
  33.7 0.3 collective-permute-done.10
  34.1 1.9 %collective-permute-start.11 = (bf16[432,128]{1,0:T(8,128)(2,1)S(1)}, bf16[432,128]{1,0:T(8,128)(2,1)S(1)}, u32[]{:S(2)}, u32[]{:S(2)}) collective-permute-start(bf16[432,128]{1,0:T(8,128)(2,1)S(1)} %add_convert_fusion.2), channel_id=1, source_target_pairs={{0,4},{1,5},{2,6},{3,7},{4,0},{5,1},{6,2},{7,3},{8,12},{9,13},{10,... | collective-permute-start | bytes 331784 | tf_op jit(solution)/shard_map/ppermute | solution.py:300
  35.9 1.2 %collective-permute-done.6 = bf16[224,128]{1,0:T(8,128)(2,1)S(1)} collective-permute-done((bf16[224,128]{1,0:T(8,128)(2,1)S(1)}, bf16[224,128]{1,0:T(8,128)(2,1)S(1)}, u32[]{:S(2)}, u32[]{:S(2)}) %collective-permute-start.6) | collective-permute-done | bytes 57376 | tf_op jit(solution)/shard_map/ppermute | solution.py:300
  37.1 1.6 %collective-permute-start.7 = (bf16[224,128]{1,0:T(8,128)(2,1)S(1)}, bf16[224,128]{1,0:T(8,128)(2,1)S(1)}, u32[]{:S(2)}, u32[]{:S(2)}) collective-permute-start(bf16[224,128]{1,0:T(8,128)(2,1)S(1)} %add_convert_fusion.4), channel_id=1, source_target_pairs={{0,4},{1,5},{2,6},{3,7},{4,0},{5,1},{6,2},{7,3},{8,12},{9,13},{10,... | collective-permute-start | bytes 172040 | tf_op jit(solution)/shard_map/ppermute | solution.py:300
  38.8 0.4 collective-permute-done.11
  39.2 2.9 %collective-permute-start.12 = (bf16[432,128]{1,0:T(8,128)(2,1)S(1)}, bf16[432,128]{1,0:T(8,128)(2,1)S(1)}, u32[]{:S(2)}, u32[]{:S(2)}) collective-permute-start(bf16[432,128]{1,0:T(8,128)(2,1)S(1)} %add_convert_fusion.1), channel_id=1, source_target_pairs={{0,8},{1,9},{2,10},{3,11},{4,12},{5,13},{6,14},{7,15},{8,0},{9,1},... | collective-permute-start | bytes 331784 | tf_op jit(solution)/shard_map/ppermute | solution.py:300
  42.1 0.0 collective-permute-done.7
  42.1 2.2 %collective-permute-start.8 = (bf16[224,128]{1,0:T(8,128)(2,1)S(1)}, bf16[224,128]{1,0:T(8,128)(2,1)S(1)}, u32[]{:S(2)}, u32[]{:S(2)}) collective-permute-start(bf16[224,128]{1,0:T(8,128)(2,1)S(1)} %add_convert_fusion.3), channel_id=1, source_target_pairs={{0,8},{1,9},{2,10},{3,11},{4,12},{5,13},{6,14},{7,15},{8,0},{9,1},... | collective-permute-start | bytes 172040 | tf_op jit(solution)/shard_map/ppermute | solution.py:300
  44.4 3.3 %collective-permute-done.12 = bf16[432,128]{1,0:T(8,128)(2,1)S(1)} collective-permute-done((bf16[432,128]{1,0:T(8,128)(2,1)S(1)}, bf16[432,128]{1,0:T(8,128)(2,1)S(1)}, u32[]{:S(2)}, u32[]{:S(2)}) %collective-permute-start.12) | collective-permute-done | bytes 110624 | tf_op jit(solution)/shard_map/ppermute | solution.py:300
  47.7 2.2 %collective-permute-start.13 = (bf16[432,128]{1,0:T(8,128)(2,1)S(1)}, bf16[432,128]{1,0:T(8,128)(2,1)S(1)}, u32[]{:S(2)}, u32[]{:S(2)}) collective-permute-start(bf16[432,128]{1,0:T(8,128)(2,1)S(1)} %add_convert_fusion), channel_id=1, source_target_pairs={{0,2},{1,3},{2,0},{3,1},{4,6},{5,7},{6,4},{7,5},{8,10},{9,11},{10,... | collective-permute-start | bytes 331784 | tf_op jit(solution)/shard_map/ppermute | solution.py:300
  49.9 0.0 collective-permute-done.8
  49.9 0.1 collective-permute-start.9
  50.0 2.6 %collective-permute-done.13 = bf16[432,128]{1,0:T(8,128)(2,1)S(1)} collective-permute-done((bf16[432,128]{1,0:T(8,128)(2,1)S(1)}, bf16[432,128]{1,0:T(8,128)(2,1)S(1)}, u32[]{:S(2)}, u32[]{:S(2)}) %collective-permute-start.13) | collective-permute-done | bytes 110624 | tf_op jit(solution)/shard_map/ppermute | solution.py:300
  52.7 0.1 collective-permute-start.14
  52.7 0.0 collective-permute-done.9
  52.8 0.9 %finish.1 = f32[864,64]{1,0:T(8,128)} custom-call(f32[224,128]{1,0:T(8,128)S(1)} %get-tuple-element.36.refs_0_, f32[224,128]{1,0:T(8,128)S(1)} %get-tuple-element.35.refs_1_), custom_call_target="tpu_custom_call" | custom-call | bytes 1000000 | tf_op jit(solution)/shard_map/finish/pallas_call | solution.py:20
  53.7 0.5 collective-permute-done.14
  54.2 0.1 broadcast_select_fusion.1
  54.3 1.0 %convert_multiply_fusion = f32[1728,128]{1,0:T(8,128)} fusion(bf16[864,128]{1,0:T(8,128)(2,1)S(1)} %get-tuple-element.32, bf16[864,128]{1,0:T(8,128)(2,1)S(1)} %get-tuple-element.31), kind=kLoop, calls=%fused_computation | loop fusion | flops 1105920 | bytes 1327104 | tf_op jit(solution)/shard_map/mul | solution.py:387
  (16 shorter events, 0.3 us)
Async XLA Ops:
  0.6 3.9 %copy-start.2 = (bf16[128,2,2,128]{3,2,1,0:T(2,128)(2,1)S(1)}, bf16[128,2,2,128]{3,2,1,0:T(2,128)(2,1)}, u32[]{:S(2)}) copy-start(bf16[128,2,2,128]{3,2,1,0:T(2,128)(2,1)} %param.7) | copy-start | bytes 393220
  0.6 4.0 %copy-start = (bf16[128,27,64]{0,2,1:T(8,128)(2,1)S(1)}, bf16[128,27,64]{0,2,1:T(8,128)(2,1)}, u32[]{:S(2)}) copy-start(bf16[128,27,64]{0,2,1:T(8,128)(2,1)} %param.6) | copy-start | bytes 1327108
  1.9 2.7 %collective-permute-start = (bf16[32,3072]{1,0:T(8,128)(2,1)S(1)}, bf16[32,3072]{1,0:T(8,128)(2,1)S(1)}, u32[]{:S(2)}, u32[]{:S(2)}) collective-permute-start(bf16[32,3072]{1,0:T(8,128)(2,1)S(1)} %get-tuple-element.34), channel_id=1, source_target_pairs={{0,1},{1,0},{2,3},{3,2},{4,5},{5,4},{6,7},{7,6},{8,9},{9,8},{10,11... | collective-permute-start | bytes 589832 | tf_op jit(solution)/shard_map/ppermute | solution.py:300
  2.4 2.2 %collective-permute-start.1 = (bf16[32,3072]{1,0:T(8,128)(2,1)S(1)}, bf16[32,3072]{1,0:T(8,128)(2,1)S(1)}, u32[]{:S(2)}, u32[]{:S(2)}) collective-permute-start(bf16[32,3072]{1,0:T(8,128)(2,1)S(1)} %get-tuple-element.33), channel_id=1, source_target_pairs={{1,2},{3,4},{5,6},{7,8},{9,10},{11,12},{13,14},{2,1},{4,3},{6,5},{... | collective-permute-start | bytes 589832 | tf_op jit(solution)/shard_map/ppermute | solution.py:306
  8.8 8.2 %collective-permute-start.2 = (bf16[864,128]{1,0:T(8,128)(2,1)S(1)}, bf16[864,128]{1,0:T(8,128)(2,1)S(1)}, u32[]{:S(2)}, u32[]{:S(2)}) collective-permute-start(bf16[864,128]{1,0:T(8,128)(2,1)S(1)} %get-tuple-element.20), channel_id=1, source_target_pairs={{0,1},{1,0},{2,3},{3,2},{4,5},{5,4},{6,7},{7,6},{8,9},{9,8},{10,11... | collective-permute-start | bytes 663560 | tf_op jit(solution)/shard_map/ppermute | solution.py:300
  15.9 1.3 %collective-permute-start.3 = (bf16[128,512]{1,0:T(8,128)(2,1)S(1)}, bf16[128,512]{1,0:T(8,128)(2,1)S(1)}, u32[]{:S(2)}, u32[]{:S(2)}) collective-permute-start(bf16[128,512]{1,0:T(8,128)(2,1)S(1)} %get-tuple-element.17.refs_0_.refs_1_), channel_id=1, source_target_pairs={{0,1},{1,0},{2,3},{3,2},{4,5},{5,4},{6,7},{7,6},{8,9},{9,8},{10,11... | collective-permute-start | bytes 393224 | tf_op jit(solution)/shard_map/ppermute | solution.py:300
  16.0 1.2 %collective-permute-start.4 = (bf16[128,512]{1,0:T(8,128)(2,1)S(1)}, bf16[128,512]{1,0:T(8,128)(2,1)S(1)}, u32[]{:S(2)}, u32[]{:S(2)}) collective-permute-start(bf16[128,512]{1,0:T(8,128)(2,1)S(1)} %get-tuple-element.17.refs_0_.refs_1_), channel_id=1, source_target_pairs={{1,2},{3,4},{5,6},{7,8},{9,10},{11,12},{13,14},{2,1},{4,3},{6,5},{... | collective-permute-start | bytes 393224 | tf_op jit(solution)/shard_map/ppermute | solution.py:306
  17.2 9.6 %copy-start.1 = (bf16[64,27,32]{0,2,1:T(8,128)(2,1)S(1)}, bf16[64,27,32]{0,2,1:T(8,128)(2,1)}, u32[]{:S(2)}) copy-start(bf16[64,27,32]{0,2,1:T(8,128)(2,1)} %param.5) | copy-start | bytes 331780
  20.6 9.7 %collective-permute-start.5 = (bf16[224,128]{1,0:T(8,128)(2,1)S(1)}, bf16[224,128]{1,0:T(8,128)(2,1)S(1)}, u32[]{:S(2)}, u32[]{:S(2)}) collective-permute-start(bf16[224,128]{1,0:T(8,128)(2,1)S(1)} %get-tuple-element.26), channel_id=1, source_target_pairs={{0,1},{1,0},{2,3},{3,2},{4,5},{5,4},{6,7},{7,6},{8,9},{9,8},{10,11... | collective-permute-start | bytes 172040 | tf_op jit(solution)/shard_map/ppermute | solution.py:300
  27.2 6.8 %collective-permute-start.10 = (bf16[432,128]{1,0:T(8,128)(2,1)S(1)}, bf16[432,128]{1,0:T(8,128)(2,1)S(1)}, u32[]{:S(2)}, u32[]{:S(2)}) collective-permute-start(bf16[432,128]{1,0:T(8,128)(2,1)S(1)} %select_convert_fusion), channel_id=1, source_target_pairs={{0,2},{1,3},{2,0},{3,1},{4,6},{5,7},{6,4},{7,5},{8,10},{9,11},{10,... | collective-permute-start | bytes 331784 | tf_op jit(solution)/shard_map/ppermute | solution.py:300
  32.9 4.2 %collective-permute-start.6 = (bf16[224,128]{1,0:T(8,128)(2,1)S(1)}, bf16[224,128]{1,0:T(8,128)(2,1)S(1)}, u32[]{:S(2)}, u32[]{:S(2)}) collective-permute-start(bf16[224,128]{1,0:T(8,128)(2,1)S(1)} %convert_add_fusion.2), channel_id=1, source_target_pairs={{0,2},{1,3},{2,0},{3,1},{4,6},{5,7},{6,4},{7,5},{8,10},{9,11},{10,... | collective-permute-start | bytes 172040 | tf_op jit(solution)/shard_map/ppermute | solution.py:300
  34.1 5.1 %collective-permute-start.11 = (bf16[432,128]{1,0:T(8,128)(2,1)S(1)}, bf16[432,128]{1,0:T(8,128)(2,1)S(1)}, u32[]{:S(2)}, u32[]{:S(2)}) collective-permute-start(bf16[432,128]{1,0:T(8,128)(2,1)S(1)} %add_convert_fusion.2), channel_id=1, source_target_pairs={{0,4},{1,5},{2,6},{3,7},{4,0},{5,1},{6,2},{7,3},{8,12},{9,13},{10,... | collective-permute-start | bytes 331784 | tf_op jit(solution)/shard_map/ppermute | solution.py:300
  37.1 5.0 %collective-permute-start.7 = (bf16[224,128]{1,0:T(8,128)(2,1)S(1)}, bf16[224,128]{1,0:T(8,128)(2,1)S(1)}, u32[]{:S(2)}, u32[]{:S(2)}) collective-permute-start(bf16[224,128]{1,0:T(8,128)(2,1)S(1)} %add_convert_fusion.4), channel_id=1, source_target_pairs={{0,4},{1,5},{2,6},{3,7},{4,0},{5,1},{6,2},{7,3},{8,12},{9,13},{10,... | collective-permute-start | bytes 172040 | tf_op jit(solution)/shard_map/ppermute | solution.py:300
  39.2 8.4 %collective-permute-start.12 = (bf16[432,128]{1,0:T(8,128)(2,1)S(1)}, bf16[432,128]{1,0:T(8,128)(2,1)S(1)}, u32[]{:S(2)}, u32[]{:S(2)}) collective-permute-start(bf16[432,128]{1,0:T(8,128)(2,1)S(1)} %add_convert_fusion.1), channel_id=1, source_target_pairs={{0,8},{1,9},{2,10},{3,11},{4,12},{5,13},{6,14},{7,15},{8,0},{9,1},... | collective-permute-start | bytes 331784 | tf_op jit(solution)/shard_map/ppermute | solution.py:300
  42.1 7.8 %collective-permute-start.8 = (bf16[224,128]{1,0:T(8,128)(2,1)S(1)}, bf16[224,128]{1,0:T(8,128)(2,1)S(1)}, u32[]{:S(2)}, u32[]{:S(2)}) collective-permute-start(bf16[224,128]{1,0:T(8,128)(2,1)S(1)} %add_convert_fusion.3), channel_id=1, source_target_pairs={{0,8},{1,9},{2,10},{3,11},{4,12},{5,13},{6,14},{7,15},{8,0},{9,1},... | collective-permute-start | bytes 172040 | tf_op jit(solution)/shard_map/ppermute | solution.py:300
  47.7 5.0 %collective-permute-start.13 = (bf16[432,128]{1,0:T(8,128)(2,1)S(1)}, bf16[432,128]{1,0:T(8,128)(2,1)S(1)}, u32[]{:S(2)}, u32[]{:S(2)}) collective-permute-start(bf16[432,128]{1,0:T(8,128)(2,1)S(1)} %add_convert_fusion), channel_id=1, source_target_pairs={{0,2},{1,3},{2,0},{3,1},{4,6},{5,7},{6,4},{7,5},{8,10},{9,11},{10,... | collective-permute-start | bytes 331784 | tf_op jit(solution)/shard_map/ppermute | solution.py:300
  49.9 2.8 %collective-permute-start.9 = (f32[224,128]{1,0:T(8,128)S(1)}, f32[224,128]{1,0:T(8,128)S(1)}, u32[]{:S(2)}, u32[]{:S(2)}) collective-permute-start(f32[224,128]{1,0:T(8,128)S(1)} %convert_add_fusion.1), channel_id=1, source_target_pairs={{0,1},{1,0},{2,3},{3,2},{4,5},{5,4},{6,7},{7,6},{8,9},{9,8},{10,11... | collective-permute-start | bytes 344072 | tf_op jit(solution)/shard_map/ppermute | solution.py:300
  52.7 1.5 %collective-permute-start.14 = (bf16[864,128]{1,0:T(8,128)(2,1)S(1)}, bf16[864,128]{1,0:T(8,128)(2,1)S(1)}, u32[]{:S(2)}, u32[]{:S(2)}) collective-permute-start(bf16[864,128]{1,0:T(8,128)(2,1)S(1)} %pad_maximum_fusion), channel_id=1, source_target_pairs={{0,1},{1,0},{2,3},{3,2},{4,5},{5,4},{6,7},{7,6},{8,9},{9,8},{10,11... | collective-permute-start | bytes 663560 | tf_op jit(solution)/shard_map/ppermute | solution.py:300

commit v2 on v1

--- a/solution.py
+++ b/solution.py
@@ -12,11 +12,14 @@
 ROOT = math.sqrt(2.0 / math.pi)
 CUBIC = 0.044715
 THREE = (0, 1, 2)
-VMEM_LIMIT = 50 << 20
-
-
-def kernel_call(body, name, outs, args, scratch=(), flops=0, moved=0):
+VMEM_LIMIT = 20 << 20
+
+
+def kernel_call(body, name, outs, args, scratch=(), flops=0, moved=0, last=False):
     whole = pl.BlockSpec(memory_space=pltpu.VMEM)
+    args = [pltpu.with_memory_space_constraint(arg, pltpu.VMEM) for arg in args]
+    if not last:
+        outs = jax.tree.map(lambda out: pltpu.VMEM(out.shape, out.dtype), outs)
     return pl.pallas_call(
         body,
         name=name,
@@ -53,15 +56,18 @@
     return jnp.where(lane == last, 0.0, pltpu.roll(row, last, 1))
 
 
-def gelu_parts(value):
+def gelu(value):
+    return (0.5 * value) * (1.0 + jnp.tanh(value * (ROOT + ROOT * CUBIC * (value * value))))
+
+
+def gelu_slope(value):
     square = value * value
-    tanh = jnp.tanh(ROOT * value * (1.0 + CUBIC * square))
-    outer = 0.5 * (1.0 + tanh)
-    slope = outer + 0.5 * value * (1.0 - tanh * tanh) * (ROOT * (1.0 + 3.0 * CUBIC * square))
-    return value * outer, slope
-
-
-def forward_kernel(near_ref, own_ref, far_ref, wmid_ref, wtop_ref, cot_ref, delta_ref, slope_ref, vol_ref, pool_ref, *, h, w, spatial):
+    tanh = jnp.tanh(value * (ROOT + ROOT * CUBIC * square))
+    inner = 0.5 * ROOT + 1.5 * ROOT * CUBIC * square
+    return 0.5 + 0.5 * tanh + value * inner * (1.0 - tanh * tanh)
+
+
+def forward_kernel(near_ref, own_ref, far_ref, wmid_ref, wtop_ref, cot_ref, delta_ref, pre_ref, vol_ref, pool_ref, *, h, w, spatial):
     half = w // 2
     here = lax.axis_index("spatial")
     first = here % 2 == 0
@@ -87,7 +93,7 @@
         vol_ref[:, base + (h + 1) * w : base + (h + 2) * w] = zero_row
         for y in range(h):
             vol_ref[:, base + (y + 1) * w : base + (y + 2) * w] = sorted_rows[y * channels : (y + 1) * channels]
-    mid = slope_ref.shape[0]
+    mid = pre_ref.shape[0]
     count = len(planes) - 2
     hp = h // 2
     prow = (hp + 2) * half
@@ -105,13 +111,11 @@
                 odd = slice(y * w + half, (y + 1) * w)
                 pre_even = part[mid : 2 * mid, even] + later(part[:mid, odd]) + part[2 * mid :, odd]
                 pre_odd = part[mid : 2 * mid, odd] + part[:mid, even] + earlier(part[2 * mid :, even])
-                value_even, slope_even = gelu_parts(pre_even)
-                value_odd, slope_odd = gelu_parts(pre_odd)
                 if 0 < j < count - 1:
                     out = ((j - 1) * h + y) * w
-                    slope_ref[:, out : out + half] = slope_even * 0.125
-                    slope_ref[:, out + half : out + w] = slope_odd * 0.125
-                both = value_even + value_odd
+                    pre_ref[:, out : out + half] = pre_even
+                    pre_ref[:, out + half : out + w] = pre_odd
+                both = gelu(pre_even) + gelu(pre_odd)
                 sums[y // 2] = both if sums[y // 2] is None else sums[y // 2] + both
         base = pz * prow
         pool_ref[:, base : base + half] = pool_zero
@@ -133,17 +137,26 @@
         )
         pre_top = dot(wtop_ref[...], cols, ((0,), (0,)))
         at = slice(j * hp * half, (j + 1) * hp * half)
-        delta_ref[:, at] = (cot_ref[:, at].astype(F32) * gelu_parts(pre_top)[1]).astype(BF16)
+        delta_ref[:, at] = (cot_ref[:, at].astype(F32) * gelu_slope(pre_top)).astype(BF16)
 
 
 def halve(whole_ref, keep_ref, send_ref):
     core = lax.axis_index("spatial") % 2
     rows = keep_ref.shape[0]
     keep_ref[...] = whole_ref[pl.ds(pl.multiple_of(core * rows, 16), rows), :]
-    send_ref[...] = whole_ref[pl.ds(pl.multiple_of((1 - core) * rows, 16), rows), :].astype(BF16)
+    sent = whole_ref[pl.ds(pl.multiple_of((1 - core) * rows, 16), rows), :].astype(BF16)
+    send_ref[send_ref.shape[0] - rows :, :] = sent
+
+
+def slope_kernel(pre_ref, slope_ref):
+    for at in range(0, pre_ref.shape[1], 128):
+        slope_ref[:, at : at + 128] = 0.125 * gelu_slope(pre_ref[:, at : at + 128])
 
 
 def top_kernel(delta_ref, pool_ref, keep_ref, send_ref, out_ref, *, hp, wp):
+    cout = delta_ref.shape[0]
+    for at in range(0, delta_ref.shape[1], wp):
+        send_ref[at // wp * cout : (at // wp + 1) * cout, :] = delta_ref[:, at : at + wp]
     prow = (hp + 2) * wp
     planes = delta_ref.shape[1] // (hp * wp)
     for a in THREE:
@@ -170,7 +183,10 @@
         if z // depth == 1:
             plane = own_ref[:, at]
         else:
-            plane = jnp.where((here % 2 == 0) == (z < depth), far_ref[:, at], near_ref[:, at])
+            cout = own_ref.shape[0]
+            blocks = range((z % depth) * hp, (z % depth + 1) * hp)
+            near = jnp.concatenate([near_ref[k * cout : (k + 1) * cout, :] for k in blocks], axis=1)
+            plane = jnp.where((here % 2 == 0) == (z < depth), far_ref[:, at], near)
         base = z * trow
         top_ref[:, base : base + half] = top_zero
         top_ref[:, base + half : base + (hp + 1) * half] = plane
@@ -279,20 +295,29 @@
             out_ref[:, (z * h + y) * w : (z * h + y + 1) * w] = joined[y * ch : (y + 1) * ch]
 
 
-def finish_kernel(low_ref, high_ref, out_ref, *, scale):
-    rows = out_ref.shape[0] // 3
-    mid = out_ref.shape[1]
-    whole = jnp.concatenate([low_ref[...], high_ref[...]], axis=0) * scale
+def finish_kernel(own_ref, other_ref, top_ref, mid_ref, *, scale_top, scale_mid):
+    core = lax.axis_index("spatial") % 2
+    top_rows = top_ref.shape[0] // 2
+    top_ref[pl.ds(pl.multiple_of(core * top_rows, 16), top_rows), :] = own_ref[:top_rows].astype(F32) * scale_top
+    top_ref[pl.ds(pl.multiple_of((1 - core) * top_rows, 16), top_rows), :] = other_ref[:top_rows].astype(F32) * scale_top
+    mid_rows = (own_ref.shape[0] - top_rows) // 2
+    own = own_ref[top_rows : top_rows + mid_rows].astype(F32) + own_ref[top_rows + mid_rows :].astype(F32)
+    other = other_ref[top_rows : top_rows + mid_rows].astype(F32) + other_ref[top_rows + mid_rows :].astype(F32)
+    low = jnp.where(core == 0, own, other)
+    high = jnp.where(core == 0, other, own)
+    whole = jnp.concatenate([low, high], axis=0) * scale_mid
+    rows = mid_ref.shape[0] // 3
+    mid = mid_ref.shape[1]
     q = rows // 9
     for ab in range(9):
         block = whole[ab * q : (ab + 1) * q]
-        out_ref[(3 * ab) * q : (3 * ab + 1) * q, :] = block[:, :mid]
-        out_ref[(3 * ab + 1) * q : (3 * ab + 2) * q, :] = block[:, mid:]
+        mid_ref[(3 * ab) * q : (3 * ab + 1) * q, :] = block[:, :mid]
+        mid_ref[(3 * ab + 1) * q : (3 * ab + 2) * q, :] = block[:, mid:]
     half_rows = rows // 2
     last = whole[rows : rows + half_rows]
     last = jnp.concatenate([last[:, :mid], last[:, mid:]], axis=0)
     for ab in range(9):
-        out_ref[(3 * ab + 2) * q : (3 * ab + 3) * q, :] = last[ab * q : (ab + 1) * q]
+        mid_ref[(3 * ab + 2) * q : (3 * ab + 3) * q, :] = last[ab * q : (ab + 1) * q]
 
 
 def partner(block, bit):
@@ -307,24 +332,25 @@
 
 
 def bit_is_clear(bit):
-    return (lax.axis_index("spatial") // bit) % 2 == 0
-
-
-def add_both(block, bit):
-    rounded = block.astype(BF16)
-    return rounded.astype(F32) + partner(rounded, bit).astype(F32)
-
-
-def halves(block, bit):
+    return (lax.axis_index("spatial") & bit) == 0
+
+
+def rounded(block):
+    return lax.optimization_barrier(block.astype(BF16))
+
+
+def add_both(sent, bit):
+    return sent.astype(F32) + partner(sent, bit).astype(F32)
+
+
+def halves(block, low):
     rows = block.shape[0] // 2
-    low = bit_is_clear(bit)
     mine = jnp.where(low, block[:rows], block[rows:])
     other = jnp.where(low, block[rows:], block[:rows])
-    return mine, other.astype(BF16)
-
-
-def in_order(block, other, bit):
-    low = bit_is_clear(bit)
+    return mine, rounded(other)
+
+
+def in_order(block, other, low):
     return jnp.where(low, block, other), jnp.where(low, other, block)
 
 
@@ -339,9 +365,9 @@
     cout, nzp, hp, wp = cotangent.shape
     shape = jax.ShapeDtypeStruct
     plane = h * w
+    volume, first_core, low = lax.optimization_barrier((volume, bit_is_clear(1), bit_is_clear(2)))
     flat = volume.reshape(cin, nz * plane)
     early, late = flat[:, : (nz - 1) * plane], flat[:, plane:]
-    first_core = bit_is_clear(1)
     far = across(jnp.where(first_core, early, late))
     near = partner(jnp.where(first_core, late, early), 1)
     split = weights_mid.reshape(mid, 9, 3, cin)
@@ -349,8 +375,9 @@
     wback = jnp.transpose(split, (2, 3, 1, 0)).reshape(3 * cin, 9 * mid)
     wtop = jnp.transpose(weights_top, (1, 2, 0)).reshape(27 * mid, cout)
     cot = cotangent.reshape(cout, nzp * hp * wp)
+    near, far, wback = lax.optimization_barrier((near, far, wback))
     padded = (3 * nz - 2) * (h + 2) * w
-    delta, slope, vol, pool = kernel_call(
+    delta, pre, vol, pool = kernel_call(
         lambda *refs: forward_kernel(*refs, h=h, w=w, spatial=spatial),
         "forward",
         (
@@ -364,27 +391,21 @@
         moved=6_000_000,
     )
     delta_far = across(delta)
-    delta_near = partner(delta, 1)
     top_rows = 27 * mid
+    delta_rows = delta.size // cout
     keep, send = kernel_call(
         lambda *refs: top_kernel(*refs, hp=hp, wp=wp),
         "top_part",
-        (shape((top_rows // 2, cout), F32), shape((top_rows // 2, cout), BF16)),
+        (shape((top_rows // 2, cout), F32), shape((delta_rows + top_rows // 2, cout), BF16)),
         (delta, pool),
         scratch=(pltpu.VMEM((top_rows, cout), F32),),
         flops=226_000_000,
         moved=1_500_000,
     )
-    top_sum = keep + partner(send, 1).astype(F32)
-    mine, other = halves(top_sum, 2)
-    other, delta_near, delta_far = lax.optimization_barrier((other, delta_near, delta_far))
-    top_sum = mine + partner(other, 2).astype(F32)
-    for bit in far_bits():
-        top_sum = add_both(top_sum, bit)
-    top_sum = top_sum.astype(BF16)
-    top_sum = jnp.concatenate(in_order(top_sum, partner(top_sum, 2), 2), axis=0)
-    top_sum = jnp.concatenate(in_order(top_sum, partner(top_sum, 1), 1), axis=0)
-    top_grad = top_sum.astype(F32) * (1.0 / math.sqrt(nzp * hp * wp * spatial))
+    slope = kernel_call(slope_kernel, "slope", shape(pre.shape, F32), (pre,), flops=100_000_000, moved=3_000_000)
+    delta_near = partner(send, 1)
+    mine, other = halves(keep + delta_near[delta_rows:].astype(F32), low)
+    top_received = partner(other, 2)
     mid_rows = -(-27 * cin // 64) * 16
     keep, send, field = kernel_call(
         lambda *refs: backward_kernel(*refs, h=h, w=w, spatial=spatial),
@@ -403,18 +424,17 @@
         flops=900_000_000,
         moved=5_000_000,
     )
-    mid_sum = keep + partner(send, 1).astype(F32)
-    mid_sum, field = lax.optimization_barrier((mid_sum, field))
-    for bit in [2] + far_bits():
-        mid_sum = add_both(mid_sum, bit)
-    mid_low, mid_high = in_order(mid_sum, partner(mid_sum, 1), 1)
-    mid_grad = kernel_call(
-        lambda *refs: finish_kernel(*refs, scale=1.0 / math.sqrt(nz * plane * spatial)),
-        "finish",
-        shape((27 * cin, mid), F32),
-        (mid_low, mid_high),
-        moved=1_000_000,
-    )
+    keep, send, mine, top_received = lax.optimization_barrier((keep, send, mine, top_received))
+    top_sum = rounded(mine + top_received.astype(F32))
+    bits = far_bits()
+    top_sum = rounded(add_both(top_sum, bits[0]))
+    for bit in bits[1:]:
+        top_sum = rounded(add_both(top_sum, bit))
+    mid_sum = rounded(keep + partner(send, 1).astype(F32))
+    for bit in bits:
+        mid_sum = rounded(add_both(mid_sum, bit))
+        if bit == bits[0]:
+            mid_sum, field = lax.optimization_barrier((mid_sum, field))
     input_grad = kernel_call(
         lambda *refs: input_kernel(*refs, h=h, w=w),
         "input_grad",
@@ -422,9 +442,29 @@
         (field, wback),
         flops=452_000_000,
         moved=2_000_000,
-    ).reshape(volume.shape)
+    )
+    both = jnp.concatenate([top_sum, mid_sum], axis=0)
+    both, input_grad = lax.optimization_barrier((both, input_grad))
+    received = partner(both, 2)
+    top_sum = jnp.concatenate(in_order(top_sum, received[: top_sum.shape[0]], low), axis=0)
+    mid_sum = mid_sum.astype(F32) + received[-mid_rows:].astype(F32)
+    mid_high = rounded(mid_sum)
+    mid_low = rounded(mid_sum - mid_high.astype(F32))
+    both = jnp.concatenate([top_sum, mid_high, mid_low], axis=0)
+    top_grad, mid_grad = kernel_call(
+        lambda *refs: finish_kernel(
+            *refs,
+            scale_top=1.0 / math.sqrt(nzp * hp * wp * spatial),
+            scale_mid=1.0 / math.sqrt(nz * plane * spatial),
+        ),
+        "finish",
+        (shape((27 * mid, cout), F32), shape((27 * cin, mid), F32)),
+        (both, partner(both, 1)),
+        moved=2_000_000,
+        last=True,
+    )
     return (
-        input_grad,
+        input_grad.reshape(volume.shape),
         jnp.transpose(mid_grad.reshape(27, cin, mid), (2, 0, 1)),
         jnp.transpose(top_grad.reshape(27, mid, cout), (2, 0, 1)),
     )

time: 55.5 us -> 51.4 us (0.926)
  starting transfers between devices: 30.2 us -> 23.1 us
  waiting for transfers between devices: 8.79 us -> 13.9 us
  Pallas kernels: 10.1 us -> 9.03 us
  other arithmetic: 1.39 us -> 0.39 us
    ppermute x13 -> x10, starting transfers between devices: 28.9 us -> 21.6 us  [partner(): return lax.ppermute(block, 'spatial', [(i, i ^ bit) for i in range(size)])]
    ppermute x13 -> x10, waiting for transfers between devices: 8.79 us -> 13.9 us  [partner(): return lax.ppermute(block, 'spatial', [(i, i ^ bit) for i in range(size)])]
    pallas_call x5 -> x6, Pallas kernels: 10.1 us -> 9.03 us  [kernel_call(): pl.pallas_call(body, name=name, out_shape=outs, in_specs=[whole] * len(ar...]
    mul x1 -> x0, other arithmetic: 0.98 us -> none  [shards(): top_grad = top_sum.astype(F32) * (1.0 / math.sqrt(nzp * hp * wp * spatial))]
  transfers between devices with their start and end apart: 15 -> 12, of which waited for: 8 -> 6; matrix products, arithmetic and copies ran while one was open for 6% -> 6% of each run, Pallas kernels for 5% -> 9%
where the time goes in v2:
time: 51.4 us; the launch traced here: 51.2 us
  starting transfers between devices  23.1 us (45%)
  waiting for transfers between devices  13.9 us (27%)
  Pallas kernels  9.03 us (18%)
  local copies, waits for them, and re-layouts  3.93 us (8%)
  between operations  0.88 us (2%)
    ppermute x10, starting transfers between devices, partner(): return lax.ppermute(block, 'spatial', [(i, i ^ bit) for i in range(size)])  21.6 us
    ppermute x10, waiting for transfers between devices, partner(): return lax.ppermute(block, 'spatial', [(i, i ^ bit) for i in range(size)])  13.9 us
    pallas_call x6, Pallas kernels, kernel_call(): pl.pallas_call(body, name=name, out_shape=outs, in_specs=[whole] * len(ar...  9.03 us
    ppermute x2, starting transfers between devices, across(): return lax.ppermute(block, 'spatial', pairs + [(j, i) for i, j in pairs])  1.46 us
    reshape x2, local copies, waits for them, and re-layouts, shards(): split = weights_mid.reshape(mid, 9, 3, cin)  1.2 us
    reshape x1, local copies, waits for them, and re-layouts, shards(): flat = volume.reshape(cin, nz * plane)  1.17 us
  transfers between devices with their start and end apart: 12, of which 6 were waited for; matrix products, arithmetic and copies ran while one was open for 6% of the time, Pallas kernels for 9%

profile of v2, /device:TPU:0, one launch (start us, length us, event | category | flops | bytes accessed | tf_op | source)
XLA Modules:
  0.0 51.2 jit_solution(7176215054813302834)
XLA Ops:
  0.6 0.0 copy-start.1
  0.6 0.0 copy-start.2
  0.7 1.2 %reshape.33.refs_1_ = bf16[32,4096]{1,0:T(8,128)(2,1)S(1)} reshape(bf16[32,4,4,256]{3,2,1,0:T(4,128)(2,1)} %param.4) | data formatting | bytes 524288 | tf_op jit(solution)/shard_map/reshape | solution.py:369
  1.8 0.0 copy-start
  1.9 0.8 %collective-permute-start.1 = (bf16[32,3072]{1,0:T(8,128)(2,1)S(1)}, bf16[32,3072]{1,0:T(8,128)(2,1)S(1)}, u32[]{:S(2)}, u32[]{:S(2)}) collective-permute-start(bf16[32,3072]{1,0:T(8,128)(2,1)S(1)} %get-tuple-element.55), channel_id=1, source_target_pairs={{1,2},{3,4},{5,6},{7,8},{9,10},{11,12},{13,14},{2,1},{4,3},{6,5},{... | collective-permute-start | bytes 589832 | tf_op jit(solution)/shard_map/ppermute | solution.py:331
  2.7 4.4 %collective-permute-start = (bf16[32,3072]{1,0:T(8,128)(2,1)S(1)}, bf16[32,3072]{1,0:T(8,128)(2,1)S(1)}, u32[]{:S(2)}, u32[]{:S(2)}) collective-permute-start(bf16[32,3072]{1,0:T(8,128)(2,1)S(1)} %get-tuple-element.56), channel_id=1, source_target_pairs={{0,1},{1,0},{2,3},{3,2},{4,5},{5,4},{6,7},{7,6},{8,9},{9,8},{10,11... | collective-permute-start | bytes 589832 | tf_op jit(solution)/shard_map/ppermute | solution.py:325
  7.1 1.1 %copy.15 = bf16[64,9,3,32]{0,2,3,1:T(4,128)(2,1)S(1)} copy(bf16[64,9,3,32]{0,3,2,1:T(8,128)(2,1)} %bitcast.22) | data formatting | bytes 221184 | tf_op jit(solution)/shard_map/reshape | solution.py:373
  8.2 0.0 copy-done.1
  8.2 0.1 copy.14
  8.3 0.0 copy-done.2
  8.3 0.1 reshape.38.refs_5_
  8.4 0.2 reshape.36
  8.6 0.1 copy.11.refs_3_
  8.7 0.2 reshape.35.refs_1_
  9.0 0.0 collective-permute-done.1.refs_2_
  9.0 0.0 collective-permute-done.refs_0_
  9.0 0.0 copy-done
  9.0 2.7 %forward.1 = (bf16[128,512]{1,0:T(8,128)(2,1)S(1)}, f32[64,6144]{1,0:T(8,128)S(1)}, bf16[32,15360]{1,0:T(8,128)(2,1)S(1)}, bf16[192,2048]{1,0:T(8,128)(2,1)S(1)}) custom-call(bf16[32,3072]{1,0:T(8,128)(2,1)S(1)} %collective-permute-done.refs_0_, bf16[32,4096]{1,0:T(8,128)(2,1)S(1)} %reshape.33.refs_1_, bf16[32,3072]{1,0:T(8,128)(2,1)S(1)} %collective-permute-done.1.refs_2_, ...), custom_call_target="tpu_custom_call" | custom-call | flops 1200000000 | bytes 6000000 | tf_op jit(solution)/shard_map/forward/pallas_call | solution.py:23
  11.7 0.7 %top_part.1 = (f32[864,128]{1,0:T(8,128)S(1)}, bf16[1376,128]{1,0:T(8,128)(2,1)S(1)}) custom-call(bf16[128,512]{1,0:T(8,128)(2,1)S(1)} %get-tuple-element.32.refs_0_.refs_1_, bf16[192,2048]{1,0:T(8,128)(2,1)S(1)} %get-tuple-element.33.refs_1_), custom_call_target="tpu_custom_call" | custom-call | flops 226000000 | bytes 1500000 | tf_op jit(solution)/shard_map/top_part/pallas_call | solution.py:23
  12.5 2.7 %collective-permute-start.2 = (bf16[1376,128]{1,0:T(8,128)(2,1)S(1)}, bf16[1376,128]{1,0:T(8,128)(2,1)S(1)}, u32[]{:S(2)}, u32[]{:S(2)}) collective-permute-start(bf16[1376,128]{1,0:T(8,128)(2,1)S(1)} %get-tuple-element.34), channel_id=1, source_target_pairs={{0,1},{1,0},{2,3},{3,2},{4,5},{5,4},{6,7},{7,6},{8,9},{9,8},{10,11... | collective-permute-start | bytes 1056776 | tf_op jit(solution)/shard_map/ppermute | solution.py:325
  15.2 0.7 %collective-permute-start.3 = (bf16[128,512]{1,0:T(8,128)(2,1)S(1)}, bf16[128,512]{1,0:T(8,128)(2,1)S(1)}, u32[]{:S(2)}, u32[]{:S(2)}) collective-permute-start(bf16[128,512]{1,0:T(8,128)(2,1)S(1)} %get-tuple-element.32.refs_0_.refs_1_), channel_id=1, source_target_pairs={{1,2},{3,4},{5,6},{7,8},{9,10},{11,12},{13,14},{2,1},{4,3},{6,5},{... | collective-permute-start | bytes 393224 | tf_op jit(solution)/shard_map/ppermute | solution.py:331
  15.9 0.8 %slope.1.refs_3_ = f32[64,6144]{1,0:T(8,128)S(1)} custom-call(f32[64,6144]{1,0:T(8,128)S(1)} %get-tuple-element.35.pre_ref), custom_call_target="tpu_custom_call" | custom-call | flops 100000000 | bytes 3000000 | tf_op jit(solution)/shard_map/slope/pallas_call | solution.py:23
  16.7 0.0 collective-permute-done.2.refs_0_
  16.7 3.7 %collective-permute-start.4 = (bf16[432,128]{1,0:T(8,128)(2,1)S(1)}, bf16[432,128]{1,0:T(8,128)(2,1)S(1)}, u32[]{:S(2)}, u32[]{:S(2)}) collective-permute-start(bf16[432,128]{1,0:T(8,128)(2,1)S(1)} %select_convert_fusion), channel_id=1, source_target_pairs={{0,2},{1,3},{2,0},{3,1},{4,6},{5,7},{6,4},{7,5},{8,10},{9,11},{10,... | collective-permute-start | bytes 331784 | tf_op jit(solution)/shard_map/ppermute | solution.py:325
  20.5 0.0 collective-permute-done.3.refs_2_
  20.5 1.9 %backward.1 = (f32[224,128]{1,0:T(8,128)S(1)}, bf16[224,128]{1,0:T(8,128)(2,1)S(1)}, bf16[64,9216]{1,0:T(8,128)(2,1)S(1)}) custom-call(bf16[1376,128]{1,0:T(8,128)(2,1)S(1)} %collective-permute-done.2.refs_0_, bf16[128,512]{1,0:T(8,128)(2,1)S(1)} %get-tuple-element.32.refs_0_.refs_1_, bf16[128,512]{1,0:T(8,128)(2,1)S(1)} %collective-permute-done.3.refs_2_, ...), custom_call_target="tpu_custom_call" | custom-call | flops 900000000 | bytes 5000000 | tf_op jit(solution)/shard_map/backward/pallas_call | solution.py:23
  22.4 2.8 %collective-permute-done.4 = bf16[432,128]{1,0:T(8,128)(2,1)S(1)} collective-permute-done((bf16[432,128]{1,0:T(8,128)(2,1)S(1)}, bf16[432,128]{1,0:T(8,128)(2,1)S(1)}, u32[]{:S(2)}, u32[]{:S(2)}) %collective-permute-start.4) | collective-permute-done | bytes 110624 | tf_op jit(solution)/shard_map/ppermute | solution.py:325
  25.2 0.3 collective-permute-start.7
  25.5 0.9 %collective-permute-done.7 = bf16[224,128]{1,0:T(8,128)(2,1)S(1)} collective-permute-done((bf16[224,128]{1,0:T(8,128)(2,1)S(1)}, bf16[224,128]{1,0:T(8,128)(2,1)S(1)}, u32[]{:S(2)}, u32[]{:S(2)}) %collective-permute-start.7) | collective-permute-done | bytes 57376 | tf_op jit(solution)/shard_map/ppermute | solution.py:325
  26.4 2.7 %collective-permute-start.8 = (bf16[224,128]{1,0:T(8,128)(2,1)S(1)}, bf16[224,128]{1,0:T(8,128)(2,1)S(1)}, u32[]{:S(2)}, u32[]{:S(2)}) collective-permute-start(bf16[224,128]{1,0:T(8,128)(2,1)S(1)} %add_convert_fusion.5), channel_id=1, source_target_pairs={{0,4},{1,5},{2,6},{3,7},{4,0},{5,1},{6,2},{7,3},{8,12},{9,13},{10,... | collective-permute-start | bytes 172040 | tf_op jit(solution)/shard_map/ppermute | solution.py:325
  29.1 0.1 collective-permute-start.5
  29.2 2.2 %collective-permute-done.8 = bf16[224,128]{1,0:T(8,128)(2,1)S(1)} collective-permute-done((bf16[224,128]{1,0:T(8,128)(2,1)S(1)}, bf16[224,128]{1,0:T(8,128)(2,1)S(1)}, u32[]{:S(2)}, u32[]{:S(2)}) %collective-permute-start.8) | collective-permute-done | bytes 57376 | tf_op jit(solution)/shard_map/ppermute | solution.py:325
  31.4 3.0 %collective-permute-start.9 = (bf16[224,128]{1,0:T(8,128)(2,1)S(1)}, bf16[224,128]{1,0:T(8,128)(2,1)S(1)}, u32[]{:S(2)}, u32[]{:S(2)}) collective-permute-start(bf16[224,128]{1,0:T(8,128)(2,1)S(1)} %add_convert_fusion.4), channel_id=1, source_target_pairs={{0,8},{1,9},{2,10},{3,11},{4,12},{5,13},{6,14},{7,15},{8,0},{9,1},... | collective-permute-start | bytes 172040 | tf_op jit(solution)/shard_map/ppermute | solution.py:325
  34.4 0.0 collective-permute-done.5
  34.5 3.3 %collective-permute-start.6 = (bf16[432,128]{1,0:T(8,128)(2,1)S(1)}, bf16[432,128]{1,0:T(8,128)(2,1)S(1)}, u32[]{:S(2)}, u32[]{:S(2)}) collective-permute-start(bf16[432,128]{1,0:T(8,128)(2,1)S(1)} %add_convert_fusion.1), channel_id=1, source_target_pairs={{0,8},{1,9},{2,10},{3,11},{4,12},{5,13},{6,14},{7,15},{8,0},{9,1},... | collective-permute-start | bytes 331784 | tf_op jit(solution)/shard_map/ppermute | solution.py:325
  37.8 1.7 %input_grad.1 = bf16[32,4096]{1,0:T(8,128)(2,1)S(1)} custom-call(bf16[64,9216]{1,0:T(8,128)(2,1)S(1)} %get-tuple-element.47.refs_0_, bf16[96,576]{1,0:T(8,128)(2,1)S(1)} %reshape.35.refs_1_), custom_call_target="tpu_custom_call" | custom-call | flops 452000000 | bytes 2000000 | tf_op jit(solution)/shard_map/input_grad/pallas_call | solution.py:23
  39.5 0.0 collective-permute-done.9
  39.5 3.2 %collective-permute-done.6 = bf16[432,128]{1,0:T(8,128)(2,1)S(1)} collective-permute-done((bf16[432,128]{1,0:T(8,128)(2,1)S(1)}, bf16[432,128]{1,0:T(8,128)(2,1)S(1)}, u32[]{:S(2)}, u32[]{:S(2)}) %collective-permute-start.6) | collective-permute-done | bytes 110624 | tf_op jit(solution)/shard_map/ppermute | solution.py:325
  42.8 1.3 %collective-permute-start.10 = (bf16[656,128]{1,0:T(8,128)(2,1)S(1)}, bf16[656,128]{1,0:T(8,128)(2,1)S(1)}, u32[]{:S(2)}, u32[]{:S(2)}) collective-permute-start(bf16[656,128]{1,0:T(8,128)(2,1)S(1)} %pad_maximum_fusion.1), channel_id=1, source_target_pairs={{0,2},{1,3},{2,0},{3,1},{4,6},{5,7},{6,4},{7,5},{8,10},{9,11},{10,... | collective-permute-start | bytes 503816 | tf_op jit(solution)/shard_map/ppermute | solution.py:325
  44.1 4.1 %collective-permute-done.10 = bf16[656,128]{1,0:T(8,128)(2,1)S(1)} collective-permute-done((bf16[656,128]{1,0:T(8,128)(2,1)S(1)}, bf16[656,128]{1,0:T(8,128)(2,1)S(1)}, u32[]{:S(2)}, u32[]{:S(2)}) %collective-permute-start.10) | collective-permute-done | bytes 167968 | tf_op jit(solution)/shard_map/ppermute | solution.py:325
  48.3 0.1 collective-permute-start.11
  48.4 0.9 %reshape.39 = bf16[32,4,4,256]{3,2,1,0:T(4,128)(2,1)} reshape(bf16[32,4096]{1,0:T(8,128)(2,1)S(1)} %input_grad.1) | data formatting | bytes 524288 | tf_op jit(solution)/shard_map/reshape | solution.py:467
  49.3 0.7 %collective-permute-done.11.refs_1_ = bf16[1312,128]{1,0:T(8,128)(2,1)S(1)} collective-permute-done((bf16[1312,128]{1,0:T(8,128)(2,1)S(1)}, bf16[1312,128]{1,0:T(8,128)(2,1)S(1)}, u32[]{:S(2)}, u32[]{:S(2)}) %collective-permute-start.11) | collective-permute-done | bytes 335904 | tf_op jit(solution)/shard_map/ppermute | solution.py:325
  50.0 1.2 %finish.1 = (f32[1728,128]{1,0:T(8,128)}, f32[864,64]{1,0:T(8,128)}) custom-call(bf16[1312,128]{1,0:T(8,128)(2,1)S(1)} %pad_maximum_fusion.refs_0_, bf16[1312,128]{1,0:T(8,128)(2,1)S(1)} %collective-permute-done.11.refs_1_), custom_call_target="tpu_custom_call" | custom-call | bytes 2000000 | tf_op jit(solution)/shard_map/finish/pallas_call | solution.py:23
  (15 shorter events, 0.4 us)
Async XLA Ops:
  0.6 7.6 %copy-start.1 = (bf16[64,27,32]{0,2,1:T(8,128)(2,1)S(1)}, bf16[64,27,32]{0,2,1:T(8,128)(2,1)}, u32[]{:S(2)}) copy-start(bf16[64,27,32]{0,2,1:T(8,128)(2,1)} %param.5) | copy-start | bytes 331780
  0.6 7.7 %copy-start.2 = (bf16[128,2,2,128]{3,2,1,0:T(2,128)(2,1)S(1)}, bf16[128,2,2,128]{3,2,1,0:T(2,128)(2,1)}, u32[]{:S(2)}) copy-start(bf16[128,2,2,128]{3,2,1,0:T(2,128)(2,1)} %param.7) | copy-start | bytes 393220
  1.8 7.2 %copy-start = (bf16[128,27,64]{0,2,1:T(8,128)(2,1)S(1)}, bf16[128,27,64]{0,2,1:T(8,128)(2,1)}, u32[]{:S(2)}) copy-start(bf16[128,27,64]{0,2,1:T(8,128)(2,1)} %param.6) | copy-start | bytes 1327108
  1.9 7.1 %collective-permute-start.1 = (bf16[32,3072]{1,0:T(8,128)(2,1)S(1)}, bf16[32,3072]{1,0:T(8,128)(2,1)S(1)}, u32[]{:S(2)}, u32[]{:S(2)}) collective-permute-start(bf16[32,3072]{1,0:T(8,128)(2,1)S(1)} %get-tuple-element.55), channel_id=1, source_target_pairs={{1,2},{3,4},{5,6},{7,8},{9,10},{11,12},{13,14},{2,1},{4,3},{6,5},{... | collective-permute-start | bytes 589832 | tf_op jit(solution)/shard_map/ppermute | solution.py:331
  2.7 6.3 %collective-permute-start = (bf16[32,3072]{1,0:T(8,128)(2,1)S(1)}, bf16[32,3072]{1,0:T(8,128)(2,1)S(1)}, u32[]{:S(2)}, u32[]{:S(2)}) collective-permute-start(bf16[32,3072]{1,0:T(8,128)(2,1)S(1)} %get-tuple-element.56), channel_id=1, source_target_pairs={{0,1},{1,0},{2,3},{3,2},{4,5},{5,4},{6,7},{7,6},{8,9},{9,8},{10,11... | collective-permute-start | bytes 589832 | tf_op jit(solution)/shard_map/ppermute | solution.py:325
  12.5 4.2 %collective-permute-start.2 = (bf16[1376,128]{1,0:T(8,128)(2,1)S(1)}, bf16[1376,128]{1,0:T(8,128)(2,1)S(1)}, u32[]{:S(2)}, u32[]{:S(2)}) collective-permute-start(bf16[1376,128]{1,0:T(8,128)(2,1)S(1)} %get-tuple-element.34), channel_id=1, source_target_pairs={{0,1},{1,0},{2,3},{3,2},{4,5},{5,4},{6,7},{7,6},{8,9},{9,8},{10,11... | collective-permute-start | bytes 1056776 | tf_op jit(solution)/shard_map/ppermute | solution.py:325
  15.2 5.2 %collective-permute-start.3 = (bf16[128,512]{1,0:T(8,128)(2,1)S(1)}, bf16[128,512]{1,0:T(8,128)(2,1)S(1)}, u32[]{:S(2)}, u32[]{:S(2)}) collective-permute-start(bf16[128,512]{1,0:T(8,128)(2,1)S(1)} %get-tuple-element.32.refs_0_.refs_1_), channel_id=1, source_target_pairs={{1,2},{3,4},{5,6},{7,8},{9,10},{11,12},{13,14},{2,1},{4,3},{6,5},{... | collective-permute-start | bytes 393224 | tf_op jit(solution)/shard_map/ppermute | solution.py:331
  16.7 8.4 %collective-permute-start.4 = (bf16[432,128]{1,0:T(8,128)(2,1)S(1)}, bf16[432,128]{1,0:T(8,128)(2,1)S(1)}, u32[]{:S(2)}, u32[]{:S(2)}) collective-permute-start(bf16[432,128]{1,0:T(8,128)(2,1)S(1)} %select_convert_fusion), channel_id=1, source_target_pairs={{0,2},{1,3},{2,0},{3,1},{4,6},{5,7},{6,4},{7,5},{8,10},{9,11},{10,... | collective-permute-start | bytes 331784 | tf_op jit(solution)/shard_map/ppermute | solution.py:325
  25.2 1.2 %collective-permute-start.7 = (bf16[224,128]{1,0:T(8,128)(2,1)S(1)}, bf16[224,128]{1,0:T(8,128)(2,1)S(1)}, u32[]{:S(2)}, u32[]{:S(2)}) collective-permute-start(bf16[224,128]{1,0:T(8,128)(2,1)S(1)} %get-tuple-element.44), channel_id=1, source_target_pairs={{0,1},{1,0},{2,3},{3,2},{4,5},{5,4},{6,7},{7,6},{8,9},{9,8},{10,11... | collective-permute-start | bytes 172040 | tf_op jit(solution)/shard_map/ppermute | solution.py:325
  26.4 5.0 %collective-permute-start.8 = (bf16[224,128]{1,0:T(8,128)(2,1)S(1)}, bf16[224,128]{1,0:T(8,128)(2,1)S(1)}, u32[]{:S(2)}, u32[]{:S(2)}) collective-permute-start(bf16[224,128]{1,0:T(8,128)(2,1)S(1)} %add_convert_fusion.5), channel_id=1, source_target_pairs={{0,4},{1,5},{2,6},{3,7},{4,0},{5,1},{6,2},{7,3},{8,12},{9,13},{10,... | collective-permute-start | bytes 172040 | tf_op jit(solution)/shard_map/ppermute | solution.py:325
  29.1 5.3 %collective-permute-start.5 = (bf16[432,128]{1,0:T(8,128)(2,1)S(1)}, bf16[432,128]{1,0:T(8,128)(2,1)S(1)}, u32[]{:S(2)}, u32[]{:S(2)}) collective-permute-start(bf16[432,128]{1,0:T(8,128)(2,1)S(1)} %add_convert_fusion.2), channel_id=1, source_target_pairs={{0,4},{1,5},{2,6},{3,7},{4,0},{5,1},{6,2},{7,3},{8,12},{9,13},{10,... | collective-permute-start | bytes 331784 | tf_op jit(solution)/shard_map/ppermute | solution.py:325
  31.4 8.0 %collective-permute-start.9 = (bf16[224,128]{1,0:T(8,128)(2,1)S(1)}, bf16[224,128]{1,0:T(8,128)(2,1)S(1)}, u32[]{:S(2)}, u32[]{:S(2)}) collective-permute-start(bf16[224,128]{1,0:T(8,128)(2,1)S(1)} %add_convert_fusion.4), channel_id=1, source_target_pairs={{0,8},{1,9},{2,10},{3,11},{4,12},{5,13},{6,14},{7,15},{8,0},{9,1},... | collective-permute-start | bytes 172040 | tf_op jit(solution)/shard_map/ppermute | solution.py:325
  34.5 8.2 %collective-permute-start.6 = (bf16[432,128]{1,0:T(8,128)(2,1)S(1)}, bf16[432,128]{1,0:T(8,128)(2,1)S(1)}, u32[]{:S(2)}, u32[]{:S(2)}) collective-permute-start(bf16[432,128]{1,0:T(8,128)(2,1)S(1)} %add_convert_fusion.1), channel_id=1, source_target_pairs={{0,8},{1,9},{2,10},{3,11},{4,12},{5,13},{6,14},{7,15},{8,0},{9,1},... | collective-permute-start | bytes 331784 | tf_op jit(solution)/shard_map/ppermute | solution.py:325
  42.8 5.4 %collective-permute-start.10 = (bf16[656,128]{1,0:T(8,128)(2,1)S(1)}, bf16[656,128]{1,0:T(8,128)(2,1)S(1)}, u32[]{:S(2)}, u32[]{:S(2)}) collective-permute-start(bf16[656,128]{1,0:T(8,128)(2,1)S(1)} %pad_maximum_fusion.1), channel_id=1, source_target_pairs={{0,2},{1,3},{2,0},{3,1},{4,6},{5,7},{6,4},{7,5},{8,10},{9,11},{10,... | collective-permute-start | bytes 503816 | tf_op jit(solution)/shard_map/ppermute | solution.py:325
  48.3 1.7 %collective-permute-start.11 = (bf16[1312,128]{1,0:T(8,128)(2,1)S(1)}, bf16[1312,128]{1,0:T(8,128)(2,1)S(1)}, u32[]{:S(2)}, u32[]{:S(2)}) collective-permute-start(bf16[1312,128]{1,0:T(8,128)(2,1)S(1)} %pad_maximum_fusion.refs_0_), channel_id=1, source_target_pairs={{0,1},{1,0},{2,3},{3,2},{4,5},{5,4},{6,7},{7,6},{8,9},{9,8},{10,11... | collective-permute-start | bytes 1007624 | tf_op jit(solution)/shard_map/ppermute | solution.py:325

commit v3 on v2

--- a/solution.py
+++ b/solution.py
@@ -67,71 +67,113 @@
     return 0.5 + 0.5 * tanh + value * inner * (1.0 - tanh * tanh)
 
 
-def forward_kernel(near_ref, own_ref, far_ref, wmid_ref, wtop_ref, cot_ref, delta_ref, pre_ref, vol_ref, pool_ref, *, h, w, spatial):
+def sort_plane(rows, split, store, h, w):
+    channels = rows[0].shape[0]
+    done = dot(jnp.concatenate(rows, axis=0), split).astype(BF16)
+    store(0, jnp.zeros((channels, w), BF16))
+    store(h + 1, jnp.zeros((channels, w), BF16))
+    for y in range(h):
+        store(y + 1, done[y * channels : (y + 1) * channels])
+
+
+def lanes(start, size):
+    return pl.ds(pl.multiple_of(start, 128), size)
+
+
+def middle_planes(vol_ref, wmid_ref, pre_ref, begin, count, h, w, emit):
     half = w // 2
-    here = lax.axis_index("spatial")
-    first = here % 2 == 0
-    split = parity_matrix(w, False)
-    vrows = h + 2
-    zero_row = jnp.zeros((vol_ref.shape[0], w), BF16)
-    planes = []
-    for part, ref in enumerate((near_ref, own_ref, near_ref)):
-        for start in range(0, ref.shape[1], h * w):
-            planes.append((part, start))
-    channels = vol_ref.shape[0]
-    for z, (part, start) in enumerate(planes):
-        rows = []
-        for at in range(start, start + h * w, w):
-            if part == 1:
-                rows.append(own_ref[:, at : at + w])
-            else:
-                rows.append(jnp.where(first == (part == 0), far_ref[:, at : at + w], near_ref[:, at : at + w]))
-        rows = jnp.concatenate(rows, axis=0)
-        sorted_rows = dot(rows, split).astype(BF16)
-        base = z * vrows * w
-        vol_ref[:, base : base + w] = zero_row
-        vol_ref[:, base + (h + 1) * w : base + (h + 2) * w] = zero_row
-        for y in range(h):
-            vol_ref[:, base + (y + 1) * w : base + (y + 2) * w] = sorted_rows[y * channels : (y + 1) * channels]
     mid = pre_ref.shape[0]
-    count = len(planes) - 2
-    hp = h // 2
-    prow = (hp + 2) * half
-    pool_zero = jnp.zeros((pool_ref.shape[0], half), BF16)
     for pz in range(count // 2):
-        sums = [None] * hp
+        sums = [None] * (h // 2)
         for j in (2 * pz, 2 * pz + 1):
-            cols = jnp.concatenate(
-                [vol_ref[:, ((j + a) * vrows + b) * w : ((j + a) * vrows + b + h) * w] for a in THREE for b in THREE],
-                axis=0,
-            )
+            at = (begin + j) * (h + 2) * w
+            cols = jnp.concatenate([vol_ref[:, lanes(at + (a * (h + 2) + b) * w, h * w)] for a in THREE for b in THREE], axis=0)
             part = dot(wmid_ref[...], cols)
             for y in range(h):
                 even = slice(y * w, y * w + half)
                 odd = slice(y * w + half, (y + 1) * w)
                 pre_even = part[mid : 2 * mid, even] + later(part[:mid, odd]) + part[2 * mid :, odd]
                 pre_odd = part[mid : 2 * mid, odd] + part[:mid, even] + earlier(part[2 * mid :, even])
-                if 0 < j < count - 1:
-                    out = ((j - 1) * h + y) * w
-                    pre_ref[:, out : out + half] = pre_even
-                    pre_ref[:, out + half : out + w] = pre_odd
+                out = (j * h + y) * w
+                pre_ref[:, out : out + half] = pre_even
+                pre_ref[:, out + half : out + w] = pre_odd
                 both = gelu(pre_even) + gelu(pre_odd)
                 sums[y // 2] = both if sums[y // 2] is None else sums[y // 2] + both
-        base = pz * prow
-        pool_ref[:, base : base + half] = pool_zero
-        pool_ref[:, base + (hp + 1) * half : base + prow] = pool_zero
-        for y in range(hp):
-            row = sums[y] * 0.125
-            if pz == 0:
-                row = jnp.where(here == 0, 0.0, row)
-            if pz == count // 2 - 1:
-                row = jnp.where(here == spatial - 1, 0.0, row)
-            row = row.astype(BF16).astype(F32)
-            at = slice(base + (y + 1) * half, base + (y + 2) * half)
-            pool_ref[:mid, at] = later(row).astype(BF16)
-            pool_ref[mid : 2 * mid, at] = row.astype(BF16)
-            pool_ref[2 * mid :, at] = earlier(row).astype(BF16)
-    for j in range(count // 2 - 2):
+        emit(pz, [row * 0.125 for row in sums])
+
+
+def pool_rows(pool_ref, base, rows, outside):
+    mid, half = rows[0].shape
+    zero = jnp.zeros((3 * mid, half), BF16)
+    pool_ref[:, lanes(base, half)] = zero
+    pool_ref[:, lanes(base + (len(rows) + 1) * half, half)] = zero
+    for y, row in enumerate(rows):
+        row = jnp.where(outside, 0.0, row).astype(BF16)
+        wide = row.astype(F32)
+        at = lanes(base + (y + 1) * half, half)
+        pool_ref[:mid, at] = later(wide).astype(BF16)
+        pool_ref[mid : 2 * mid, at] = row
+        pool_ref[2 * mid :, at] = earlier(wide).astype(BF16)
+
+
+def near_kernel(near_ref, own_ref, wmid_ref, vol_ref, pre_ref, pool_ref, *, h, w, spatial):
+    here = lax.axis_index("spatial")
+    core = here % 2
+    split = parity_matrix(w, False)
+    size = (h + 2) * w
+    halo = near_ref.shape[1] // (h * w)
+    own = own_ref.shape[1] // (h * w)
+    for ref, count, start in ((own_ref, own, core * halo), (near_ref, halo, (1 - core) * own)):
+        for z in range(count):
+            rows = [ref[:, (z * h + y) * w : (z * h + y + 1) * w] for y in range(h)]
+
+            def store(row, value, at=(start + z) * size):
+                vol_ref[:, lanes(at + row * w, w)] = value
+
+            sort_plane(rows, split, store, h, w)
+    count = pre_ref.shape[1] // (h * w)
+    pooled = count // 2
+    prow = pool_ref.shape[1] // pooled
+
+    def emit(pz, rows):
+        first = (core == 1) & (here == 0) if pz == 0 else False
+        last = (core == 0) & (here == spatial - 1) if pz == pooled - 1 else False
+        pool_rows(pool_ref, pz * prow, rows, jnp.logical_or(first, last))
+
+    middle_planes(vol_ref, wmid_ref, pre_ref, 1 - core, count, h, w, emit)
+
+
+def far_kernel(
+    far_ref, vol_near_ref, pool_near_ref, wmid_ref, wtop_ref, cot_ref, delta_ref, pre_ref, vol_ref, pool_ref, *, h, w, spatial
+):
+    half = w // 2
+    here = lax.axis_index("spatial")
+    core = here % 2
+    split = parity_matrix(w, False)
+    size = (h + 2) * w
+    halo = far_ref.shape[1] // (h * w)
+    known = vol_near_ref.shape[1]
+    vol_ref[:, lanes((1 - core) * halo * size, known)] = vol_near_ref[...]
+    for z in range(halo):
+        rows = [far_ref[:, (z * h + y) * w : (z * h + y + 1) * w] for y in range(h)]
+
+        def store(row, value, at=core * known + z * size):
+            vol_ref[:, lanes(at + row * w, w)] = value
+
+        sort_plane(rows, split, store, h, w)
+    count = pre_ref.shape[1] // (h * w)
+    pooled = count // 2
+    hp = h // 2
+    prow = (hp + 2) * half
+    pool_ref[:, lanes((1 - core) * pooled * prow, pooled * prow)] = pool_near_ref[...]
+
+    def emit(pz, rows):
+        first = (core == 0) & (here == 0) if pz == 0 else False
+        last = (core == 1) & (here == spatial - 1) if pz == pooled - 1 else False
+        pool_rows(pool_ref, (core * pooled + pz) * prow, rows, jnp.logical_or(first, last))
+
+    middle_planes(vol_ref, wmid_ref, pre_ref, core * count, count, h, w, emit)
+    for j in range(delta_ref.shape[1] // (hp * half)):
         cols = jnp.concatenate(
             [pool_ref[:, (j + a) * prow + b * half : (j + a) * prow + (b + hp) * half] for a in THREE for b in THREE], axis=0
         )
@@ -148,9 +190,13 @@
     send_ref[send_ref.shape[0] - rows :, :] = sent
 
 
-def slope_kernel(pre_ref, slope_ref):
-    for at in range(0, pre_ref.shape[1], 128):
-        slope_ref[:, at : at + 128] = 0.125 * gelu_slope(pre_ref[:, at : at + 128])
+def slope_kernel(near_ref, far_ref, slope_ref, *, plane):
+    core = lax.axis_index("spatial") % 2
+    part = slope_ref.shape[1] // 2
+    for ref, side in ((near_ref, 1 - core), (far_ref, core)):
+        for at in range(0, part, 128):
+            value = 0.125 * gelu_slope(ref[:, lanes((1 - side) * plane + at, 128)])
+            slope_ref[:, lanes(side * part + at, 128)] = value
 
 
 def top_kernel(delta_ref, pool_ref, keep_ref, send_ref, out_ref, *, hp, wp):
@@ -365,7 +411,7 @@
     cout, nzp, hp, wp = cotangent.shape
     shape = jax.ShapeDtypeStruct
     plane = h * w
-    volume, first_core, low = lax.optimization_barrier((volume, bit_is_clear(1), bit_is_clear(2)))
+    volume, first_core, low = lax.optimization_barrier((volume, bit_is_clear(1), bit_is_clear(4)))
     flat = volume.reshape(cin, nz * plane)
     early, late = flat[:, : (nz - 1) * plane], flat[:, plane:]
     far = across(jnp.where(first_core, early, late))
@@ -375,20 +421,35 @@
     wback = jnp.transpose(split, (2, 3, 1, 0)).reshape(3 * cin, 9 * mid)
     wtop = jnp.transpose(weights_top, (1, 2, 0)).reshape(27 * mid, cout)
     cot = cotangent.reshape(cout, nzp * hp * wp)
-    near, far, wback = lax.optimization_barrier((near, far, wback))
-    padded = (3 * nz - 2) * (h + 2) * w
-    delta, pre, vol, pool = kernel_call(
-        lambda *refs: forward_kernel(*refs, h=h, w=w, spatial=spatial),
-        "forward",
+    size = (h + 2) * w
+    count = nz // 2 + 2
+    halo = nz - 1
+    pool_size = (hp + 2) * wp
+    vol_near, pre_near, pool_near = kernel_call(
+        lambda *refs: near_kernel(*refs, h=h, w=w, spatial=spatial),
+        "near_side",
+        (
+            shape((cin, (nz + halo) * size), BF16),
+            shape((mid, count * plane), F32),
+            shape((3 * mid, count // 2 * pool_size), BF16),
+        ),
+        (near, flat, wmid),
+        flops=900_000_000,
+        moved=3_000_000,
+    )
+    far, wback, vol_near, pool_near = lax.optimization_barrier((far, wback, vol_near, pool_near))
+    delta, pre_far, vol, pool = kernel_call(
+        lambda *refs: far_kernel(*refs, h=h, w=w, spatial=spatial),
+        "far_side",
         (
             shape(cot.shape, BF16),
-            shape((mid, (nz + 2) * plane), F32),
-            shape((cin, padded), BF16),
-            shape((3 * mid, (nzp + 2) * (hp + 2) * wp), BF16),
+            shape((mid, count * plane), F32),
+            shape((cin, (nz + 2 * halo) * size), BF16),
+            shape((3 * mid, count * pool_size), BF16),
         ),
-        (near, flat, far, wmid, wtop, cot),
-        flops=1_200_000_000,
-        moved=6_000_000,
+        (far, vol_near, pool_near, wmid, wtop, cot),
+        flops=900_000_000,
+        moved=4_000_000,
     )
     delta_far = across(delta)
     top_rows = 27 * mid
@@ -402,10 +463,17 @@
         flops=226_000_000,
         moved=1_500_000,
     )
-    slope = kernel_call(slope_kernel, "slope", shape(pre.shape, F32), (pre,), flops=100_000_000, moved=3_000_000)
+    slope = kernel_call(
+        lambda *refs: slope_kernel(*refs, plane=plane),
+        "slope",
+        shape((mid, (nz + 2) * plane), F32),
+        (pre_near, pre_far),
+        flops=100_000_000,
+        moved=3_000_000,
+    )
     delta_near = partner(send, 1)
     mine, other = halves(keep + delta_near[delta_rows:].astype(F32), low)
-    top_received = partner(other, 2)
+    top_received = partner(other, 4)
     mid_rows = -(-27 * cin // 64) * 16
     keep, send, field = kernel_call(
         lambda *refs: backward_kernel(*refs, h=h, w=w, spatial=spatial),
@@ -426,15 +494,17 @@
     )
     keep, send, mine, top_received = lax.optimization_barrier((keep, send, mine, top_received))
     top_sum = rounded(mine + top_received.astype(F32))
-    bits = far_bits()
-    top_sum = rounded(add_both(top_sum, bits[0]))
-    for bit in bits[1:]:
+    bits = far_bits()[1:]
+    top_sum, send = lax.optimization_barrier((top_sum, send))
+    for bit in bits:
         top_sum = rounded(add_both(top_sum, bit))
     mid_sum = rounded(keep + partner(send, 1).astype(F32))
+    mid_sum = rounded(add_both(mid_sum, 2))
+    top_sum, mid_sum = lax.optimization_barrier((top_sum, mid_sum))
+    mid_sum, field = lax.optimization_barrier((mid_sum, field))
     for bit in bits:
         mid_sum = rounded(add_both(mid_sum, bit))
-        if bit == bits[0]:
-            mid_sum, field = lax.optimization_barrier((mid_sum, field))
+    top_sum = rounded(add_both(top_sum, 2))
     input_grad = kernel_call(
         lambda *refs: input_kernel(*refs, h=h, w=w),
         "input_grad",
@@ -445,7 +515,7 @@
     )
     both = jnp.concatenate([top_sum, mid_sum], axis=0)
     both, input_grad = lax.optimization_barrier((both, input_grad))
-    received = partner(both, 2)
+    received = partner(both, 4)
     top_sum = jnp.concatenate(in_order(top_sum, received[: top_sum.shape[0]], low), axis=0)
     mid_sum = mid_sum.astype(F32) + received[-mid_rows:].astype(F32)
     mid_high = rounded(mid_sum)

time: 51.4 us -> 49.9 us (0.971)
  starting transfers between devices: 23.1 us -> 21.3 us
  Pallas kernels: 9.03 us -> 9.88 us
    ppermute x10, starting transfers between devices: 21.6 us -> 19.9 us  [partner(): return lax.ppermute(block, 'spatial', [(i, i ^ bit) for i in range(size)])]
    pallas_call x6 -> x7, Pallas kernels: 9.03 us -> 9.88 us  [kernel_call(): pl.pallas_call(body, name=name, out_shape=outs, in_specs=[whole] * len(ar...]
    ppermute x10, waiting for transfers between devices: 13.9 us -> 13.4 us  [partner(): return lax.ppermute(block, 'spatial', [(i, i ^ bit) for i in range(size)])]
  transfers between devices with their start and end apart: 12 -> 12, of which waited for: 6 -> 5; matrix products, arithmetic and copies ran while one was open for 6% -> 6% of each run, Pallas kernels for 9% -> 12%
where the time goes in v3:
time: 49.9 us; the launch traced here: 49.8 us
  starting transfers between devices  21.3 us (43%)
  waiting for transfers between devices  13.4 us (27%)
  Pallas kernels  9.88 us (20%)
  local copies, waits for them, and re-layouts  3.93 us (8%)
  between operations  0.92 us (2%)
    ppermute x10, starting transfers between devices, partner(): return lax.ppermute(block, 'spatial', [(i, i ^ bit) for i in range(size)])  19.9 us
    ppermute x10, waiting for transfers between devices, partner(): return lax.ppermute(block, 'spatial', [(i, i ^ bit) for i in range(size)])  13.4 us
    pallas_call x7, Pallas kernels, kernel_call(): pl.pallas_call(body, name=name, out_shape=outs, in_specs=[whole] * len(ar...  9.88 us
    ppermute x2, starting transfers between devices, across(): return lax.ppermute(block, 'spatial', pairs + [(j, i) for i, j in pairs])  1.32 us
    reshape x2, local copies, waits for them, and re-layouts, shards(): split = weights_mid.reshape(mid, 9, 3, cin)  1.21 us
    reshape x1, local copies, waits for them, and re-layouts, shards(): flat = volume.reshape(cin, nz * plane)  1.17 us
  transfers between devices with their start and end apart: 12, of which 5 were waited for; matrix products, arithmetic and copies ran while one was open for 6% of the time, Pallas kernels for 12%

profile of v3, /device:TPU:0, one launch (start us, length us, event | category | flops | bytes accessed | tf_op | source)
XLA Modules:
  0.0 49.8 jit_solution(12727019483030919865)
XLA Ops:
  0.6 0.0 copy-start.1
  0.7 1.2 %reshape.33.refs_1_ = bf16[32,4096]{1,0:T(8,128)(2,1)S(1)} reshape(bf16[32,4,4,256]{3,2,1,0:T(4,128)(2,1)} %param.4) | data formatting | bytes 524288 | tf_op jit(solution)/shard_map/reshape | solution.py:415
  1.8 0.0 copy-start.2
  1.9 0.5 %collective-permute-start.1 = (bf16[32,3072]{1,0:T(8,128)(2,1)S(1)}, bf16[32,3072]{1,0:T(8,128)(2,1)S(1)}, u32[]{:S(2)}, u32[]{:S(2)}) collective-permute-start(bf16[32,3072]{1,0:T(8,128)(2,1)S(1)} %get-tuple-element.71), channel_id=1, source_target_pairs={{0,1},{1,0},{2,3},{3,2},{4,5},{5,4},{6,7},{7,6},{8,9},{9,8},{10,11... | collective-permute-start | bytes 589832 | tf_op jit(solution)/shard_map/ppermute | solution.py:371
  2.4 0.7 %collective-permute-start = (bf16[32,3072]{1,0:T(8,128)(2,1)S(1)}, bf16[32,3072]{1,0:T(8,128)(2,1)S(1)}, u32[]{:S(2)}, u32[]{:S(2)}) collective-permute-start(bf16[32,3072]{1,0:T(8,128)(2,1)S(1)} %get-tuple-element.72), channel_id=1, source_target_pairs={{1,2},{3,4},{5,6},{7,8},{9,10},{11,12},{13,14},{2,1},{4,3},{6,5},{... | collective-permute-start | bytes 589832 | tf_op jit(solution)/shard_map/ppermute | solution.py:377
  3.1 1.1 %copy.16 = bf16[64,9,3,32]{0,2,3,1:T(4,128)(2,1)S(1)} copy(bf16[64,9,3,32]{0,3,2,1:T(8,128)(2,1)} %bitcast.22) | data formatting | bytes 221184 | tf_op jit(solution)/shard_map/reshape | solution.py:419
  4.2 0.0 copy-done.1
  4.2 0.1 copy.15
  4.3 0.2 reshape.36
  4.5 0.1 copy.11.refs_2_.refs_3_
  4.6 0.2 reshape.35.refs_1_
  4.9 0.0 copy-done.2
  4.9 0.1 reshape.38.refs_5_
  5.0 0.0 copy-start
  5.0 0.0 collective-permute-done.1.refs_0_
  5.0 1.5 %near_side.1 = (bf16[32,10752]{1,0:T(8,128)(2,1)S(1)}, f32[64,4096]{1,0:T(8,128)S(1)}, bf16[192,1024]{1,0:T(8,128)(2,1)S(1)}) custom-call(bf16[32,3072]{1,0:T(8,128)(2,1)S(1)} %collective-permute-done.1.refs_0_, bf16[32,4096]{1,0:T(8,128)(2,1)S(1)} %reshape.33.refs_1_, bf16[192,288]{1,0:T(8,128)(2,1)S(1)} %copy.11.refs_2_.refs_3_), custom_call_target="tpu_custom_call" | custom-call | flops 900000000 | bytes 3000000 | tf_op jit(solution)/shard_map/near_side/pallas_call | solution.py:23
  6.5 0.0 collective-permute-done.refs_0_
  6.5 0.0 copy-done
  6.5 2.1 %far_side.1 = (bf16[128,512]{1,0:T(8,128)(2,1)S(1)}, f32[64,4096]{1,0:T(8,128)S(1)}, bf16[32,15360]{1,0:T(8,128)(2,1)S(1)}, bf16[192,2048]{1,0:T(8,128)(2,1)S(1)}) custom-call(bf16[32,3072]{1,0:T(8,128)(2,1)S(1)} %collective-permute-done.refs_0_, bf16[32,10752]{1,0:T(8,128)(2,1)S(1)} %get-tuple-element.41.refs_1_, ...), custom_call_target="tpu_custom_call" | custom-call | flops 900000000 | bytes 4000000 | tf_op jit(solution)/shard_map/far_side/pallas_call | solution.py:23
  8.6 0.7 %top_part.1 = (f32[864,128]{1,0:T(8,128)S(1)}, bf16[1376,128]{1,0:T(8,128)(2,1)S(1)}) custom-call(bf16[128,512]{1,0:T(8,128)(2,1)S(1)} %get-tuple-element.43.refs_0_.refs_1_, bf16[192,2048]{1,0:T(8,128)(2,1)S(1)} %get-tuple-element.44.refs_1_), custom_call_target="tpu_custom_call" | custom-call | flops 226000000 | bytes 1500000 | tf_op jit(solution)/shard_map/top_part/pallas_call | solution.py:23
  9.3 5.2 %collective-permute-start.2 = (bf16[1376,128]{1,0:T(8,128)(2,1)S(1)}, bf16[1376,128]{1,0:T(8,128)(2,1)S(1)}, u32[]{:S(2)}, u32[]{:S(2)}) collective-permute-start(bf16[1376,128]{1,0:T(8,128)(2,1)S(1)} %get-tuple-element.45), channel_id=1, source_target_pairs={{0,1},{1,0},{2,3},{3,2},{4,5},{5,4},{6,7},{7,6},{8,9},{9,8},{10,11... | collective-permute-start | bytes 1056776 | tf_op jit(solution)/shard_map/ppermute | solution.py:371
  14.5 0.7 %collective-permute-start.3 = (bf16[128,512]{1,0:T(8,128)(2,1)S(1)}, bf16[128,512]{1,0:T(8,128)(2,1)S(1)}, u32[]{:S(2)}, u32[]{:S(2)}) collective-permute-start(bf16[128,512]{1,0:T(8,128)(2,1)S(1)} %get-tuple-element.43.refs_0_.refs_1_), channel_id=1, source_target_pairs={{1,2},{3,4},{5,6},{7,8},{9,10},{11,12},{13,14},{2,1},{4,3},{6,5},{... | collective-permute-start | bytes 393224 | tf_op jit(solution)/shard_map/ppermute | solution.py:377
  15.2 0.8 %slope.1.refs_3_ = f32[64,6144]{1,0:T(8,128)S(1)} custom-call(f32[64,4096]{1,0:T(8,128)S(1)} %get-tuple-element.46.refs_0_, f32[64,4096]{1,0:T(8,128)S(1)} %get-tuple-element.47.refs_1_), custom_call_target="tpu_custom_call" | custom-call | flops 100000000 | bytes 3000000 | tf_op jit(solution)/shard_map/slope/pallas_call | solution.py:23
  16.0 0.0 collective-permute-done.2.refs_0_
  16.1 5.3 %collective-permute-start.4 = (bf16[432,128]{1,0:T(8,128)(2,1)S(1)}, bf16[432,128]{1,0:T(8,128)(2,1)S(1)}, u32[]{:S(2)}, u32[]{:S(2)}) collective-permute-start(bf16[432,128]{1,0:T(8,128)(2,1)S(1)} %select_convert_fusion), channel_id=1, source_target_pairs={{0,4},{1,5},{2,6},{3,7},{4,0},{5,1},{6,2},{7,3},{8,12},{9,13},{10,... | collective-permute-start | bytes 331784 | tf_op jit(solution)/shard_map/ppermute | solution.py:371
  21.3 0.0 collective-permute-done.3.refs_2_
  21.3 1.9 %backward.1 = (f32[224,128]{1,0:T(8,128)S(1)}, bf16[224,128]{1,0:T(8,128)(2,1)S(1)}, bf16[64,9216]{1,0:T(8,128)(2,1)S(1)}) custom-call(bf16[1376,128]{1,0:T(8,128)(2,1)S(1)} %collective-permute-done.2.refs_0_, bf16[128,512]{1,0:T(8,128)(2,1)S(1)} %get-tuple-element.43.refs_0_.refs_1_, bf16[128,512]{1,0:T(8,128)(2,1)S(1)} %collective-permute-done.3.refs_2_, ...), custom_call_target="tpu_custom_call" | custom-call | flops 900000000 | bytes 5000000 | tf_op jit(solution)/shard_map/backward/pallas_call | solution.py:23
  23.3 2.4 %collective-permute-done.4 = bf16[432,128]{1,0:T(8,128)(2,1)S(1)} collective-permute-done((bf16[432,128]{1,0:T(8,128)(2,1)S(1)}, bf16[432,128]{1,0:T(8,128)(2,1)S(1)}, u32[]{:S(2)}, u32[]{:S(2)}) %collective-permute-start.4) | collective-permute-done | bytes 110624 | tf_op jit(solution)/shard_map/ppermute | solution.py:371
  25.7 0.1 collective-permute-start.6
  25.8 2.6 %collective-permute-start.5 = (bf16[432,128]{1,0:T(8,128)(2,1)S(1)}, bf16[432,128]{1,0:T(8,128)(2,1)S(1)}, u32[]{:S(2)}, u32[]{:S(2)}) collective-permute-start(bf16[432,128]{1,0:T(8,128)(2,1)S(1)} %add_convert_fusion.2), channel_id=1, source_target_pairs={{0,8},{1,9},{2,10},{3,11},{4,12},{5,13},{6,14},{7,15},{8,0},{9,1},... | collective-permute-start | bytes 331784 | tf_op jit(solution)/shard_map/ppermute | solution.py:371
  28.4 0.0 collective-permute-done.6
  28.4 1.7 %collective-permute-start.7 = (bf16[224,128]{1,0:T(8,128)(2,1)S(1)}, bf16[224,128]{1,0:T(8,128)(2,1)S(1)}, u32[]{:S(2)}, u32[]{:S(2)}) collective-permute-start(bf16[224,128]{1,0:T(8,128)(2,1)S(1)} %add_convert_fusion.5), channel_id=1, source_target_pairs={{0,2},{1,3},{2,0},{3,1},{4,6},{5,7},{6,4},{7,5},{8,10},{9,11},{10,... | collective-permute-start | bytes 172040 | tf_op jit(solution)/shard_map/ppermute | solution.py:371
  30.1 4.4 %collective-permute-done.5 = bf16[432,128]{1,0:T(8,128)(2,1)S(1)} collective-permute-done((bf16[432,128]{1,0:T(8,128)(2,1)S(1)}, bf16[432,128]{1,0:T(8,128)(2,1)S(1)}, u32[]{:S(2)}, u32[]{:S(2)}) %collective-permute-start.5) | collective-permute-done | bytes 110624 | tf_op jit(solution)/shard_map/ppermute | solution.py:371
  34.5 0.0 collective-permute-done.7
  34.6 0.4 collective-permute-start.9
  35.0 1.3 %collective-permute-start.8 = (bf16[432,128]{1,0:T(8,128)(2,1)S(1)}, bf16[432,128]{1,0:T(8,128)(2,1)S(1)}, u32[]{:S(2)}, u32[]{:S(2)}) collective-permute-start(bf16[432,128]{1,0:T(8,128)(2,1)S(1)} %add_convert_fusion.1), channel_id=1, source_target_pairs={{0,2},{1,3},{2,0},{3,1},{4,6},{5,7},{6,4},{7,5},{8,10},{9,11},{10,... | collective-permute-start | bytes 331784 | tf_op jit(solution)/shard_map/ppermute | solution.py:371
  36.2 1.7 %input_grad.1 = bf16[32,4096]{1,0:T(8,128)(2,1)S(1)} custom-call(bf16[64,9216]{1,0:T(8,128)(2,1)S(1)} %get-tuple-element.63.refs_0_, bf16[96,576]{1,0:T(8,128)(2,1)S(1)} %reshape.35.refs_1_), custom_call_target="tpu_custom_call" | custom-call | flops 452000000 | bytes 2000000 | tf_op jit(solution)/shard_map/input_grad/pallas_call | solution.py:23
  37.9 2.5 %collective-permute-done.9 = bf16[224,128]{1,0:T(8,128)(2,1)S(1)} collective-permute-done((bf16[224,128]{1,0:T(8,128)(2,1)S(1)}, bf16[224,128]{1,0:T(8,128)(2,1)S(1)}, u32[]{:S(2)}, u32[]{:S(2)}) %collective-permute-start.9) | collective-permute-done | bytes 57376 | tf_op jit(solution)/shard_map/ppermute | solution.py:371
  40.5 0.0 collective-permute-done.8
  40.6 2.8 %collective-permute-start.10 = (bf16[656,128]{1,0:T(8,128)(2,1)S(1)}, bf16[656,128]{1,0:T(8,128)(2,1)S(1)}, u32[]{:S(2)}, u32[]{:S(2)}) collective-permute-start(bf16[656,128]{1,0:T(8,128)(2,1)S(1)} %pad_maximum_fusion.1), channel_id=1, source_target_pairs={{0,4},{1,5},{2,6},{3,7},{4,0},{5,1},{6,2},{7,3},{8,12},{9,13},{10,... | collective-permute-start | bytes 503816 | tf_op jit(solution)/shard_map/ppermute | solution.py:371
  43.4 3.3 %collective-permute-done.10 = bf16[656,128]{1,0:T(8,128)(2,1)S(1)} collective-permute-done((bf16[656,128]{1,0:T(8,128)(2,1)S(1)}, bf16[656,128]{1,0:T(8,128)(2,1)S(1)}, u32[]{:S(2)}, u32[]{:S(2)}) %collective-permute-start.10) | collective-permute-done | bytes 167968 | tf_op jit(solution)/shard_map/ppermute | solution.py:371
  46.8 0.1 collective-permute-start.11
  46.9 0.9 %reshape.39 = bf16[32,4,4,256]{3,2,1,0:T(4,128)(2,1)} reshape(bf16[32,4096]{1,0:T(8,128)(2,1)S(1)} %input_grad.1) | data formatting | bytes 524288 | tf_op jit(solution)/shard_map/reshape | solution.py:537
  47.8 0.7 %collective-permute-done.11.refs_1_ = bf16[1312,128]{1,0:T(8,128)(2,1)S(1)} collective-permute-done((bf16[1312,128]{1,0:T(8,128)(2,1)S(1)}, bf16[1312,128]{1,0:T(8,128)(2,1)S(1)}, u32[]{:S(2)}, u32[]{:S(2)}) %collective-permute-start.11) | collective-permute-done | bytes 335904 | tf_op jit(solution)/shard_map/ppermute | solution.py:371
  48.6 1.2 %finish.1 = (f32[1728,128]{1,0:T(8,128)}, f32[864,64]{1,0:T(8,128)}) custom-call(bf16[1312,128]{1,0:T(8,128)(2,1)S(1)} %pad_maximum_fusion.refs_0_, bf16[1312,128]{1,0:T(8,128)(2,1)S(1)} %collective-permute-done.11.refs_1_), custom_call_target="tpu_custom_call" | custom-call | bytes 2000000 | tf_op jit(solution)/shard_map/finish/pallas_call | solution.py:23
  (15 shorter events, 0.4 us)
Async XLA Ops:
  0.6 3.5 %copy-start.1 = (bf16[64,27,32]{0,2,1:T(8,128)(2,1)S(1)}, bf16[64,27,32]{0,2,1:T(8,128)(2,1)}, u32[]{:S(2)}) copy-start(bf16[64,27,32]{0,2,1:T(8,128)(2,1)} %param.5) | copy-start | bytes 331780
  1.8 3.1 %copy-start.2 = (bf16[128,2,2,128]{3,2,1,0:T(2,128)(2,1)S(1)}, bf16[128,2,2,128]{3,2,1,0:T(2,128)(2,1)}, u32[]{:S(2)}) copy-start(bf16[128,2,2,128]{3,2,1,0:T(2,128)(2,1)} %param.7) | copy-start | bytes 393220
  1.9 3.1 %collective-permute-start.1 = (bf16[32,3072]{1,0:T(8,128)(2,1)S(1)}, bf16[32,3072]{1,0:T(8,128)(2,1)S(1)}, u32[]{:S(2)}, u32[]{:S(2)}) collective-permute-start(bf16[32,3072]{1,0:T(8,128)(2,1)S(1)} %get-tuple-element.71), channel_id=1, source_target_pairs={{0,1},{1,0},{2,3},{3,2},{4,5},{5,4},{6,7},{7,6},{8,9},{9,8},{10,11... | collective-permute-start | bytes 589832 | tf_op jit(solution)/shard_map/ppermute | solution.py:371
  2.4 4.1 %collective-permute-start = (bf16[32,3072]{1,0:T(8,128)(2,1)S(1)}, bf16[32,3072]{1,0:T(8,128)(2,1)S(1)}, u32[]{:S(2)}, u32[]{:S(2)}) collective-permute-start(bf16[32,3072]{1,0:T(8,128)(2,1)S(1)} %get-tuple-element.72), channel_id=1, source_target_pairs={{1,2},{3,4},{5,6},{7,8},{9,10},{11,12},{13,14},{2,1},{4,3},{6,5},{... | collective-permute-start | bytes 589832 | tf_op jit(solution)/shard_map/ppermute | solution.py:377
  5.0 1.5 %copy-start = (bf16[128,27,64]{0,2,1:T(8,128)(2,1)S(1)}, bf16[128,27,64]{0,2,1:T(8,128)(2,1)}, u32[]{:S(2)}) copy-start(bf16[128,27,64]{0,2,1:T(8,128)(2,1)} %param.6) | copy-start | bytes 1327108
  9.3 6.7 %collective-permute-start.2 = (bf16[1376,128]{1,0:T(8,128)(2,1)S(1)}, bf16[1376,128]{1,0:T(8,128)(2,1)S(1)}, u32[]{:S(2)}, u32[]{:S(2)}) collective-permute-start(bf16[1376,128]{1,0:T(8,128)(2,1)S(1)} %get-tuple-element.45), channel_id=1, source_target_pairs={{0,1},{1,0},{2,3},{3,2},{4,5},{5,4},{6,7},{7,6},{8,9},{9,8},{10,11... | collective-permute-start | bytes 1056776 | tf_op jit(solution)/shard_map/ppermute | solution.py:371
  14.5 6.8 %collective-permute-start.3 = (bf16[128,512]{1,0:T(8,128)(2,1)S(1)}, bf16[128,512]{1,0:T(8,128)(2,1)S(1)}, u32[]{:S(2)}, u32[]{:S(2)}) collective-permute-start(bf16[128,512]{1,0:T(8,128)(2,1)S(1)} %get-tuple-element.43.refs_0_.refs_1_), channel_id=1, source_target_pairs={{1,2},{3,4},{5,6},{7,8},{9,10},{11,12},{13,14},{2,1},{4,3},{6,5},{... | collective-permute-start | bytes 393224 | tf_op jit(solution)/shard_map/ppermute | solution.py:377
  16.1 9.6 %collective-permute-start.4 = (bf16[432,128]{1,0:T(8,128)(2,1)S(1)}, bf16[432,128]{1,0:T(8,128)(2,1)S(1)}, u32[]{:S(2)}, u32[]{:S(2)}) collective-permute-start(bf16[432,128]{1,0:T(8,128)(2,1)S(1)} %select_convert_fusion), channel_id=1, source_target_pairs={{0,4},{1,5},{2,6},{3,7},{4,0},{5,1},{6,2},{7,3},{8,12},{9,13},{10,... | collective-permute-start | bytes 331784 | tf_op jit(solution)/shard_map/ppermute | solution.py:371
  25.7 2.7 %collective-permute-start.6 = (bf16[224,128]{1,0:T(8,128)(2,1)S(1)}, bf16[224,128]{1,0:T(8,128)(2,1)S(1)}, u32[]{:S(2)}, u32[]{:S(2)}) collective-permute-start(bf16[224,128]{1,0:T(8,128)(2,1)S(1)} %get-tuple-element.58), channel_id=1, source_target_pairs={{0,1},{1,0},{2,3},{3,2},{4,5},{5,4},{6,7},{7,6},{8,9},{9,8},{10,11... | collective-permute-start | bytes 172040 | tf_op jit(solution)/shard_map/ppermute | solution.py:371
  25.8 8.7 %collective-permute-start.5 = (bf16[432,128]{1,0:T(8,128)(2,1)S(1)}, bf16[432,128]{1,0:T(8,128)(2,1)S(1)}, u32[]{:S(2)}, u32[]{:S(2)}) collective-permute-start(bf16[432,128]{1,0:T(8,128)(2,1)S(1)} %add_convert_fusion.2), channel_id=1, source_target_pairs={{0,8},{1,9},{2,10},{3,11},{4,12},{5,13},{6,14},{7,15},{8,0},{9,1},... | collective-permute-start | bytes 331784 | tf_op jit(solution)/shard_map/ppermute | solution.py:371
  28.4 6.1 %collective-permute-start.7 = (bf16[224,128]{1,0:T(8,128)(2,1)S(1)}, bf16[224,128]{1,0:T(8,128)(2,1)S(1)}, u32[]{:S(2)}, u32[]{:S(2)}) collective-permute-start(bf16[224,128]{1,0:T(8,128)(2,1)S(1)} %add_convert_fusion.5), channel_id=1, source_target_pairs={{0,2},{1,3},{2,0},{3,1},{4,6},{5,7},{6,4},{7,5},{8,10},{9,11},{10,... | collective-permute-start | bytes 172040 | tf_op jit(solution)/shard_map/ppermute | solution.py:371
  34.6 5.9 %collective-permute-start.9 = (bf16[224,128]{1,0:T(8,128)(2,1)S(1)}, bf16[224,128]{1,0:T(8,128)(2,1)S(1)}, u32[]{:S(2)}, u32[]{:S(2)}) collective-permute-start(bf16[224,128]{1,0:T(8,128)(2,1)S(1)} %add_convert_fusion.4), channel_id=1, source_target_pairs={{0,8},{1,9},{2,10},{3,11},{4,12},{5,13},{6,14},{7,15},{8,0},{9,1},... | collective-permute-start | bytes 172040 | tf_op jit(solution)/shard_map/ppermute | solution.py:371
  35.0 5.5 %collective-permute-start.8 = (bf16[432,128]{1,0:T(8,128)(2,1)S(1)}, bf16[432,128]{1,0:T(8,128)(2,1)S(1)}, u32[]{:S(2)}, u32[]{:S(2)}) collective-permute-start(bf16[432,128]{1,0:T(8,128)(2,1)S(1)} %add_convert_fusion.1), channel_id=1, source_target_pairs={{0,2},{1,3},{2,0},{3,1},{4,6},{5,7},{6,4},{7,5},{8,10},{9,11},{10,... | collective-permute-start | bytes 331784 | tf_op jit(solution)/shard_map/ppermute | solution.py:371
  40.6 6.2 %collective-permute-start.10 = (bf16[656,128]{1,0:T(8,128)(2,1)S(1)}, bf16[656,128]{1,0:T(8,128)(2,1)S(1)}, u32[]{:S(2)}, u32[]{:S(2)}) collective-permute-start(bf16[656,128]{1,0:T(8,128)(2,1)S(1)} %pad_maximum_fusion.1), channel_id=1, source_target_pairs={{0,4},{1,5},{2,6},{3,7},{4,0},{5,1},{6,2},{7,3},{8,12},{9,13},{10,... | collective-permute-start | bytes 503816 | tf_op jit(solution)/shard_map/ppermute | solution.py:371
  46.8 1.7 %collective-permute-start.11 = (bf16[1312,128]{1,0:T(8,128)(2,1)S(1)}, bf16[1312,128]{1,0:T(8,128)(2,1)S(1)}, u32[]{:S(2)}, u32[]{:S(2)}) collective-permute-start(bf16[1312,128]{1,0:T(8,128)(2,1)S(1)} %pad_maximum_fusion.refs_0_), channel_id=1, source_target_pairs={{0,1},{1,0},{2,3},{3,2},{4,5},{5,4},{6,7},{7,6},{8,9},{9,8},{10,11... | collective-permute-start | bytes 1007624 | tf_op jit(solution)/shard_map/ppermute | solution.py:371

commit v4 on v3

--- a/solution.py
+++ b/solution.py
@@ -215,28 +215,20 @@
     halve(out_ref, keep_ref, send_ref)
 
 
-def backward_kernel(
-    near_ref, own_ref, far_ref, slope_ref, vol_ref, wtop_ref, keep_ref, send_ref, field_ref, top_ref, shift_ref, mid_ref, *, h, w, spatial
-):
+def backward_side(side, neighbour, own_ref, slope_ref, vol_ref, wtop_ref, field_ref, field_base, top_ref, shift_ref, h, w, spatial):
     half, hp = w // 2, h // 2
     here = lax.axis_index("spatial")
     trow = (hp + 2) * half
-    top_zero = jnp.zeros((top_ref.shape[0], half), BF16)
     depth = own_ref.shape[1] // (hp * half)
-    for z in range(3 * depth):
-        start = (z % depth) * hp * half
-        at = slice(start, start + hp * half)
-        if z // depth == 1:
-            plane = own_ref[:, at]
-        else:
-            cout = own_ref.shape[0]
-            blocks = range((z % depth) * hp, (z % depth + 1) * hp)
-            near = jnp.concatenate([near_ref[k * cout : (k + 1) * cout, :] for k in blocks], axis=1)
-            plane = jnp.where((here % 2 == 0) == (z < depth), far_ref[:, at], near)
-        base = z * trow
-        top_ref[:, base : base + half] = top_zero
-        top_ref[:, base + half : base + (hp + 1) * half] = plane
-        top_ref[:, base + (hp + 1) * half : base + trow] = top_zero
+    zero = jnp.zeros((top_ref.shape[0], half), BF16)
+    for z in range(depth):
+        near_plane = neighbour(z)
+        own_plane = own_ref[:, z * hp * half : (z + 1) * hp * half]
+        for plane, base in ((own_plane, (1 - side) * depth * trow), (near_plane, side * depth * trow)):
+            base = base + z * trow
+            top_ref[:, lanes(base, half)] = zero
+            top_ref[:, lanes(base + half, hp * half)] = plane
+            top_ref[:, lanes(base + (hp + 1) * half, half)] = zero
     mid = slope_ref.shape[0]
     weights = jnp.concatenate(
         [
@@ -245,14 +237,13 @@
         ],
         axis=0,
     )
-    outer = depth + 2
-    first = depth - 1
+    count = 2 * depth - 2
     cols = jnp.concatenate(
         [
             jnp.concatenate(
                 [
-                    top_ref[:, (first + j + 1 - a) * trow + (2 - b) * half : (first + j + 1 - a) * trow + (2 - b + hp) * half]
-                    for j in range(outer)
+                    top_ref[:, (j + 2 - a) * trow + (2 - b) * half : (j + 2 - a) * trow + (2 - b + hp) * half]
+                    for j in range(count)
                 ],
                 axis=1,
             )
@@ -262,47 +253,77 @@
         axis=0,
     )
     part = dot(weights, cols)
-    vrows = h + 2
+    pools = []
+    for k in range(count * hp):
+        at = slice(k * half, (k + 1) * half)
+        pools.append(part[mid : 2 * mid, at] + later(part[2 * mid :, at]) + earlier(part[:mid, at]))
+    size = (h + 2) * w
     field_zero = jnp.zeros((mid, w), BF16)
-    fine = 2 * depth
-    for m in range(fine + 2):
-        j = (m + 1) // 2
-        base = m * vrows * w
-        field_ref[:, base : base + w] = field_zero
-        field_ref[:, base + (h + 1) * w : base + vrows * w] = field_zero
+    planes = 2 * count - 1
+    for k in range(planes):
+        base = field_base + k * size
+        field_ref[:, lanes(base, w)] = field_zero
+        field_ref[:, lanes(base + (h + 1) * w, w)] = field_zero
         for y in range(h):
-            at = slice((j * hp + y // 2) * half, (j * hp + y // 2 + 1) * half)
-            pool = part[mid : 2 * mid, at] + later(part[2 * mid :, at]) + earlier(part[:mid, at])
-            if m == 0:
-                pool = jnp.where(here == 0, 0.0, pool)
-            if m == fine + 1:
-                pool = jnp.where(here == spatial - 1, 0.0, pool)
-            out = (m * h + y) * w
-            even = (slope_ref[:, out : out + half] * pool).astype(BF16)
-            odd = (slope_ref[:, out + half : out + w] * pool).astype(BF16)
+            pool = jnp.where(side == 1, pools[k // 2 * hp + y // 2], pools[(k + 1) // 2 * hp + y // 2])
+            if k == 0:
+                pool = jnp.where((side == 0) & (here == 0), 0.0, pool)
+            if k == planes - 1:
+                pool = jnp.where((side == 1) & (here == spatial - 1), 0.0, pool)
+            row = (k * h + y) * w
+            at = side * planes * h * w + row
+            even = (slope_ref[:, lanes(at, half)] * pool).astype(BF16)
+            odd = (slope_ref[:, lanes(at + half, half)] * pool).astype(BF16)
             to = base + (y + 1) * w
-            field_ref[:, to : to + half] = even
-            field_ref[:, to + half : to + w] = odd
-            if 0 < m <= fine:
-                to = ((m - 1) * h + y) * w
-                shift_ref[:mid, to : to + half] = odd
-                shift_ref[:mid, to + half : to + w] = earlier(even.astype(F32)).astype(BF16)
-                shift_ref[mid : 2 * mid, to : to + half] = even
-                shift_ref[mid : 2 * mid, to + half : to + w] = odd
-                shift_ref[2 * mid :, to : to + half] = later(odd.astype(F32)).astype(BF16)
-                shift_ref[2 * mid :, to + half : to + w] = even
+            field_ref[:, lanes(to, half)] = even
+            field_ref[:, lanes(to + half, half)] = odd
+            shift_ref[:mid, row : row + half] = odd
+            shift_ref[:mid, row + half : row + w] = earlier(even.astype(F32)).astype(BF16)
+            shift_ref[mid : 2 * mid, row : row + half] = even
+            shift_ref[mid : 2 * mid, row + half : row + w] = odd
+            shift_ref[2 * mid :, row : row + half] = later(odd.astype(F32)).astype(BF16)
+            shift_ref[2 * mid :, row + half : row + w] = even
     total = None
-    for z in range(fine):
-        piece = jnp.concatenate(
-            [
-                vol_ref[:, ((z + 2 + a) * vrows + b) * w : ((z + 2 + a) * vrows + b + h) * w]
-                for a in THREE
-                for b in THREE
-            ],
-            axis=0,
-        )
-        product = dot(piece, shift_ref[:, z * h * w : (z + 1) * h * w], ((1,), (1,)))
+    for z in range(depth):
+        at = (side * depth + z + 2) * size
+        piece = jnp.concatenate([vol_ref[:, lanes(at + a * size + b * w, h * w)] for a in THREE for b in THREE], axis=0)
+        moved = shift_ref[:, lanes((1 - side + z) * h * w, h * w)]
+        product = dot(piece, moved, ((1,), (1,)))
         total = product if total is None else total + product
+    return total
+
+
+def backward_near_kernel(
+    near_ref, own_ref, slope_ref, vol_ref, wtop_ref, part_ref, field_ref, top_ref, shift_ref, *, h, w, spatial
+):
+    core = lax.axis_index("spatial") % 2
+    hp = h // 2
+    cout = own_ref.shape[0]
+
+    def neighbour(z):
+        return jnp.concatenate([near_ref[k * cout : (k + 1) * cout, :] for k in range(z * hp, (z + 1) * hp)], axis=1)
+
+    part_ref[...] = backward_side(
+        1 - core, neighbour, own_ref, slope_ref, vol_ref, wtop_ref, field_ref, 0, top_ref, shift_ref, h, w, spatial
+    )
+
+
+def backward_far_kernel(
+    far_ref, own_ref, slope_ref, vol_ref, wtop_ref, part_ref, field_near_ref, keep_ref, send_ref, field_ref, top_ref, shift_ref,
+    mid_ref, *, h, w, spatial
+):
+    core = lax.axis_index("spatial") % 2
+    size = h // 2 * (w // 2)
+    known = field_near_ref.shape[1]
+    field_ref[:, lanes((1 - core) * known, known)] = field_near_ref[...]
+
+    def neighbour(z):
+        return far_ref[:, z * size : (z + 1) * size]
+
+    total = part_ref[...] + backward_side(
+        core, neighbour, own_ref, slope_ref, vol_ref, wtop_ref, field_ref, core * known, top_ref, shift_ref, h, w, spatial
+    )
+    mid = field_ref.shape[0]
     rows = total.shape[0]
     half_rows = rows // 2
     mid_ref[:rows, :] = total[:, : 2 * mid]
@@ -475,22 +496,32 @@
     mine, other = halves(keep + delta_near[delta_rows:].astype(F32), low)
     top_received = partner(other, 4)
     mid_rows = -(-27 * cin // 64) * 16
+    side_scratch = (
+        pltpu.VMEM((cout, 2 * nzp * (hp + 2) * wp), BF16),
+        pltpu.VMEM((3 * mid, (nz // 2 + 1) * plane), BF16),
+    )
+    part, field_near = kernel_call(
+        lambda *refs: backward_near_kernel(*refs, h=h, w=w, spatial=spatial),
+        "backward_near",
+        (shape((9 * cin, 3 * mid), F32), shape((mid, (nz // 2 + 1) * size), BF16)),
+        (delta_near, delta, slope, vol, wtop),
+        scratch=side_scratch,
+        flops=500_000_000,
+        moved=3_000_000,
+    )
+    delta_far, part, field_near = lax.optimization_barrier((delta_far, part, field_near))
     keep, send, field = kernel_call(
-        lambda *refs: backward_kernel(*refs, h=h, w=w, spatial=spatial),
-        "backward",
+        lambda *refs: backward_far_kernel(*refs, h=h, w=w, spatial=spatial),
+        "backward_far",
         (
             shape((mid_rows, 2 * mid), F32),
             shape((mid_rows, 2 * mid), BF16),
-            shape((mid, (nz + 2) * (h + 2) * w), BF16),
+            shape((mid, (nz + 2) * size), BF16),
         ),
-        (delta_near, delta, delta_far, slope, vol, wtop),
-        scratch=(
-            pltpu.VMEM((cout, 3 * nzp * (hp + 2) * wp), BF16),
-            pltpu.VMEM((3 * mid, nz * plane), BF16),
-            pltpu.VMEM((2 * mid_rows, 2 * mid), F32),
-        ),
-        flops=900_000_000,
-        moved=5_000_000,
+        (delta_far, delta, slope, vol, wtop, part, field_near),
+        scratch=side_scratch + (pltpu.VMEM((2 * mid_rows, 2 * mid), F32),),
+        flops=500_000_000,
+        moved=4_000_000,
     )
     keep, send, mine, top_received = lax.optimization_barrier((keep, send, mine, top_received))
     top_sum = rounded(mine + top_received.astype(F32))

time: 49.9 us -> 49.5 us (level)
  starting transfers between devices: 21.3 us -> 20.2 us
  Pallas kernels: 9.88 us -> 10.9 us
    ppermute x10, starting transfers between devices: 19.9 us -> 18.9 us  [partner(): return lax.ppermute(block, 'spatial', [(i, i ^ bit) for i in range(size)])]
    pallas_call x7 -> x8, Pallas kernels: 9.88 us -> 10.9 us  [kernel_call(): pl.pallas_call(body, name=name, out_shape=outs, in_specs=[whole] * len(ar...]
  transfers between devices with their start and end apart: 12 -> 12, of which waited for: 5 -> 5; matrix products, arithmetic and copies ran while one was open for 6% -> 6% of each run, Pallas kernels for 12% -> 14%
where the time goes in v4:
time: 49.5 us; the launch traced here: 49.4 us
  starting transfers between devices  20.2 us (41%)
  waiting for transfers between devices  13 us (26%)
  Pallas kernels  10.9 us (22%)
  local copies, waits for them, and re-layouts  3.93 us (8%)
  between operations  0.92 us (2%)
    ppermute x10, starting transfers between devices, partner(): return lax.ppermute(block, 'spatial', [(i, i ^ bit) for i in range(size)])  18.9 us
    ppermute x10, waiting for transfers between devices, partner(): return lax.ppermute(block, 'spatial', [(i, i ^ bit) for i in range(size)])  13 us
    pallas_call x8, Pallas kernels, kernel_call(): pl.pallas_call(body, name=name, out_shape=outs, in_specs=[whole] * len(ar...  10.9 us
    ppermute x2, starting transfers between devices, across(): return lax.ppermute(block, 'spatial', pairs + [(j, i) for i, j in pairs])  1.32 us
    reshape x2, local copies, waits for them, and re-layouts, shards(): split = weights_mid.reshape(mid, 9, 3, cin)  1.21 us
    reshape x1, local copies, waits for them, and re-layouts, shards(): flat = volume.reshape(cin, nz * plane)  1.17 us
  transfers between devices with their start and end apart: 12, of which 5 were waited for; matrix products, arithmetic and copies ran while one was open for 6% of the time, Pallas kernels for 14%

profile of v4, /device:TPU:0, one launch (start us, length us, event | category | flops | bytes accessed | tf_op | source)
XLA Modules:
  0.0 49.4 jit_solution(6158526271247345271)
XLA Ops:
  0.6 0.0 copy-start.1
  0.7 1.2 %reshape.33.refs_1_ = bf16[32,4096]{1,0:T(8,128)(2,1)S(1)} reshape(bf16[32,4,4,256]{3,2,1,0:T(4,128)(2,1)} %param.4) | data formatting | bytes 524288 | tf_op jit(solution)/shard_map/reshape | solution.py:436
  1.8 0.0 copy-start.2
  1.9 0.5 %collective-permute-start.1 = (bf16[32,3072]{1,0:T(8,128)(2,1)S(1)}, bf16[32,3072]{1,0:T(8,128)(2,1)S(1)}, u32[]{:S(2)}, u32[]{:S(2)}) collective-permute-start(bf16[32,3072]{1,0:T(8,128)(2,1)S(1)} %get-tuple-element.81), channel_id=1, source_target_pairs={{0,1},{1,0},{2,3},{3,2},{4,5},{5,4},{6,7},{7,6},{8,9},{9,8},{10,11... | collective-permute-start | bytes 589832 | tf_op jit(solution)/shard_map/ppermute | solution.py:392
  2.4 0.7 %collective-permute-start = (bf16[32,3072]{1,0:T(8,128)(2,1)S(1)}, bf16[32,3072]{1,0:T(8,128)(2,1)S(1)}, u32[]{:S(2)}, u32[]{:S(2)}) collective-permute-start(bf16[32,3072]{1,0:T(8,128)(2,1)S(1)} %get-tuple-element.82), channel_id=1, source_target_pairs={{1,2},{3,4},{5,6},{7,8},{9,10},{11,12},{13,14},{2,1},{4,3},{6,5},{... | collective-permute-start | bytes 589832 | tf_op jit(solution)/shard_map/ppermute | solution.py:398
  3.1 1.1 %copy.16 = bf16[64,9,3,32]{0,2,3,1:T(4,128)(2,1)S(1)} copy(bf16[64,9,3,32]{0,3,2,1:T(8,128)(2,1)} %bitcast.23) | data formatting | bytes 221184 | tf_op jit(solution)/shard_map/reshape | solution.py:440
  4.2 0.0 copy-done.1
  4.2 0.1 copy.15
  4.3 0.2 reshape.36
  4.5 0.1 copy.11.refs_2_.refs_3_
  4.6 0.2 reshape.35.refs_1_
  4.9 0.0 copy-done.2
  4.9 0.1 reshape.38.refs_5_
  5.0 0.0 copy-start
  5.0 0.0 collective-permute-done.1.refs_0_
  5.0 1.5 %near_side.1 = (bf16[32,10752]{1,0:T(8,128)(2,1)S(1)}, f32[64,4096]{1,0:T(8,128)S(1)}, bf16[192,1024]{1,0:T(8,128)(2,1)S(1)}) custom-call(bf16[32,3072]{1,0:T(8,128)(2,1)S(1)} %collective-permute-done.1.refs_0_, bf16[32,4096]{1,0:T(8,128)(2,1)S(1)} %reshape.33.refs_1_, bf16[192,288]{1,0:T(8,128)(2,1)S(1)} %copy.11.refs_2_.refs_3_), custom_call_target="tpu_custom_call" | custom-call | flops 900000000 | bytes 3000000 | tf_op jit(solution)/shard_map/near_side/pallas_call | solution.py:23
  6.5 0.0 collective-permute-done.refs_0_
  6.5 0.0 copy-done
  6.5 2.1 %far_side.1 = (bf16[128,512]{1,0:T(8,128)(2,1)S(1)}, f32[64,4096]{1,0:T(8,128)S(1)}, bf16[32,15360]{1,0:T(8,128)(2,1)S(1)}, bf16[192,2048]{1,0:T(8,128)(2,1)S(1)}) custom-call(bf16[32,3072]{1,0:T(8,128)(2,1)S(1)} %collective-permute-done.refs_0_, bf16[32,10752]{1,0:T(8,128)(2,1)S(1)} %get-tuple-element.46.refs_1_, ...), custom_call_target="tpu_custom_call" | custom-call | flops 900000000 | bytes 4000000 | tf_op jit(solution)/shard_map/far_side/pallas_call | solution.py:23
  8.6 0.7 %top_part.1 = (f32[864,128]{1,0:T(8,128)S(1)}, bf16[1376,128]{1,0:T(8,128)(2,1)S(1)}) custom-call(bf16[128,512]{1,0:T(8,128)(2,1)S(1)} %get-tuple-element.48.refs_0_.refs_1_, bf16[192,2048]{1,0:T(8,128)(2,1)S(1)} %get-tuple-element.49.refs_1_), custom_call_target="tpu_custom_call" | custom-call | flops 226000000 | bytes 1500000 | tf_op jit(solution)/shard_map/top_part/pallas_call | solution.py:23
  9.3 5.2 %collective-permute-start.3 = (bf16[1376,128]{1,0:T(8,128)(2,1)S(1)}, bf16[1376,128]{1,0:T(8,128)(2,1)S(1)}, u32[]{:S(2)}, u32[]{:S(2)}) collective-permute-start(bf16[1376,128]{1,0:T(8,128)(2,1)S(1)} %get-tuple-element.50), channel_id=1, source_target_pairs={{0,1},{1,0},{2,3},{3,2},{4,5},{5,4},{6,7},{7,6},{8,9},{9,8},{10,11... | collective-permute-start | bytes 1056776 | tf_op jit(solution)/shard_map/ppermute | solution.py:392
  14.5 0.7 %collective-permute-start.2 = (bf16[128,512]{1,0:T(8,128)(2,1)S(1)}, bf16[128,512]{1,0:T(8,128)(2,1)S(1)}, u32[]{:S(2)}, u32[]{:S(2)}) collective-permute-start(bf16[128,512]{1,0:T(8,128)(2,1)S(1)} %get-tuple-element.48.refs_0_.refs_1_), channel_id=1, source_target_pairs={{1,2},{3,4},{5,6},{7,8},{9,10},{11,12},{13,14},{2,1},{4,3},{6,5},{... | collective-permute-start | bytes 393224 | tf_op jit(solution)/shard_map/ppermute | solution.py:398
  15.2 0.8 %slope.1.refs_2_ = f32[64,6144]{1,0:T(8,128)S(1)} custom-call(f32[64,4096]{1,0:T(8,128)S(1)} %get-tuple-element.51.refs_0_, f32[64,4096]{1,0:T(8,128)S(1)} %get-tuple-element.52.refs_1_), custom_call_target="tpu_custom_call" | custom-call | flops 100000000 | bytes 3000000 | tf_op jit(solution)/shard_map/slope/pallas_call | solution.py:23
  16.0 0.0 collective-permute-done.3.refs_0_
  16.1 5.3 %collective-permute-start.4 = (bf16[432,128]{1,0:T(8,128)(2,1)S(1)}, bf16[432,128]{1,0:T(8,128)(2,1)S(1)}, u32[]{:S(2)}, u32[]{:S(2)}) collective-permute-start(bf16[432,128]{1,0:T(8,128)(2,1)S(1)} %select_convert_fusion), channel_id=1, source_target_pairs={{0,4},{1,5},{2,6},{3,7},{4,0},{5,1},{6,2},{7,3},{8,12},{9,13},{10,... | collective-permute-start | bytes 331784 | tf_op jit(solution)/shard_map/ppermute | solution.py:392
  21.3 1.4 %backward_near.1 = (f32[288,192]{1,0:T(8,128)S(1)}, bf16[64,4608]{1,0:T(8,128)(2,1)S(1)}) custom-call(bf16[1376,128]{1,0:T(8,128)(2,1)S(1)} %collective-permute-done.3.refs_0_, bf16[128,512]{1,0:T(8,128)(2,1)S(1)} %get-tuple-element.48.refs_0_.refs_1_, f32[64,6144]{1,0:T(8,128)S(1)} %slope.1.refs_2_, bf16[32,15360]{1,0:T(8,128)(2,1)S(1)} %get-tuple-element.53.refs_3_, ...), custom_call_target="tpu_custom_call" | custom-call | flops 500000000 | bytes 3000000 | tf_op jit(solution)/shard_map/backward_near/pallas_call | solution.py:23
  22.8 0.0 collective-permute-done.2.refs_0_
  22.8 1.5 %backward_far.1 = (f32[224,128]{1,0:T(8,128)S(1)}, bf16[224,128]{1,0:T(8,128)(2,1)S(1)}, bf16[64,9216]{1,0:T(8,128)(2,1)S(1)}) custom-call(bf16[128,512]{1,0:T(8,128)(2,1)S(1)} %collective-permute-done.2.refs_0_, bf16[128,512]{1,0:T(8,128)(2,1)S(1)} %get-tuple-element.48.refs_0_.refs_1_, f32[64,6144]{1,0:T(8,128)S(1)} %slope.1.refs_2_, ...), custom_call_target="tpu_custom_call" | custom-call | flops 500000000 | bytes 4000000 | tf_op jit(solution)/shard_map/backward_far/pallas_call | solution.py:23
  24.3 1.3 %collective-permute-done.4 = bf16[432,128]{1,0:T(8,128)(2,1)S(1)} collective-permute-done((bf16[432,128]{1,0:T(8,128)(2,1)S(1)}, bf16[432,128]{1,0:T(8,128)(2,1)S(1)}, u32[]{:S(2)}, u32[]{:S(2)}) %collective-permute-start.4) | collective-permute-done | bytes 110624 | tf_op jit(solution)/shard_map/ppermute | solution.py:392
  25.7 0.1 collective-permute-start.6
  25.8 2.6 %collective-permute-start.5 = (bf16[432,128]{1,0:T(8,128)(2,1)S(1)}, bf16[432,128]{1,0:T(8,128)(2,1)S(1)}, u32[]{:S(2)}, u32[]{:S(2)}) collective-permute-start(bf16[432,128]{1,0:T(8,128)(2,1)S(1)} %add_convert_fusion.2), channel_id=1, source_target_pairs={{0,8},{1,9},{2,10},{3,11},{4,12},{5,13},{6,14},{7,15},{8,0},{9,1},... | collective-permute-start | bytes 331784 | tf_op jit(solution)/shard_map/ppermute | solution.py:392
  28.4 0.0 collective-permute-done.6
  28.4 1.3 %collective-permute-start.7 = (bf16[224,128]{1,0:T(8,128)(2,1)S(1)}, bf16[224,128]{1,0:T(8,128)(2,1)S(1)}, u32[]{:S(2)}, u32[]{:S(2)}) collective-permute-start(bf16[224,128]{1,0:T(8,128)(2,1)S(1)} %add_convert_fusion.5), channel_id=1, source_target_pairs={{0,2},{1,3},{2,0},{3,1},{4,6},{5,7},{6,4},{7,5},{8,10},{9,11},{10,... | collective-permute-start | bytes 172040 | tf_op jit(solution)/shard_map/ppermute | solution.py:392
  29.8 4.8 %collective-permute-done.5 = bf16[432,128]{1,0:T(8,128)(2,1)S(1)} collective-permute-done((bf16[432,128]{1,0:T(8,128)(2,1)S(1)}, bf16[432,128]{1,0:T(8,128)(2,1)S(1)}, u32[]{:S(2)}, u32[]{:S(2)}) %collective-permute-start.5) | collective-permute-done | bytes 110624 | tf_op jit(solution)/shard_map/ppermute | solution.py:392
  34.6 0.0 collective-permute-done.7
  34.6 0.4 collective-permute-start.9
  35.0 0.9 %collective-permute-start.8 = (bf16[432,128]{1,0:T(8,128)(2,1)S(1)}, bf16[432,128]{1,0:T(8,128)(2,1)S(1)}, u32[]{:S(2)}, u32[]{:S(2)}) collective-permute-start(bf16[432,128]{1,0:T(8,128)(2,1)S(1)} %add_convert_fusion.1), channel_id=1, source_target_pairs={{0,2},{1,3},{2,0},{3,1},{4,6},{5,7},{6,4},{7,5},{8,10},{9,11},{10,... | collective-permute-start | bytes 331784 | tf_op jit(solution)/shard_map/ppermute | solution.py:392
  35.9 1.7 %input_grad.1 = bf16[32,4096]{1,0:T(8,128)(2,1)S(1)} custom-call(bf16[64,9216]{1,0:T(8,128)(2,1)S(1)} %get-tuple-element.73.refs_0_, bf16[96,576]{1,0:T(8,128)(2,1)S(1)} %reshape.35.refs_1_), custom_call_target="tpu_custom_call" | custom-call | flops 452000000 | bytes 2000000 | tf_op jit(solution)/shard_map/input_grad/pallas_call | solution.py:23
  37.5 2.8 %collective-permute-done.9 = bf16[224,128]{1,0:T(8,128)(2,1)S(1)} collective-permute-done((bf16[224,128]{1,0:T(8,128)(2,1)S(1)}, bf16[224,128]{1,0:T(8,128)(2,1)S(1)}, u32[]{:S(2)}, u32[]{:S(2)}) %collective-permute-start.9) | collective-permute-done | bytes 57376 | tf_op jit(solution)/shard_map/ppermute | solution.py:392
  40.3 0.0 collective-permute-done.8
  40.4 2.6 %collective-permute-start.10 = (bf16[656,128]{1,0:T(8,128)(2,1)S(1)}, bf16[656,128]{1,0:T(8,128)(2,1)S(1)}, u32[]{:S(2)}, u32[]{:S(2)}) collective-permute-start(bf16[656,128]{1,0:T(8,128)(2,1)S(1)} %pad_maximum_fusion.1), channel_id=1, source_target_pairs={{0,4},{1,5},{2,6},{3,7},{4,0},{5,1},{6,2},{7,3},{8,12},{9,13},{10,... | collective-permute-start | bytes 503816 | tf_op jit(solution)/shard_map/ppermute | solution.py:392
  43.0 3.3 %collective-permute-done.10 = bf16[656,128]{1,0:T(8,128)(2,1)S(1)} collective-permute-done((bf16[656,128]{1,0:T(8,128)(2,1)S(1)}, bf16[656,128]{1,0:T(8,128)(2,1)S(1)}, u32[]{:S(2)}, u32[]{:S(2)}) %collective-permute-start.10) | collective-permute-done | bytes 167968 | tf_op jit(solution)/shard_map/ppermute | solution.py:392
  46.4 0.1 collective-permute-start.11
  46.5 0.9 %reshape.39 = bf16[32,4,4,256]{3,2,1,0:T(4,128)(2,1)} reshape(bf16[32,4096]{1,0:T(8,128)(2,1)S(1)} %input_grad.1) | data formatting | bytes 524288 | tf_op jit(solution)/shard_map/reshape | solution.py:568
  47.4 0.7 %collective-permute-done.11.refs_1_ = bf16[1312,128]{1,0:T(8,128)(2,1)S(1)} collective-permute-done((bf16[1312,128]{1,0:T(8,128)(2,1)S(1)}, bf16[1312,128]{1,0:T(8,128)(2,1)S(1)}, u32[]{:S(2)}, u32[]{:S(2)}) %collective-permute-start.11) | collective-permute-done | bytes 335904 | tf_op jit(solution)/shard_map/ppermute | solution.py:392
  48.2 1.2 %finish.1 = (f32[1728,128]{1,0:T(8,128)}, f32[864,64]{1,0:T(8,128)}) custom-call(bf16[1312,128]{1,0:T(8,128)(2,1)S(1)} %pad_maximum_fusion.refs_0_, bf16[1312,128]{1,0:T(8,128)(2,1)S(1)} %collective-permute-done.11.refs_1_), custom_call_target="tpu_custom_call" | custom-call | bytes 2000000 | tf_op jit(solution)/shard_map/finish/pallas_call | solution.py:23
  (15 shorter events, 0.4 us)
Async XLA Ops:
  0.6 3.5 %copy-start.1 = (bf16[64,27,32]{0,2,1:T(8,128)(2,1)S(1)}, bf16[64,27,32]{0,2,1:T(8,128)(2,1)}, u32[]{:S(2)}) copy-start(bf16[64,27,32]{0,2,1:T(8,128)(2,1)} %param.5) | copy-start | bytes 331780
  1.8 3.1 %copy-start.2 = (bf16[128,2,2,128]{3,2,1,0:T(2,128)(2,1)S(1)}, bf16[128,2,2,128]{3,2,1,0:T(2,128)(2,1)}, u32[]{:S(2)}) copy-start(bf16[128,2,2,128]{3,2,1,0:T(2,128)(2,1)} %param.7) | copy-start | bytes 393220
  1.9 3.1 %collective-permute-start.1 = (bf16[32,3072]{1,0:T(8,128)(2,1)S(1)}, bf16[32,3072]{1,0:T(8,128)(2,1)S(1)}, u32[]{:S(2)}, u32[]{:S(2)}) collective-permute-start(bf16[32,3072]{1,0:T(8,128)(2,1)S(1)} %get-tuple-element.81), channel_id=1, source_target_pairs={{0,1},{1,0},{2,3},{3,2},{4,5},{5,4},{6,7},{7,6},{8,9},{9,8},{10,11... | collective-permute-start | bytes 589832 | tf_op jit(solution)/shard_map/ppermute | solution.py:392
  2.4 4.1 %collective-permute-start = (bf16[32,3072]{1,0:T(8,128)(2,1)S(1)}, bf16[32,3072]{1,0:T(8,128)(2,1)S(1)}, u32[]{:S(2)}, u32[]{:S(2)}) collective-permute-start(bf16[32,3072]{1,0:T(8,128)(2,1)S(1)} %get-tuple-element.82), channel_id=1, source_target_pairs={{1,2},{3,4},{5,6},{7,8},{9,10},{11,12},{13,14},{2,1},{4,3},{6,5},{... | collective-permute-start | bytes 589832 | tf_op jit(solution)/shard_map/ppermute | solution.py:398
  5.0 1.5 %copy-start = (bf16[128,27,64]{0,2,1:T(8,128)(2,1)S(1)}, bf16[128,27,64]{0,2,1:T(8,128)(2,1)}, u32[]{:S(2)}) copy-start(bf16[128,27,64]{0,2,1:T(8,128)(2,1)} %param.6) | copy-start | bytes 1327108
  9.3 6.7 %collective-permute-start.3 = (bf16[1376,128]{1,0:T(8,128)(2,1)S(1)}, bf16[1376,128]{1,0:T(8,128)(2,1)S(1)}, u32[]{:S(2)}, u32[]{:S(2)}) collective-permute-start(bf16[1376,128]{1,0:T(8,128)(2,1)S(1)} %get-tuple-element.50), channel_id=1, source_target_pairs={{0,1},{1,0},{2,3},{3,2},{4,5},{5,4},{6,7},{7,6},{8,9},{9,8},{10,11... | collective-permute-start | bytes 1056776 | tf_op jit(solution)/shard_map/ppermute | solution.py:392
  14.5 8.2 %collective-permute-start.2 = (bf16[128,512]{1,0:T(8,128)(2,1)S(1)}, bf16[128,512]{1,0:T(8,128)(2,1)S(1)}, u32[]{:S(2)}, u32[]{:S(2)}) collective-permute-start(bf16[128,512]{1,0:T(8,128)(2,1)S(1)} %get-tuple-element.48.refs_0_.refs_1_), channel_id=1, source_target_pairs={{1,2},{3,4},{5,6},{7,8},{9,10},{11,12},{13,14},{2,1},{4,3},{6,5},{... | collective-permute-start | bytes 393224 | tf_op jit(solution)/shard_map/ppermute | solution.py:398
  16.1 9.6 %collective-permute-start.4 = (bf16[432,128]{1,0:T(8,128)(2,1)S(1)}, bf16[432,128]{1,0:T(8,128)(2,1)S(1)}, u32[]{:S(2)}, u32[]{:S(2)}) collective-permute-start(bf16[432,128]{1,0:T(8,128)(2,1)S(1)} %select_convert_fusion), channel_id=1, source_target_pairs={{0,4},{1,5},{2,6},{3,7},{4,0},{5,1},{6,2},{7,3},{8,12},{9,13},{10,... | collective-permute-start | bytes 331784 | tf_op jit(solution)/shard_map/ppermute | solution.py:392
  25.7 2.7 %collective-permute-start.6 = (bf16[224,128]{1,0:T(8,128)(2,1)S(1)}, bf16[224,128]{1,0:T(8,128)(2,1)S(1)}, u32[]{:S(2)}, u32[]{:S(2)}) collective-permute-start(bf16[224,128]{1,0:T(8,128)(2,1)S(1)} %get-tuple-element.68), channel_id=1, source_target_pairs={{0,1},{1,0},{2,3},{3,2},{4,5},{5,4},{6,7},{7,6},{8,9},{9,8},{10,11... | collective-permute-start | bytes 172040 | tf_op jit(solution)/shard_map/ppermute | solution.py:392
  25.8 8.7 %collective-permute-start.5 = (bf16[432,128]{1,0:T(8,128)(2,1)S(1)}, bf16[432,128]{1,0:T(8,128)(2,1)S(1)}, u32[]{:S(2)}, u32[]{:S(2)}) collective-permute-start(bf16[432,128]{1,0:T(8,128)(2,1)S(1)} %add_convert_fusion.2), channel_id=1, source_target_pairs={{0,8},{1,9},{2,10},{3,11},{4,12},{5,13},{6,14},{7,15},{8,0},{9,1},... | collective-permute-start | bytes 331784 | tf_op jit(solution)/shard_map/ppermute | solution.py:392
  28.4 6.1 %collective-permute-start.7 = (bf16[224,128]{1,0:T(8,128)(2,1)S(1)}, bf16[224,128]{1,0:T(8,128)(2,1)S(1)}, u32[]{:S(2)}, u32[]{:S(2)}) collective-permute-start(bf16[224,128]{1,0:T(8,128)(2,1)S(1)} %add_convert_fusion.5), channel_id=1, source_target_pairs={{0,2},{1,3},{2,0},{3,1},{4,6},{5,7},{6,4},{7,5},{8,10},{9,11},{10,... | collective-permute-start | bytes 172040 | tf_op jit(solution)/shard_map/ppermute | solution.py:392
  34.6 5.7 %collective-permute-start.9 = (bf16[224,128]{1,0:T(8,128)(2,1)S(1)}, bf16[224,128]{1,0:T(8,128)(2,1)S(1)}, u32[]{:S(2)}, u32[]{:S(2)}) collective-permute-start(bf16[224,128]{1,0:T(8,128)(2,1)S(1)} %add_convert_fusion.4), channel_id=1, source_target_pairs={{0,8},{1,9},{2,10},{3,11},{4,12},{5,13},{6,14},{7,15},{8,0},{9,1},... | collective-permute-start | bytes 172040 | tf_op jit(solution)/shard_map/ppermute | solution.py:392
  35.0 5.4 %collective-permute-start.8 = (bf16[432,128]{1,0:T(8,128)(2,1)S(1)}, bf16[432,128]{1,0:T(8,128)(2,1)S(1)}, u32[]{:S(2)}, u32[]{:S(2)}) collective-permute-start(bf16[432,128]{1,0:T(8,128)(2,1)S(1)} %add_convert_fusion.1), channel_id=1, source_target_pairs={{0,2},{1,3},{2,0},{3,1},{4,6},{5,7},{6,4},{7,5},{8,10},{9,11},{10,... | collective-permute-start | bytes 331784 | tf_op jit(solution)/shard_map/ppermute | solution.py:392
  40.4 5.9 %collective-permute-start.10 = (bf16[656,128]{1,0:T(8,128)(2,1)S(1)}, bf16[656,128]{1,0:T(8,128)(2,1)S(1)}, u32[]{:S(2)}, u32[]{:S(2)}) collective-permute-start(bf16[656,128]{1,0:T(8,128)(2,1)S(1)} %pad_maximum_fusion.1), channel_id=1, source_target_pairs={{0,4},{1,5},{2,6},{3,7},{4,0},{5,1},{6,2},{7,3},{8,12},{9,13},{10,... | collective-permute-start | bytes 503816 | tf_op jit(solution)/shard_map/ppermute | solution.py:392
  46.4 1.7 %collective-permute-start.11 = (bf16[1312,128]{1,0:T(8,128)(2,1)S(1)}, bf16[1312,128]{1,0:T(8,128)(2,1)S(1)}, u32[]{:S(2)}, u32[]{:S(2)}) collective-permute-start(bf16[1312,128]{1,0:T(8,128)(2,1)S(1)} %pad_maximum_fusion.refs_0_), channel_id=1, source_target_pairs={{0,1},{1,0},{2,3},{3,2},{4,5},{5,4},{6,7},{7,6},{8,9},{9,8},{10,11... | collective-permute-start | bytes 1007624 | tf_op jit(solution)/shard_map/ppermute | solution.py:392

commit v5 on v4

--- a/solution.py
+++ b/solution.py
@@ -144,7 +144,8 @@
 
 
 def far_kernel(
-    far_ref, vol_near_ref, pool_near_ref, wmid_ref, wtop_ref, cot_ref, delta_ref, pre_ref, vol_ref, pool_ref, *, h, w, spatial
+    far_ref, vol_near_ref, pool_near_ref, wmid_ref, wtop_ref, cot_ref, delta_ref, pre_ref, vol_ref, keep_ref, send_ref, pool_ref,
+    grad_ref, *, h, w, spatial
 ):
     half = w // 2
     here = lax.axis_index("spatial")
@@ -180,6 +181,7 @@
         pre_top = dot(wtop_ref[...], cols, ((0,), (0,)))
         at = slice(j * hp * half, (j + 1) * hp * half)
         delta_ref[:, at] = (cot_ref[:, at].astype(F32) * gelu_slope(pre_top)).astype(BF16)
+    top_part(delta_ref, pool_ref, keep_ref, send_ref, grad_ref, hp, half)
 
 
 def halve(whole_ref, keep_ref, send_ref):
@@ -199,7 +201,7 @@
             slope_ref[:, lanes(side * part + at, 128)] = value
 
 
-def top_kernel(delta_ref, pool_ref, keep_ref, send_ref, out_ref, *, hp, wp):
+def top_part(delta_ref, pool_ref, keep_ref, send_ref, out_ref, hp, wp):
     cout = delta_ref.shape[0]
     for at in range(0, delta_ref.shape[1], wp):
         send_ref[at // wp * cout : (at // wp + 1) * cout, :] = delta_ref[:, at : at + wp]
@@ -459,31 +461,24 @@
         moved=3_000_000,
     )
     far, wback, vol_near, pool_near = lax.optimization_barrier((far, wback, vol_near, pool_near))
-    delta, pre_far, vol, pool = kernel_call(
+    top_rows = 27 * mid
+    delta_rows = cot.size // cout
+    delta, pre_far, vol, keep, send = kernel_call(
         lambda *refs: far_kernel(*refs, h=h, w=w, spatial=spatial),
         "far_side",
         (
             shape(cot.shape, BF16),
             shape((mid, count * plane), F32),
             shape((cin, (nz + 2 * halo) * size), BF16),
-            shape((3 * mid, count * pool_size), BF16),
+            shape((top_rows // 2, cout), F32),
+            shape((delta_rows + top_rows // 2, cout), BF16),
         ),
         (far, vol_near, pool_near, wmid, wtop, cot),
-        flops=900_000_000,
-        moved=4_000_000,
+        scratch=(pltpu.VMEM((3 * mid, count * pool_size), BF16), pltpu.VMEM((top_rows, cout), F32)),
+        flops=1_100_000_000,
+        moved=5_000_000,
     )
     delta_far = across(delta)
-    top_rows = 27 * mid
-    delta_rows = delta.size // cout
-    keep, send = kernel_call(
-        lambda *refs: top_kernel(*refs, hp=hp, wp=wp),
-        "top_part",
-        (shape((top_rows // 2, cout), F32), shape((delta_rows + top_rows // 2, cout), BF16)),
-        (delta, pool),
-        scratch=(pltpu.VMEM((top_rows, cout), F32),),
-        flops=226_000_000,
-        moved=1_500_000,
-    )
     slope = kernel_call(
         lambda *refs: slope_kernel(*refs, plane=plane),
         "slope",
@@ -531,10 +526,12 @@
         top_sum = rounded(add_both(top_sum, bit))
     mid_sum = rounded(keep + partner(send, 1).astype(F32))
     mid_sum = rounded(add_both(mid_sum, 2))
-    top_sum, mid_sum = lax.optimization_barrier((top_sum, mid_sum))
+    top_sum, _ = lax.optimization_barrier((top_sum, mid_sum))
+    mid_sum = rounded(add_both(mid_sum, 4))
     mid_sum, field = lax.optimization_barrier((mid_sum, field))
-    for bit in bits:
+    for bit in bits[:-1]:
         mid_sum = rounded(add_both(mid_sum, bit))
+    mid_sum = add_both(mid_sum, bits[-1])
     top_sum = rounded(add_both(top_sum, 2))
     input_grad = kernel_call(
         lambda *refs: input_kernel(*refs, h=h, w=w),
@@ -544,11 +541,8 @@
         flops=452_000_000,
         moved=2_000_000,
     )
-    both = jnp.concatenate([top_sum, mid_sum], axis=0)
-    both, input_grad = lax.optimization_barrier((both, input_grad))
-    received = partner(both, 4)
-    top_sum = jnp.concatenate(in_order(top_sum, received[: top_sum.shape[0]], low), axis=0)
-    mid_sum = mid_sum.astype(F32) + received[-mid_rows:].astype(F32)
+    top_sum, input_grad = lax.optimization_barrier((top_sum, input_grad))
+    top_sum = jnp.concatenate(in_order(top_sum, partner(top_sum, 4), low), axis=0)
     mid_high = rounded(mid_sum)
     mid_low = rounded(mid_sum - mid_high.astype(F32))
     both = jnp.concatenate([top_sum, mid_high, mid_low], axis=0)

time: 49.5 us -> 49.3 us (level)
  waiting for transfers between devices: 13 us -> 12.4 us
    ppermute x10 -> x11, waiting for transfers between devices: 13 us -> 12.4 us  [partner(): return lax.ppermute(block, 'spatial', [(i, i ^ bit) for i in range(size)])]
    ppermute x10 -> x11, starting transfers between devices: 18.9 us -> 19.3 us  [partner(): return lax.ppermute(block, 'spatial', [(i, i ^ bit) for i in range(size)])]
    pallas_call x8 -> x7, Pallas kernels: 10.9 us -> 10.9 us  [kernel_call(): pl.pallas_call(body, name=name, out_shape=outs, in_specs=[whole] * len(ar...]
  transfers between devices with their start and end apart: 12 -> 13, of which waited for: 5 -> 8; matrix products, arithmetic and copies ran while one was open for 6% -> 6% of each run, Pallas kernels for 14% -> 14%
where the time goes in v5:
time: 49.3 us; the launch traced here: 49.1 us
  starting transfers between devices  20.6 us (42%)
  waiting for transfers between devices  12.4 us (25%)
  Pallas kernels  10.9 us (22%)
  local copies, waits for them, and re-layouts  3.93 us (8%)
  between operations  0.88 us (2%)
    ppermute x11, starting transfers between devices, partner(): return lax.ppermute(block, 'spatial', [(i, i ^ bit) for i in range(size)])  19.3 us
    ppermute x11, waiting for transfers between devices, partner(): return lax.ppermute(block, 'spatial', [(i, i ^ bit) for i in range(size)])  12.4 us
    pallas_call x7, Pallas kernels, kernel_call(): pl.pallas_call(body, name=name, out_shape=outs, in_specs=[whole] * len(ar...  10.9 us
    ppermute x2, starting transfers between devices, across(): return lax.ppermute(block, 'spatial', pairs + [(j, i) for i, j in pairs])  1.32 us
    reshape x2, local copies, waits for them, and re-layouts, shards(): split = weights_mid.reshape(mid, 9, 3, cin)  1.21 us
    reshape x1, local copies, waits for them, and re-layouts, shards(): flat = volume.reshape(cin, nz * plane)  1.17 us
  transfers between devices with their start and end apart: 13, of which 8 were waited for; matrix products, arithmetic and copies ran while one was open for 6% of the time, Pallas kernels for 14%

profile of v5, /device:TPU:0, one launch (start us, length us, event | category | flops | bytes accessed | tf_op | source)
XLA Modules:
  0.0 49.1 jit_solution(9463310459864304356)
XLA Ops:
  0.6 0.0 copy-start.1
  0.7 1.2 %reshape.33.refs_1_ = bf16[32,4096]{1,0:T(8,128)(2,1)S(1)} reshape(bf16[32,4,4,256]{3,2,1,0:T(4,128)(2,1)} %param.4) | data formatting | bytes 524288 | tf_op jit(solution)/shard_map/reshape | solution.py:438
  1.8 0.0 copy-start.2
  1.9 0.5 %collective-permute-start.1 = (bf16[32,3072]{1,0:T(8,128)(2,1)S(1)}, bf16[32,3072]{1,0:T(8,128)(2,1)S(1)}, u32[]{:S(2)}, u32[]{:S(2)}) collective-permute-start(bf16[32,3072]{1,0:T(8,128)(2,1)S(1)} %get-tuple-element.75), channel_id=1, source_target_pairs={{0,1},{1,0},{2,3},{3,2},{4,5},{5,4},{6,7},{7,6},{8,9},{9,8},{10,11... | collective-permute-start | bytes 589832 | tf_op jit(solution)/shard_map/ppermute | solution.py:394
  2.4 0.7 %collective-permute-start = (bf16[32,3072]{1,0:T(8,128)(2,1)S(1)}, bf16[32,3072]{1,0:T(8,128)(2,1)S(1)}, u32[]{:S(2)}, u32[]{:S(2)}) collective-permute-start(bf16[32,3072]{1,0:T(8,128)(2,1)S(1)} %get-tuple-element.76), channel_id=1, source_target_pairs={{1,2},{3,4},{5,6},{7,8},{9,10},{11,12},{13,14},{2,1},{4,3},{6,5},{... | collective-permute-start | bytes 589832 | tf_op jit(solution)/shard_map/ppermute | solution.py:400
  3.1 1.1 %copy.16 = bf16[64,9,3,32]{0,2,3,1:T(4,128)(2,1)S(1)} copy(bf16[64,9,3,32]{0,3,2,1:T(8,128)(2,1)} %bitcast.23) | data formatting | bytes 221184 | tf_op jit(solution)/shard_map/reshape | solution.py:442
  4.2 0.0 copy-done.1
  4.2 0.1 copy.15
  4.3 0.2 reshape.36
  4.5 0.1 copy.11.refs_2_.refs_3_
  4.6 0.2 reshape.35.refs_1_
  4.9 0.0 copy-done.2
  4.9 0.1 reshape.38.refs_5_
  5.0 0.0 copy-start
  5.0 0.0 collective-permute-done.1.refs_0_
  5.0 1.5 %near_side.1 = (bf16[32,10752]{1,0:T(8,128)(2,1)S(1)}, f32[64,4096]{1,0:T(8,128)S(1)}, bf16[192,1024]{1,0:T(8,128)(2,1)S(1)}) custom-call(bf16[32,3072]{1,0:T(8,128)(2,1)S(1)} %collective-permute-done.1.refs_0_, bf16[32,4096]{1,0:T(8,128)(2,1)S(1)} %reshape.33.refs_1_, bf16[192,288]{1,0:T(8,128)(2,1)S(1)} %copy.11.refs_2_.refs_3_), custom_call_target="tpu_custom_call" | custom-call | flops 900000000 | bytes 3000000 | tf_op jit(solution)/shard_map/near_side/pallas_call | solution.py:23
  6.5 0.0 collective-permute-done.refs_0_
  6.5 0.0 copy-done
  6.5 2.8 %far_side.1 = (bf16[128,512]{1,0:T(8,128)(2,1)S(1)}, f32[64,4096]{1,0:T(8,128)S(1)}, bf16[32,15360]{1,0:T(8,128)(2,1)S(1)}, f32[864,128]{1,0:T(8,128)S(1)}, bf16[1376,128]{1,0:T(8,128)(2,1)S(1)}) custom-call(bf16[32,3072]{1,0:T(8,128)(2,1)S(1)} %collective-permute-done.refs_0_, bf16[32,10752]{1,0:T(8,128)(2,1)S(1)} %get-tuple-element.44.refs_1_, ...), custom_call_target="tpu_custom_call" | custom-call | flops 1100000000 | bytes 5000000 | tf_op jit(solution)/shard_map/far_side/pallas_call | solution.py:23
  9.3 5.2 %collective-permute-start.3 = (bf16[1376,128]{1,0:T(8,128)(2,1)S(1)}, bf16[1376,128]{1,0:T(8,128)(2,1)S(1)}, u32[]{:S(2)}, u32[]{:S(2)}) collective-permute-start(bf16[1376,128]{1,0:T(8,128)(2,1)S(1)} %get-tuple-element.47), channel_id=1, source_target_pairs={{0,1},{1,0},{2,3},{3,2},{4,5},{5,4},{6,7},{7,6},{8,9},{9,8},{10,11... | collective-permute-start | bytes 1056776 | tf_op jit(solution)/shard_map/ppermute | solution.py:394
  14.5 0.7 %collective-permute-start.2 = (bf16[128,512]{1,0:T(8,128)(2,1)S(1)}, bf16[128,512]{1,0:T(8,128)(2,1)S(1)}, u32[]{:S(2)}, u32[]{:S(2)}) collective-permute-start(bf16[128,512]{1,0:T(8,128)(2,1)S(1)} %get-tuple-element.46.refs_1_), channel_id=1, source_target_pairs={{1,2},{3,4},{5,6},{7,8},{9,10},{11,12},{13,14},{2,1},{4,3},{6,5},{... | collective-permute-start | bytes 393224 | tf_op jit(solution)/shard_map/ppermute | solution.py:400
  15.2 0.8 %slope.1.refs_2_ = f32[64,6144]{1,0:T(8,128)S(1)} custom-call(f32[64,4096]{1,0:T(8,128)S(1)} %get-tuple-element.48.refs_0_, f32[64,4096]{1,0:T(8,128)S(1)} %get-tuple-element.49.refs_1_), custom_call_target="tpu_custom_call" | custom-call | flops 100000000 | bytes 3000000 | tf_op jit(solution)/shard_map/slope/pallas_call | solution.py:23
  16.0 0.0 collective-permute-done.3.refs_0_
  16.0 5.2 %collective-permute-start.4 = (bf16[432,128]{1,0:T(8,128)(2,1)S(1)}, bf16[432,128]{1,0:T(8,128)(2,1)S(1)}, u32[]{:S(2)}, u32[]{:S(2)}) collective-permute-start(bf16[432,128]{1,0:T(8,128)(2,1)S(1)} %select_convert_fusion), channel_id=1, source_target_pairs={{0,4},{1,5},{2,6},{3,7},{4,0},{5,1},{6,2},{7,3},{8,12},{9,13},{10,... | collective-permute-start | bytes 331784 | tf_op jit(solution)/shard_map/ppermute | solution.py:394
  21.3 1.4 %backward_near.1 = (f32[288,192]{1,0:T(8,128)S(1)}, bf16[64,4608]{1,0:T(8,128)(2,1)S(1)}) custom-call(bf16[1376,128]{1,0:T(8,128)(2,1)S(1)} %collective-permute-done.3.refs_0_, bf16[128,512]{1,0:T(8,128)(2,1)S(1)} %get-tuple-element.46.refs_1_, f32[64,6144]{1,0:T(8,128)S(1)} %slope.1.refs_2_, bf16[32,15360]{1,0:T(8,128)(2,1)S(1)} %get-tuple-element.50.refs_3_, ...), custom_call_target="tpu_custom_call" | custom-call | flops 500000000 | bytes 3000000 | tf_op jit(solution)/shard_map/backward_near/pallas_call | solution.py:23
  22.7 0.0 collective-permute-done.2.refs_0_
  22.7 1.5 %backward_far.1 = (f32[224,128]{1,0:T(8,128)S(1)}, bf16[224,128]{1,0:T(8,128)(2,1)S(1)}, bf16[64,9216]{1,0:T(8,128)(2,1)S(1)}) custom-call(bf16[128,512]{1,0:T(8,128)(2,1)S(1)} %collective-permute-done.2.refs_0_, bf16[128,512]{1,0:T(8,128)(2,1)S(1)} %get-tuple-element.46.refs_1_, f32[64,6144]{1,0:T(8,128)S(1)} %slope.1.refs_2_, ...), custom_call_target="tpu_custom_call" | custom-call | flops 500000000 | bytes 4000000 | tf_op jit(solution)/shard_map/backward_far/pallas_call | solution.py:23
  24.3 1.3 %collective-permute-done.4 = bf16[432,128]{1,0:T(8,128)(2,1)S(1)} collective-permute-done((bf16[432,128]{1,0:T(8,128)(2,1)S(1)}, bf16[432,128]{1,0:T(8,128)(2,1)S(1)}, u32[]{:S(2)}, u32[]{:S(2)}) %collective-permute-start.4) | collective-permute-done | bytes 110624 | tf_op jit(solution)/shard_map/ppermute | solution.py:394
  25.7 0.1 collective-permute-start.6
  25.7 1.2 %collective-permute-done.6 = bf16[224,128]{1,0:T(8,128)(2,1)S(1)} collective-permute-done((bf16[224,128]{1,0:T(8,128)(2,1)S(1)}, bf16[224,128]{1,0:T(8,128)(2,1)S(1)}, u32[]{:S(2)}, u32[]{:S(2)}) %collective-permute-start.6) | collective-permute-done | bytes 57376 | tf_op jit(solution)/shard_map/ppermute | solution.py:394
  27.0 1.0 %collective-permute-start.7 = (bf16[224,128]{1,0:T(8,128)(2,1)S(1)}, bf16[224,128]{1,0:T(8,128)(2,1)S(1)}, u32[]{:S(2)}, u32[]{:S(2)}) collective-permute-start(bf16[224,128]{1,0:T(8,128)(2,1)S(1)} %add_convert_fusion.5), channel_id=1, source_target_pairs={{0,2},{1,3},{2,0},{3,1},{4,6},{5,7},{6,4},{7,5},{8,10},{9,11},{10,... | collective-permute-start | bytes 172040 | tf_op jit(solution)/shard_map/ppermute | solution.py:394
  28.0 2.6 %collective-permute-start.5 = (bf16[432,128]{1,0:T(8,128)(2,1)S(1)}, bf16[432,128]{1,0:T(8,128)(2,1)S(1)}, u32[]{:S(2)}, u32[]{:S(2)}) collective-permute-start(bf16[432,128]{1,0:T(8,128)(2,1)S(1)} %add_convert_fusion.2), channel_id=1, source_target_pairs={{0,8},{1,9},{2,10},{3,11},{4,12},{5,13},{6,14},{7,15},{8,0},{9,1},... | collective-permute-start | bytes 331784 | tf_op jit(solution)/shard_map/ppermute | solution.py:394
  30.6 0.6 %collective-permute-done.7 = bf16[224,128]{1,0:T(8,128)(2,1)S(1)} collective-permute-done((bf16[224,128]{1,0:T(8,128)(2,1)S(1)}, bf16[224,128]{1,0:T(8,128)(2,1)S(1)}, u32[]{:S(2)}, u32[]{:S(2)}) %collective-permute-start.7) | collective-permute-done | bytes 57376 | tf_op jit(solution)/shard_map/ppermute | solution.py:394
  31.3 1.0 %collective-permute-start.9 = (bf16[224,128]{1,0:T(8,128)(2,1)S(1)}, bf16[224,128]{1,0:T(8,128)(2,1)S(1)}, u32[]{:S(2)}, u32[]{:S(2)}) collective-permute-start(bf16[224,128]{1,0:T(8,128)(2,1)S(1)} %add_convert_fusion.4), channel_id=1, source_target_pairs={{0,4},{1,5},{2,6},{3,7},{4,0},{5,1},{6,2},{7,3},{8,12},{9,13},{10,... | collective-permute-start | bytes 172040 | tf_op jit(solution)/shard_map/ppermute | solution.py:394
  32.3 4.1 %collective-permute-done.5 = bf16[432,128]{1,0:T(8,128)(2,1)S(1)} collective-permute-done((bf16[432,128]{1,0:T(8,128)(2,1)S(1)}, bf16[432,128]{1,0:T(8,128)(2,1)S(1)}, u32[]{:S(2)}, u32[]{:S(2)}) %collective-permute-start.5) | collective-permute-done | bytes 110624 | tf_op jit(solution)/shard_map/ppermute | solution.py:394
  36.5 0.9 %collective-permute-start.8 = (bf16[432,128]{1,0:T(8,128)(2,1)S(1)}, bf16[432,128]{1,0:T(8,128)(2,1)S(1)}, u32[]{:S(2)}, u32[]{:S(2)}) collective-permute-start(bf16[432,128]{1,0:T(8,128)(2,1)S(1)} %add_convert_fusion.1), channel_id=1, source_target_pairs={{0,2},{1,3},{2,0},{3,1},{4,6},{5,7},{6,4},{7,5},{8,10},{9,11},{10,... | collective-permute-start | bytes 331784 | tf_op jit(solution)/shard_map/ppermute | solution.py:394
  37.4 0.0 collective-permute-done.9
  37.4 0.8 %collective-permute-start.11 = (bf16[224,128]{1,0:T(8,128)(2,1)S(1)}, bf16[224,128]{1,0:T(8,128)(2,1)S(1)}, u32[]{:S(2)}, u32[]{:S(2)}) collective-permute-start(bf16[224,128]{1,0:T(8,128)(2,1)S(1)} %add_convert_fusion.3), channel_id=1, source_target_pairs={{0,8},{1,9},{2,10},{3,11},{4,12},{5,13},{6,14},{7,15},{8,0},{9,1},... | collective-permute-start | bytes 172040 | tf_op jit(solution)/shard_map/ppermute | solution.py:394
  38.3 1.7 %input_grad.1 = bf16[32,4096]{1,0:T(8,128)(2,1)S(1)} custom-call(bf16[64,9216]{1,0:T(8,128)(2,1)S(1)} %get-tuple-element.68.refs_0_, bf16[96,576]{1,0:T(8,128)(2,1)S(1)} %reshape.35.refs_1_), custom_call_target="tpu_custom_call" | custom-call | flops 452000000 | bytes 2000000 | tf_op jit(solution)/shard_map/input_grad/pallas_call | solution.py:23
  40.0 1.3 %collective-permute-done.8 = bf16[432,128]{1,0:T(8,128)(2,1)S(1)} collective-permute-done((bf16[432,128]{1,0:T(8,128)(2,1)S(1)}, bf16[432,128]{1,0:T(8,128)(2,1)S(1)}, u32[]{:S(2)}, u32[]{:S(2)}) %collective-permute-start.8) | collective-permute-done | bytes 110624 | tf_op jit(solution)/shard_map/ppermute | solution.py:394
  41.3 1.7 %collective-permute-start.10 = (bf16[432,128]{1,0:T(8,128)(2,1)S(1)}, bf16[432,128]{1,0:T(8,128)(2,1)S(1)}, u32[]{:S(2)}, u32[]{:S(2)}) collective-permute-start(bf16[432,128]{1,0:T(8,128)(2,1)S(1)} %add_convert_fusion), channel_id=1, source_target_pairs={{0,4},{1,5},{2,6},{3,7},{4,0},{5,1},{6,2},{7,3},{8,12},{9,13},{10,... | collective-permute-start | bytes 331784 | tf_op jit(solution)/shard_map/ppermute | solution.py:394
  43.0 0.2 collective-permute-done.11
  43.3 2.9 %collective-permute-done.10 = bf16[432,128]{1,0:T(8,128)(2,1)S(1)} collective-permute-done((bf16[432,128]{1,0:T(8,128)(2,1)S(1)}, bf16[432,128]{1,0:T(8,128)(2,1)S(1)}, u32[]{:S(2)}, u32[]{:S(2)}) %collective-permute-start.10) | collective-permute-done | bytes 110624 | tf_op jit(solution)/shard_map/ppermute | solution.py:394
  46.2 0.1 collective-permute-start.12
  46.3 0.9 %reshape.39 = bf16[32,4,4,256]{3,2,1,0:T(4,128)(2,1)} reshape(bf16[32,4096]{1,0:T(8,128)(2,1)S(1)} %input_grad.1) | data formatting | bytes 524288 | tf_op jit(solution)/shard_map/reshape | solution.py:562
  47.2 0.7 %collective-permute-done.12.refs_1_ = bf16[1312,128]{1,0:T(8,128)(2,1)S(1)} collective-permute-done((bf16[1312,128]{1,0:T(8,128)(2,1)S(1)}, bf16[1312,128]{1,0:T(8,128)(2,1)S(1)}, u32[]{:S(2)}, u32[]{:S(2)}) %collective-permute-start.12) | collective-permute-done | bytes 335904 | tf_op jit(solution)/shard_map/ppermute | solution.py:394
  47.9 1.2 %finish.1 = (f32[1728,128]{1,0:T(8,128)}, f32[864,64]{1,0:T(8,128)}) custom-call(bf16[1312,128]{1,0:T(8,128)(2,1)S(1)} %pad_maximum_fusion.refs_0_, bf16[1312,128]{1,0:T(8,128)(2,1)S(1)} %collective-permute-done.12.refs_1_), custom_call_target="tpu_custom_call" | custom-call | bytes 2000000 | tf_op jit(solution)/shard_map/finish/pallas_call | solution.py:23
  (14 shorter events, 0.4 us)
Async XLA Ops:
  0.6 3.5 %copy-start.1 = (bf16[64,27,32]{0,2,1:T(8,128)(2,1)S(1)}, bf16[64,27,32]{0,2,1:T(8,128)(2,1)}, u32[]{:S(2)}) copy-start(bf16[64,27,32]{0,2,1:T(8,128)(2,1)} %param.5) | copy-start | bytes 331780
  1.8 3.1 %copy-start.2 = (bf16[128,2,2,128]{3,2,1,0:T(2,128)(2,1)S(1)}, bf16[128,2,2,128]{3,2,1,0:T(2,128)(2,1)}, u32[]{:S(2)}) copy-start(bf16[128,2,2,128]{3,2,1,0:T(2,128)(2,1)} %param.7) | copy-start | bytes 393220
  1.9 3.1 %collective-permute-start.1 = (bf16[32,3072]{1,0:T(8,128)(2,1)S(1)}, bf16[32,3072]{1,0:T(8,128)(2,1)S(1)}, u32[]{:S(2)}, u32[]{:S(2)}) collective-permute-start(bf16[32,3072]{1,0:T(8,128)(2,1)S(1)} %get-tuple-element.75), channel_id=1, source_target_pairs={{0,1},{1,0},{2,3},{3,2},{4,5},{5,4},{6,7},{7,6},{8,9},{9,8},{10,11... | collective-permute-start | bytes 589832 | tf_op jit(solution)/shard_map/ppermute | solution.py:394
  2.4 4.1 %collective-permute-start = (bf16[32,3072]{1,0:T(8,128)(2,1)S(1)}, bf16[32,3072]{1,0:T(8,128)(2,1)S(1)}, u32[]{:S(2)}, u32[]{:S(2)}) collective-permute-start(bf16[32,3072]{1,0:T(8,128)(2,1)S(1)} %get-tuple-element.76), channel_id=1, source_target_pairs={{1,2},{3,4},{5,6},{7,8},{9,10},{11,12},{13,14},{2,1},{4,3},{6,5},{... | collective-permute-start | bytes 589832 | tf_op jit(solution)/shard_map/ppermute | solution.py:400
  5.0 1.5 %copy-start = (bf16[128,27,64]{0,2,1:T(8,128)(2,1)S(1)}, bf16[128,27,64]{0,2,1:T(8,128)(2,1)}, u32[]{:S(2)}) copy-start(bf16[128,27,64]{0,2,1:T(8,128)(2,1)} %param.6) | copy-start | bytes 1327108
  9.3 6.7 %collective-permute-start.3 = (bf16[1376,128]{1,0:T(8,128)(2,1)S(1)}, bf16[1376,128]{1,0:T(8,128)(2,1)S(1)}, u32[]{:S(2)}, u32[]{:S(2)}) collective-permute-start(bf16[1376,128]{1,0:T(8,128)(2,1)S(1)} %get-tuple-element.47), channel_id=1, source_target_pairs={{0,1},{1,0},{2,3},{3,2},{4,5},{5,4},{6,7},{7,6},{8,9},{9,8},{10,11... | collective-permute-start | bytes 1056776 | tf_op jit(solution)/shard_map/ppermute | solution.py:394
  14.5 8.2 %collective-permute-start.2 = (bf16[128,512]{1,0:T(8,128)(2,1)S(1)}, bf16[128,512]{1,0:T(8,128)(2,1)S(1)}, u32[]{:S(2)}, u32[]{:S(2)}) collective-permute-start(bf16[128,512]{1,0:T(8,128)(2,1)S(1)} %get-tuple-element.46.refs_1_), channel_id=1, source_target_pairs={{1,2},{3,4},{5,6},{7,8},{9,10},{11,12},{13,14},{2,1},{4,3},{6,5},{... | collective-permute-start | bytes 393224 | tf_op jit(solution)/shard_map/ppermute | solution.py:400
  16.0 9.6 %collective-permute-start.4 = (bf16[432,128]{1,0:T(8,128)(2,1)S(1)}, bf16[432,128]{1,0:T(8,128)(2,1)S(1)}, u32[]{:S(2)}, u32[]{:S(2)}) collective-permute-start(bf16[432,128]{1,0:T(8,128)(2,1)S(1)} %select_convert_fusion), channel_id=1, source_target_pairs={{0,4},{1,5},{2,6},{3,7},{4,0},{5,1},{6,2},{7,3},{8,12},{9,13},{10,... | collective-permute-start | bytes 331784 | tf_op jit(solution)/shard_map/ppermute | solution.py:394
  25.7 1.3 %collective-permute-start.6 = (bf16[224,128]{1,0:T(8,128)(2,1)S(1)}, bf16[224,128]{1,0:T(8,128)(2,1)S(1)}, u32[]{:S(2)}, u32[]{:S(2)}) collective-permute-start(bf16[224,128]{1,0:T(8,128)(2,1)S(1)} %get-tuple-element.65), channel_id=1, source_target_pairs={{0,1},{1,0},{2,3},{3,2},{4,5},{5,4},{6,7},{7,6},{8,9},{9,8},{10,11... | collective-permute-start | bytes 172040 | tf_op jit(solution)/shard_map/ppermute | solution.py:394
  27.0 4.2 %collective-permute-start.7 = (bf16[224,128]{1,0:T(8,128)(2,1)S(1)}, bf16[224,128]{1,0:T(8,128)(2,1)S(1)}, u32[]{:S(2)}, u32[]{:S(2)}) collective-permute-start(bf16[224,128]{1,0:T(8,128)(2,1)S(1)} %add_convert_fusion.5), channel_id=1, source_target_pairs={{0,2},{1,3},{2,0},{3,1},{4,6},{5,7},{6,4},{7,5},{8,10},{9,11},{10,... | collective-permute-start | bytes 172040 | tf_op jit(solution)/shard_map/ppermute | solution.py:394
  28.0 8.4 %collective-permute-start.5 = (bf16[432,128]{1,0:T(8,128)(2,1)S(1)}, bf16[432,128]{1,0:T(8,128)(2,1)S(1)}, u32[]{:S(2)}, u32[]{:S(2)}) collective-permute-start(bf16[432,128]{1,0:T(8,128)(2,1)S(1)} %add_convert_fusion.2), channel_id=1, source_target_pairs={{0,8},{1,9},{2,10},{3,11},{4,12},{5,13},{6,14},{7,15},{8,0},{9,1},... | collective-permute-start | bytes 331784 | tf_op jit(solution)/shard_map/ppermute | solution.py:394
  31.3 6.1 %collective-permute-start.9 = (bf16[224,128]{1,0:T(8,128)(2,1)S(1)}, bf16[224,128]{1,0:T(8,128)(2,1)S(1)}, u32[]{:S(2)}, u32[]{:S(2)}) collective-permute-start(bf16[224,128]{1,0:T(8,128)(2,1)S(1)} %add_convert_fusion.4), channel_id=1, source_target_pairs={{0,4},{1,5},{2,6},{3,7},{4,0},{5,1},{6,2},{7,3},{8,12},{9,13},{10,... | collective-permute-start | bytes 172040 | tf_op jit(solution)/shard_map/ppermute | solution.py:394
  36.5 4.8 %collective-permute-start.8 = (bf16[432,128]{1,0:T(8,128)(2,1)S(1)}, bf16[432,128]{1,0:T(8,128)(2,1)S(1)}, u32[]{:S(2)}, u32[]{:S(2)}) collective-permute-start(bf16[432,128]{1,0:T(8,128)(2,1)S(1)} %add_convert_fusion.1), channel_id=1, source_target_pairs={{0,2},{1,3},{2,0},{3,1},{4,6},{5,7},{6,4},{7,5},{8,10},{9,11},{10,... | collective-permute-start | bytes 331784 | tf_op jit(solution)/shard_map/ppermute | solution.py:394
  37.4 5.8 %collective-permute-start.11 = (bf16[224,128]{1,0:T(8,128)(2,1)S(1)}, bf16[224,128]{1,0:T(8,128)(2,1)S(1)}, u32[]{:S(2)}, u32[]{:S(2)}) collective-permute-start(bf16[224,128]{1,0:T(8,128)(2,1)S(1)} %add_convert_fusion.3), channel_id=1, source_target_pairs={{0,8},{1,9},{2,10},{3,11},{4,12},{5,13},{6,14},{7,15},{8,0},{9,1},... | collective-permute-start | bytes 172040 | tf_op jit(solution)/shard_map/ppermute | solution.py:394
  41.3 4.8 %collective-permute-start.10 = (bf16[432,128]{1,0:T(8,128)(2,1)S(1)}, bf16[432,128]{1,0:T(8,128)(2,1)S(1)}, u32[]{:S(2)}, u32[]{:S(2)}) collective-permute-start(bf16[432,128]{1,0:T(8,128)(2,1)S(1)} %add_convert_fusion), channel_id=1, source_target_pairs={{0,4},{1,5},{2,6},{3,7},{4,0},{5,1},{6,2},{7,3},{8,12},{9,13},{10,... | collective-permute-start | bytes 331784 | tf_op jit(solution)/shard_map/ppermute | solution.py:394
  46.2 1.7 %collective-permute-start.12 = (bf16[1312,128]{1,0:T(8,128)(2,1)S(1)}, bf16[1312,128]{1,0:T(8,128)(2,1)S(1)}, u32[]{:S(2)}, u32[]{:S(2)}) collective-permute-start(bf16[1312,128]{1,0:T(8,128)(2,1)S(1)} %pad_maximum_fusion.refs_0_), channel_id=1, source_target_pairs={{0,1},{1,0},{2,3},{3,2},{4,5},{5,4},{6,7},{7,6},{8,9},{9,8},{10,11... | collective-permute-start | bytes 1007624 | tf_op jit(solution)/shard_map/ppermute | solution.py:394

commit v6 on v5

--- a/solution.py
+++ b/solution.py
@@ -525,9 +525,8 @@
     for bit in bits:
         top_sum = rounded(add_both(top_sum, bit))
     mid_sum = rounded(keep + partner(send, 1).astype(F32))
+    mid_sum = rounded(add_both(mid_sum, 4))
     mid_sum = rounded(add_both(mid_sum, 2))
-    top_sum, _ = lax.optimization_barrier((top_sum, mid_sum))
-    mid_sum = rounded(add_both(mid_sum, 4))
     mid_sum, field = lax.optimization_barrier((mid_sum, field))
     for bit in bits[:-1]:
         mid_sum = rounded(add_both(mid_sum, bit))

time: 49.3 us -> 49.2 us (level)
  waiting for transfers between devices: 12.4 us -> 11.5 us
  starting transfers between devices: 20.6 us -> 21.4 us
    ppermute x11, waiting for transfers between devices: 12.4 us -> 11.5 us  [partner(): return lax.ppermute(block, 'spatial', [(i, i ^ bit) for i in range(size)])]
    ppermute x11, starting transfers between devices: 19.3 us -> 20.1 us  [partner(): return lax.ppermute(block, 'spatial', [(i, i ^ bit) for i in range(size)])]
  transfers between devices with their start and end apart: 13 -> 13, of which waited for: 8 -> 7; matrix products, arithmetic and copies ran while one was open for 6% -> 6% of each run, Pallas kernels for 14% -> 14%
where the time goes in v6:
time: 49.2 us; the launch traced here: 49 us
  starting transfers between devices  21.4 us (43%)
  waiting for transfers between devices  11.5 us (23%)
  Pallas kernels  10.9 us (22%)
  local copies, waits for them, and re-layouts  3.93 us (8%)
  between operations  0.88 us (2%)
    ppermute x11, starting transfers between devices, partner(): return lax.ppermute(block, 'spatial', [(i, i ^ bit) for i in range(size)])  20.1 us
    ppermute x11, waiting for transfers between devices, partner(): return lax.ppermute(block, 'spatial', [(i, i ^ bit) for i in range(size)])  11.5 us
    pallas_call x7, Pallas kernels, kernel_call(): pl.pallas_call(body, name=name, out_shape=outs, in_specs=[whole] * len(ar...  10.9 us
    ppermute x2, starting transfers between devices, across(): return lax.ppermute(block, 'spatial', pairs + [(j, i) for i, j in pairs])  1.32 us
    reshape x2, local copies, waits for them, and re-layouts, shards(): split = weights_mid.reshape(mid, 9, 3, cin)  1.21 us
    reshape x1, local copies, waits for them, and re-layouts, shards(): flat = volume.reshape(cin, nz * plane)  1.17 us
  transfers between devices with their start and end apart: 13, of which 7 were waited for; matrix products, arithmetic and copies ran while one was open for 6% of the time, Pallas kernels for 14%

profile of v6, /device:TPU:0, one launch (start us, length us, event | category | flops | bytes accessed | tf_op | source)
XLA Modules:
  0.0 49.0 jit_solution(12694451696041541626)
XLA Ops:
  0.6 0.0 copy-start.1
  0.7 1.2 %reshape.33.refs_1_ = bf16[32,4096]{1,0:T(8,128)(2,1)S(1)} reshape(bf16[32,4,4,256]{3,2,1,0:T(4,128)(2,1)} %param.4) | data formatting | bytes 524288 | tf_op jit(solution)/shard_map/reshape | solution.py:438
  1.8 0.0 copy-start.2
  1.9 0.5 %collective-permute-start.1 = (bf16[32,3072]{1,0:T(8,128)(2,1)S(1)}, bf16[32,3072]{1,0:T(8,128)(2,1)S(1)}, u32[]{:S(2)}, u32[]{:S(2)}) collective-permute-start(bf16[32,3072]{1,0:T(8,128)(2,1)S(1)} %get-tuple-element.73), channel_id=1, source_target_pairs={{0,1},{1,0},{2,3},{3,2},{4,5},{5,4},{6,7},{7,6},{8,9},{9,8},{10,11... | collective-permute-start | bytes 589832 | tf_op jit(solution)/shard_map/ppermute | solution.py:394
  2.4 0.7 %collective-permute-start = (bf16[32,3072]{1,0:T(8,128)(2,1)S(1)}, bf16[32,3072]{1,0:T(8,128)(2,1)S(1)}, u32[]{:S(2)}, u32[]{:S(2)}) collective-permute-start(bf16[32,3072]{1,0:T(8,128)(2,1)S(1)} %get-tuple-element.74), channel_id=1, source_target_pairs={{1,2},{3,4},{5,6},{7,8},{9,10},{11,12},{13,14},{2,1},{4,3},{6,5},{... | collective-permute-start | bytes 589832 | tf_op jit(solution)/shard_map/ppermute | solution.py:400
  3.1 1.1 %copy.16 = bf16[64,9,3,32]{0,2,3,1:T(4,128)(2,1)S(1)} copy(bf16[64,9,3,32]{0,3,2,1:T(8,128)(2,1)} %bitcast.23) | data formatting | bytes 221184 | tf_op jit(solution)/shard_map/reshape | solution.py:442
  4.2 0.0 copy-done.1
  4.2 0.1 copy.15
  4.3 0.2 reshape.36
  4.5 0.1 copy.11.refs_2_.refs_3_
  4.6 0.2 reshape.35.refs_1_
  4.9 0.0 copy-done.2
  4.9 0.1 reshape.38.refs_5_
  5.0 0.0 copy-start
  5.0 0.0 collective-permute-done.1.refs_0_
  5.0 1.5 %near_side.1 = (bf16[32,10752]{1,0:T(8,128)(2,1)S(1)}, f32[64,4096]{1,0:T(8,128)S(1)}, bf16[192,1024]{1,0:T(8,128)(2,1)S(1)}) custom-call(bf16[32,3072]{1,0:T(8,128)(2,1)S(1)} %collective-permute-done.1.refs_0_, bf16[32,4096]{1,0:T(8,128)(2,1)S(1)} %reshape.33.refs_1_, bf16[192,288]{1,0:T(8,128)(2,1)S(1)} %copy.11.refs_2_.refs_3_), custom_call_target="tpu_custom_call" | custom-call | flops 900000000 | bytes 3000000 | tf_op jit(solution)/shard_map/near_side/pallas_call | solution.py:23
  6.5 0.0 collective-permute-done.refs_0_
  6.5 0.0 copy-done
  6.5 2.8 %far_side.1 = (bf16[128,512]{1,0:T(8,128)(2,1)S(1)}, f32[64,4096]{1,0:T(8,128)S(1)}, bf16[32,15360]{1,0:T(8,128)(2,1)S(1)}, f32[864,128]{1,0:T(8,128)S(1)}, bf16[1376,128]{1,0:T(8,128)(2,1)S(1)}) custom-call(bf16[32,3072]{1,0:T(8,128)(2,1)S(1)} %collective-permute-done.refs_0_, bf16[32,10752]{1,0:T(8,128)(2,1)S(1)} %get-tuple-element.43.refs_1_, ...), custom_call_target="tpu_custom_call" | custom-call | flops 1100000000 | bytes 5000000 | tf_op jit(solution)/shard_map/far_side/pallas_call | solution.py:23
  9.3 5.2 %collective-permute-start.3 = (bf16[1376,128]{1,0:T(8,128)(2,1)S(1)}, bf16[1376,128]{1,0:T(8,128)(2,1)S(1)}, u32[]{:S(2)}, u32[]{:S(2)}) collective-permute-start(bf16[1376,128]{1,0:T(8,128)(2,1)S(1)} %get-tuple-element.46), channel_id=1, source_target_pairs={{0,1},{1,0},{2,3},{3,2},{4,5},{5,4},{6,7},{7,6},{8,9},{9,8},{10,11... | collective-permute-start | bytes 1056776 | tf_op jit(solution)/shard_map/ppermute | solution.py:394
  14.5 0.7 %collective-permute-start.2 = (bf16[128,512]{1,0:T(8,128)(2,1)S(1)}, bf16[128,512]{1,0:T(8,128)(2,1)S(1)}, u32[]{:S(2)}, u32[]{:S(2)}) collective-permute-start(bf16[128,512]{1,0:T(8,128)(2,1)S(1)} %get-tuple-element.45.refs_1_), channel_id=1, source_target_pairs={{1,2},{3,4},{5,6},{7,8},{9,10},{11,12},{13,14},{2,1},{4,3},{6,5},{... | collective-permute-start | bytes 393224 | tf_op jit(solution)/shard_map/ppermute | solution.py:400
  15.2 0.8 %slope.1.refs_2_ = f32[64,6144]{1,0:T(8,128)S(1)} custom-call(f32[64,4096]{1,0:T(8,128)S(1)} %get-tuple-element.47.refs_0_, f32[64,4096]{1,0:T(8,128)S(1)} %get-tuple-element.48.refs_1_), custom_call_target="tpu_custom_call" | custom-call | flops 100000000 | bytes 3000000 | tf_op jit(solution)/shard_map/slope/pallas_call | solution.py:23
  16.0 0.0 collective-permute-done.3.refs_0_
  16.0 5.2 %collective-permute-start.4 = (bf16[432,128]{1,0:T(8,128)(2,1)S(1)}, bf16[432,128]{1,0:T(8,128)(2,1)S(1)}, u32[]{:S(2)}, u32[]{:S(2)}) collective-permute-start(bf16[432,128]{1,0:T(8,128)(2,1)S(1)} %select_convert_fusion), channel_id=1, source_target_pairs={{0,4},{1,5},{2,6},{3,7},{4,0},{5,1},{6,2},{7,3},{8,12},{9,13},{10,... | collective-permute-start | bytes 331784 | tf_op jit(solution)/shard_map/ppermute | solution.py:394
  21.3 1.4 %backward_near.1 = (f32[288,192]{1,0:T(8,128)S(1)}, bf16[64,4608]{1,0:T(8,128)(2,1)S(1)}) custom-call(bf16[1376,128]{1,0:T(8,128)(2,1)S(1)} %collective-permute-done.3.refs_0_, bf16[128,512]{1,0:T(8,128)(2,1)S(1)} %get-tuple-element.45.refs_1_, f32[64,6144]{1,0:T(8,128)S(1)} %slope.1.refs_2_, bf16[32,15360]{1,0:T(8,128)(2,1)S(1)} %get-tuple-element.49.refs_3_, ...), custom_call_target="tpu_custom_call" | custom-call | flops 500000000 | bytes 3000000 | tf_op jit(solution)/shard_map/backward_near/pallas_call | solution.py:23
  22.7 0.0 collective-permute-done.2.refs_0_
  22.7 1.5 %backward_far.1 = (f32[224,128]{1,0:T(8,128)S(1)}, bf16[224,128]{1,0:T(8,128)(2,1)S(1)}, bf16[64,9216]{1,0:T(8,128)(2,1)S(1)}) custom-call(bf16[128,512]{1,0:T(8,128)(2,1)S(1)} %collective-permute-done.2.refs_0_, bf16[128,512]{1,0:T(8,128)(2,1)S(1)} %get-tuple-element.45.refs_1_, f32[64,6144]{1,0:T(8,128)S(1)} %slope.1.refs_2_, ...), custom_call_target="tpu_custom_call" | custom-call | flops 500000000 | bytes 4000000 | tf_op jit(solution)/shard_map/backward_far/pallas_call | solution.py:23
  24.3 1.3 %collective-permute-done.4 = bf16[432,128]{1,0:T(8,128)(2,1)S(1)} collective-permute-done((bf16[432,128]{1,0:T(8,128)(2,1)S(1)}, bf16[432,128]{1,0:T(8,128)(2,1)S(1)}, u32[]{:S(2)}, u32[]{:S(2)}) %collective-permute-start.4) | collective-permute-done | bytes 110624 | tf_op jit(solution)/shard_map/ppermute | solution.py:394
  25.7 0.1 collective-permute-start.7
  25.7 1.2 %collective-permute-done.7 = bf16[224,128]{1,0:T(8,128)(2,1)S(1)} collective-permute-done((bf16[224,128]{1,0:T(8,128)(2,1)S(1)}, bf16[224,128]{1,0:T(8,128)(2,1)S(1)}, u32[]{:S(2)}, u32[]{:S(2)}) %collective-permute-start.7) | collective-permute-done | bytes 57376 | tf_op jit(solution)/shard_map/ppermute | solution.py:394
  27.0 1.0 %collective-permute-start.8 = (bf16[224,128]{1,0:T(8,128)(2,1)S(1)}, bf16[224,128]{1,0:T(8,128)(2,1)S(1)}, u32[]{:S(2)}, u32[]{:S(2)}) collective-permute-start(bf16[224,128]{1,0:T(8,128)(2,1)S(1)} %add_convert_fusion.5), channel_id=1, source_target_pairs={{0,4},{1,5},{2,6},{3,7},{4,0},{5,1},{6,2},{7,3},{8,12},{9,13},{10,... | collective-permute-start | bytes 172040 | tf_op jit(solution)/shard_map/ppermute | solution.py:394
  28.0 2.6 %collective-permute-start.5 = (bf16[432,128]{1,0:T(8,128)(2,1)S(1)}, bf16[432,128]{1,0:T(8,128)(2,1)S(1)}, u32[]{:S(2)}, u32[]{:S(2)}) collective-permute-start(bf16[432,128]{1,0:T(8,128)(2,1)S(1)} %add_convert_fusion.2), channel_id=1, source_target_pairs={{0,8},{1,9},{2,10},{3,11},{4,12},{5,13},{6,14},{7,15},{8,0},{9,1},... | collective-permute-start | bytes 331784 | tf_op jit(solution)/shard_map/ppermute | solution.py:394
  30.6 0.6 %collective-permute-done.8 = bf16[224,128]{1,0:T(8,128)(2,1)S(1)} collective-permute-done((bf16[224,128]{1,0:T(8,128)(2,1)S(1)}, bf16[224,128]{1,0:T(8,128)(2,1)S(1)}, u32[]{:S(2)}, u32[]{:S(2)}) %collective-permute-start.8) | collective-permute-done | bytes 57376 | tf_op jit(solution)/shard_map/ppermute | solution.py:394
  31.3 1.0 %collective-permute-start.9 = (bf16[224,128]{1,0:T(8,128)(2,1)S(1)}, bf16[224,128]{1,0:T(8,128)(2,1)S(1)}, u32[]{:S(2)}, u32[]{:S(2)}) collective-permute-start(bf16[224,128]{1,0:T(8,128)(2,1)S(1)} %add_convert_fusion.4), channel_id=1, source_target_pairs={{0,2},{1,3},{2,0},{3,1},{4,6},{5,7},{6,4},{7,5},{8,10},{9,11},{10,... | collective-permute-start | bytes 172040 | tf_op jit(solution)/shard_map/ppermute | solution.py:394
  32.3 4.0 %collective-permute-done.5 = bf16[432,128]{1,0:T(8,128)(2,1)S(1)} collective-permute-done((bf16[432,128]{1,0:T(8,128)(2,1)S(1)}, bf16[432,128]{1,0:T(8,128)(2,1)S(1)}, u32[]{:S(2)}, u32[]{:S(2)}) %collective-permute-start.5) | collective-permute-done | bytes 110624 | tf_op jit(solution)/shard_map/ppermute | solution.py:394
  36.4 0.8 %collective-permute-start.6 = (bf16[432,128]{1,0:T(8,128)(2,1)S(1)}, bf16[432,128]{1,0:T(8,128)(2,1)S(1)}, u32[]{:S(2)}, u32[]{:S(2)}) collective-permute-start(bf16[432,128]{1,0:T(8,128)(2,1)S(1)} %add_convert_fusion.1), channel_id=1, source_target_pairs={{0,2},{1,3},{2,0},{3,1},{4,6},{5,7},{6,4},{7,5},{8,10},{9,11},{10,... | collective-permute-start | bytes 331784 | tf_op jit(solution)/shard_map/ppermute | solution.py:394
  37.2 0.0 collective-permute-done.9
  37.2 1.8 %collective-permute-start.11 = (bf16[224,128]{1,0:T(8,128)(2,1)S(1)}, bf16[224,128]{1,0:T(8,128)(2,1)S(1)}, u32[]{:S(2)}, u32[]{:S(2)}) collective-permute-start(bf16[224,128]{1,0:T(8,128)(2,1)S(1)} %add_convert_fusion.3), channel_id=1, source_target_pairs={{0,8},{1,9},{2,10},{3,11},{4,12},{5,13},{6,14},{7,15},{8,0},{9,1},... | collective-permute-start | bytes 172040 | tf_op jit(solution)/shard_map/ppermute | solution.py:394
  39.0 1.7 %input_grad.1 = bf16[32,4096]{1,0:T(8,128)(2,1)S(1)} custom-call(bf16[64,9216]{1,0:T(8,128)(2,1)S(1)} %get-tuple-element.66.refs_0_, bf16[96,576]{1,0:T(8,128)(2,1)S(1)} %reshape.35.refs_1_), custom_call_target="tpu_custom_call" | custom-call | flops 452000000 | bytes 2000000 | tf_op jit(solution)/shard_map/input_grad/pallas_call | solution.py:23
  40.7 0.5 %collective-permute-done.6 = bf16[432,128]{1,0:T(8,128)(2,1)S(1)} collective-permute-done((bf16[432,128]{1,0:T(8,128)(2,1)S(1)}, bf16[432,128]{1,0:T(8,128)(2,1)S(1)}, u32[]{:S(2)}, u32[]{:S(2)}) %collective-permute-start.6) | collective-permute-done | bytes 110624 | tf_op jit(solution)/shard_map/ppermute | solution.py:394
  41.2 1.7 %collective-permute-start.10 = (bf16[432,128]{1,0:T(8,128)(2,1)S(1)}, bf16[432,128]{1,0:T(8,128)(2,1)S(1)}, u32[]{:S(2)}, u32[]{:S(2)}) collective-permute-start(bf16[432,128]{1,0:T(8,128)(2,1)S(1)} %add_convert_fusion), channel_id=1, source_target_pairs={{0,4},{1,5},{2,6},{3,7},{4,0},{5,1},{6,2},{7,3},{8,12},{9,13},{10,... | collective-permute-start | bytes 331784 | tf_op jit(solution)/shard_map/ppermute | solution.py:394
  42.9 0.0 collective-permute-done.11
  43.0 3.0 %collective-permute-done.10 = bf16[432,128]{1,0:T(8,128)(2,1)S(1)} collective-permute-done((bf16[432,128]{1,0:T(8,128)(2,1)S(1)}, bf16[432,128]{1,0:T(8,128)(2,1)S(1)}, u32[]{:S(2)}, u32[]{:S(2)}) %collective-permute-start.10) | collective-permute-done | bytes 110624 | tf_op jit(solution)/shard_map/ppermute | solution.py:394
  46.1 0.1 collective-permute-start.12
  46.2 0.9 %reshape.39 = bf16[32,4,4,256]{3,2,1,0:T(4,128)(2,1)} reshape(bf16[32,4096]{1,0:T(8,128)(2,1)S(1)} %input_grad.1) | data formatting | bytes 524288 | tf_op jit(solution)/shard_map/reshape | solution.py:561
  47.0 0.7 %collective-permute-done.12.refs_1_ = bf16[1312,128]{1,0:T(8,128)(2,1)S(1)} collective-permute-done((bf16[1312,128]{1,0:T(8,128)(2,1)S(1)}, bf16[1312,128]{1,0:T(8,128)(2,1)S(1)}, u32[]{:S(2)}, u32[]{:S(2)}) %collective-permute-start.12) | collective-permute-done | bytes 335904 | tf_op jit(solution)/shard_map/ppermute | solution.py:394
  47.8 1.2 %finish.1 = (f32[1728,128]{1,0:T(8,128)}, f32[864,64]{1,0:T(8,128)}) custom-call(bf16[1312,128]{1,0:T(8,128)(2,1)S(1)} %pad_maximum_fusion.refs_0_, bf16[1312,128]{1,0:T(8,128)(2,1)S(1)} %collective-permute-done.12.refs_1_), custom_call_target="tpu_custom_call" | custom-call | bytes 2000000 | tf_op jit(solution)/shard_map/finish/pallas_call | solution.py:23
  (14 shorter events, 0.4 us)
Async XLA Ops:
  0.6 3.5 %copy-start.1 = (bf16[64,27,32]{0,2,1:T(8,128)(2,1)S(1)}, bf16[64,27,32]{0,2,1:T(8,128)(2,1)}, u32[]{:S(2)}) copy-start(bf16[64,27,32]{0,2,1:T(8,128)(2,1)} %param.5) | copy-start | bytes 331780
  1.8 3.1 %copy-start.2 = (bf16[128,2,2,128]{3,2,1,0:T(2,128)(2,1)S(1)}, bf16[128,2,2,128]{3,2,1,0:T(2,128)(2,1)}, u32[]{:S(2)}) copy-start(bf16[128,2,2,128]{3,2,1,0:T(2,128)(2,1)} %param.7) | copy-start | bytes 393220
  1.9 3.1 %collective-permute-start.1 = (bf16[32,3072]{1,0:T(8,128)(2,1)S(1)}, bf16[32,3072]{1,0:T(8,128)(2,1)S(1)}, u32[]{:S(2)}, u32[]{:S(2)}) collective-permute-start(bf16[32,3072]{1,0:T(8,128)(2,1)S(1)} %get-tuple-element.73), channel_id=1, source_target_pairs={{0,1},{1,0},{2,3},{3,2},{4,5},{5,4},{6,7},{7,6},{8,9},{9,8},{10,11... | collective-permute-start | bytes 589832 | tf_op jit(solution)/shard_map/ppermute | solution.py:394
  2.4 4.1 %collective-permute-start = (bf16[32,3072]{1,0:T(8,128)(2,1)S(1)}, bf16[32,3072]{1,0:T(8,128)(2,1)S(1)}, u32[]{:S(2)}, u32[]{:S(2)}) collective-permute-start(bf16[32,3072]{1,0:T(8,128)(2,1)S(1)} %get-tuple-element.74), channel_id=1, source_target_pairs={{1,2},{3,4},{5,6},{7,8},{9,10},{11,12},{13,14},{2,1},{4,3},{6,5},{... | collective-permute-start | bytes 589832 | tf_op jit(solution)/shard_map/ppermute | solution.py:400
  5.0 1.5 %copy-start = (bf16[128,27,64]{0,2,1:T(8,128)(2,1)S(1)}, bf16[128,27,64]{0,2,1:T(8,128)(2,1)}, u32[]{:S(2)}) copy-start(bf16[128,27,64]{0,2,1:T(8,128)(2,1)} %param.6) | copy-start | bytes 1327108
  9.3 6.7 %collective-permute-start.3 = (bf16[1376,128]{1,0:T(8,128)(2,1)S(1)}, bf16[1376,128]{1,0:T(8,128)(2,1)S(1)}, u32[]{:S(2)}, u32[]{:S(2)}) collective-permute-start(bf16[1376,128]{1,0:T(8,128)(2,1)S(1)} %get-tuple-element.46), channel_id=1, source_target_pairs={{0,1},{1,0},{2,3},{3,2},{4,5},{5,4},{6,7},{7,6},{8,9},{9,8},{10,11... | collective-permute-start | bytes 1056776 | tf_op jit(solution)/shard_map/ppermute | solution.py:394
  14.5 8.2 %collective-permute-start.2 = (bf16[128,512]{1,0:T(8,128)(2,1)S(1)}, bf16[128,512]{1,0:T(8,128)(2,1)S(1)}, u32[]{:S(2)}, u32[]{:S(2)}) collective-permute-start(bf16[128,512]{1,0:T(8,128)(2,1)S(1)} %get-tuple-element.45.refs_1_), channel_id=1, source_target_pairs={{1,2},{3,4},{5,6},{7,8},{9,10},{11,12},{13,14},{2,1},{4,3},{6,5},{... | collective-permute-start | bytes 393224 | tf_op jit(solution)/shard_map/ppermute | solution.py:400
  16.0 9.6 %collective-permute-start.4 = (bf16[432,128]{1,0:T(8,128)(2,1)S(1)}, bf16[432,128]{1,0:T(8,128)(2,1)S(1)}, u32[]{:S(2)}, u32[]{:S(2)}) collective-permute-start(bf16[432,128]{1,0:T(8,128)(2,1)S(1)} %select_convert_fusion), channel_id=1, source_target_pairs={{0,4},{1,5},{2,6},{3,7},{4,0},{5,1},{6,2},{7,3},{8,12},{9,13},{10,... | collective-permute-start | bytes 331784 | tf_op jit(solution)/shard_map/ppermute | solution.py:394
  25.7 1.3 %collective-permute-start.7 = (bf16[224,128]{1,0:T(8,128)(2,1)S(1)}, bf16[224,128]{1,0:T(8,128)(2,1)S(1)}, u32[]{:S(2)}, u32[]{:S(2)}) collective-permute-start(bf16[224,128]{1,0:T(8,128)(2,1)S(1)} %get-tuple-element.64), channel_id=1, source_target_pairs={{0,1},{1,0},{2,3},{3,2},{4,5},{5,4},{6,7},{7,6},{8,9},{9,8},{10,11... | collective-permute-start | bytes 172040 | tf_op jit(solution)/shard_map/ppermute | solution.py:394
  27.0 4.2 %collective-permute-start.8 = (bf16[224,128]{1,0:T(8,128)(2,1)S(1)}, bf16[224,128]{1,0:T(8,128)(2,1)S(1)}, u32[]{:S(2)}, u32[]{:S(2)}) collective-permute-start(bf16[224,128]{1,0:T(8,128)(2,1)S(1)} %add_convert_fusion.5), channel_id=1, source_target_pairs={{0,4},{1,5},{2,6},{3,7},{4,0},{5,1},{6,2},{7,3},{8,12},{9,13},{10,... | collective-permute-start | bytes 172040 | tf_op jit(solution)/shard_map/ppermute | solution.py:394
  28.0 8.3 %collective-permute-start.5 = (bf16[432,128]{1,0:T(8,128)(2,1)S(1)}, bf16[432,128]{1,0:T(8,128)(2,1)S(1)}, u32[]{:S(2)}, u32[]{:S(2)}) collective-permute-start(bf16[432,128]{1,0:T(8,128)(2,1)S(1)} %add_convert_fusion.2), channel_id=1, source_target_pairs={{0,8},{1,9},{2,10},{3,11},{4,12},{5,13},{6,14},{7,15},{8,0},{9,1},... | collective-permute-start | bytes 331784 | tf_op jit(solution)/shard_map/ppermute | solution.py:394
  31.3 5.9 %collective-permute-start.9 = (bf16[224,128]{1,0:T(8,128)(2,1)S(1)}, bf16[224,128]{1,0:T(8,128)(2,1)S(1)}, u32[]{:S(2)}, u32[]{:S(2)}) collective-permute-start(bf16[224,128]{1,0:T(8,128)(2,1)S(1)} %add_convert_fusion.4), channel_id=1, source_target_pairs={{0,2},{1,3},{2,0},{3,1},{4,6},{5,7},{6,4},{7,5},{8,10},{9,11},{10,... | collective-permute-start | bytes 172040 | tf_op jit(solution)/shard_map/ppermute | solution.py:394
  36.4 4.8 %collective-permute-start.6 = (bf16[432,128]{1,0:T(8,128)(2,1)S(1)}, bf16[432,128]{1,0:T(8,128)(2,1)S(1)}, u32[]{:S(2)}, u32[]{:S(2)}) collective-permute-start(bf16[432,128]{1,0:T(8,128)(2,1)S(1)} %add_convert_fusion.1), channel_id=1, source_target_pairs={{0,2},{1,3},{2,0},{3,1},{4,6},{5,7},{6,4},{7,5},{8,10},{9,11},{10,... | collective-permute-start | bytes 331784 | tf_op jit(solution)/shard_map/ppermute | solution.py:394
  37.2 5.8 %collective-permute-start.11 = (bf16[224,128]{1,0:T(8,128)(2,1)S(1)}, bf16[224,128]{1,0:T(8,128)(2,1)S(1)}, u32[]{:S(2)}, u32[]{:S(2)}) collective-permute-start(bf16[224,128]{1,0:T(8,128)(2,1)S(1)} %add_convert_fusion.3), channel_id=1, source_target_pairs={{0,8},{1,9},{2,10},{3,11},{4,12},{5,13},{6,14},{7,15},{8,0},{9,1},... | collective-permute-start | bytes 172040 | tf_op jit(solution)/shard_map/ppermute | solution.py:394
  41.2 4.8 %collective-permute-start.10 = (bf16[432,128]{1,0:T(8,128)(2,1)S(1)}, bf16[432,128]{1,0:T(8,128)(2,1)S(1)}, u32[]{:S(2)}, u32[]{:S(2)}) collective-permute-start(bf16[432,128]{1,0:T(8,128)(2,1)S(1)} %add_convert_fusion), channel_id=1, source_target_pairs={{0,4},{1,5},{2,6},{3,7},{4,0},{5,1},{6,2},{7,3},{8,12},{9,13},{10,... | collective-permute-start | bytes 331784 | tf_op jit(solution)/shard_map/ppermute | solution.py:394
  46.1 1.7 %collective-permute-start.12 = (bf16[1312,128]{1,0:T(8,128)(2,1)S(1)}, bf16[1312,128]{1,0:T(8,128)(2,1)S(1)}, u32[]{:S(2)}, u32[]{:S(2)}) collective-permute-start(bf16[1312,128]{1,0:T(8,128)(2,1)S(1)} %pad_maximum_fusion.refs_0_), channel_id=1, source_target_pairs={{0,1},{1,0},{2,3},{3,2},{4,5},{5,4},{6,7},{7,6},{8,9},{9,8},{10,11... | collective-permute-start | bytes 1007624 | tf_op jit(solution)/shard_map/ppermute | solution.py:394
